TPU v7x, 512 devices: a whole 4x4x16 slice. The times are simulated.
512 devices in a mesh: row: 16 (over z_lo, x), col: 32 (over z_hi, y, core).
Axes of the slice: x: 4, y: 4, z: 16 (z_hi: 4, z_lo: 4; z = z_hi * 4 + z_lo), core: 2. Of those that a mesh axis runs over, the one named last changes fastest.
Arguments:
- coeffs: float32 [8192, 8192], P('row', 'col'), may hold values from -6 to 6
- diag_energy: float32 [8192, 8192], P('row', 'col'), may hold values from 1 to 9
- energy: float32 [1], replicated, may hold values from 4 to 6
- h_blocks: bfloat16 [64, 24, 128, 128], P('row'), may hold values from -0.109375 to 0.109375
- pattern: int32 [64, 24], replicated, may hold values from 0 to 63, as said below
- counts: int32 [64], replicated, may hold values from 1 to 24, 960 in all
Outputs:
- correction: float32 [8192, 8192], P('row', 'col')
Inputs may be any that keep to these rules, and one draw needn't show every extreme that they name: `pattern`: each row lists 24 different block indices; block columns q * 2 to q * 2 + 1 form group q, and block c * 2 to c * 2 + 1 form the blocks of group c; all slots of the rows of one group together name exactly half of the blocks of every group.
All inputs are finite; a program needn't handle non-finite values.
Results may differ from a plain program's by a relative error of at most 0.0018.
Values may be sent and summed in bfloat16 or wider, within the bound.
No kernel may reach another device: no remote copies, remote signals or barrier semaphores. Data moves between devices by JAX's collectives and lax.ppermute only.
A program may use at most 128 MiB of HBM per device.

v0:
```python
import jax
import jax.numpy as jnp
from jax import lax
from jax.sharding import PartitionSpec as P


def broadcast(value, axis, root):
    mine = lax.axis_index(axis) == root
    return lax.psum(jnp.where(mine, value, jnp.zeros_like(value)), axis)


def build_panel(block_rows, h_part, blocks_all):
    onehot = (
        block_rows[:, :, None] == jnp.arange(blocks_all, dtype=jnp.int32)[None, None, :]
    ).astype(jnp.bfloat16)
    panel = jnp.einsum("msk,msab->kamb", onehot, h_part, preferred_element_type=jnp.float32).astype(
        jnp.bfloat16
    )
    return panel.reshape(blocks_all * h_part.shape[2], h_part.shape[0] * h_part.shape[3])


def on_device(coeffs, diag_energy, energy, h_blocks, pattern, counts):
    alpha_local, beta_local = coeffs.shape
    row_blocks = h_blocks.shape[0]
    slot_count = h_blocks.shape[1]
    width = h_blocks.shape[2]
    blocks_all = pattern.shape[0]
    col_blocks = beta_local // width
    row_id = lax.axis_index("row")
    col_id = lax.axis_index("col")
    coeff_half = coeffs.astype(jnp.bfloat16)
    filled = jnp.arange(slot_count, dtype=jnp.int32)[None, :] < counts[:, None]
    first_col = col_id * col_blocks
    source = first_col // row_blocks
    offset = first_col % row_blocks
    received = broadcast(h_blocks, "row", source)
    h_cols = lax.dynamic_slice_in_dim(received, offset, col_blocks, 0)
    col_pattern = lax.dynamic_slice_in_dim(pattern, first_col, col_blocks, 0)
    col_filled = lax.dynamic_slice_in_dim(filled, first_col, col_blocks, 0)
    row_pattern = lax.dynamic_slice_in_dim(pattern, row_id * row_blocks, row_blocks, 0)
    row_filled = lax.dynamic_slice_in_dim(filled, row_id * row_blocks, row_blocks, 0)
    h_cols = jnp.where(col_filled[:, :, None, None], h_cols, jnp.zeros_like(h_cols))
    h_rows = jnp.where(row_filled[:, :, None, None], h_blocks, jnp.zeros_like(h_blocks))
    panel_one = build_panel(col_pattern, h_cols, blocks_all)
    panel_rows = panel_one
    direct_term = jnp.dot(
        lax.all_gather(coeff_half, "col", axis=1, tiled=True),
        panel_rows,
        preferred_element_type=jnp.float32,
    )
    panel_two = build_panel(row_pattern, h_rows, blocks_all)
    panel_rows = panel_two
    mirror_term = lax.dot_general(
        panel_rows,
        lax.all_gather(coeff_half, "row", axis=0, tiled=True),
        (((0,), (0,)), ((), ())),
        preferred_element_type=jnp.float32,
    )
    sigma_full = direct_term + mirror_term + diag_energy * coeffs
    shift_value = energy[0]
    return (sigma_full - shift_value * coeffs) / jnp.maximum(
        jnp.abs(diag_energy - shift_value), 1.0
    )


def solution(mesh):
    placed = (P("row", "col"), P("row", "col"), P(), P("row", None, None, None), P(), P())
    return jax.shard_map(
        on_device, mesh=mesh, in_specs=placed, out_specs=P("row", "col"), check_vma=False
    )
```

profile of v0, /device:TPU:16, one launch (start us, length us, event | category | flops | bytes accessed | tf_op | source)
XLA Modules:
  0.0 315.2 jit_solution(13559559978218991884)
XLA Ops:
  7.4 0.0 copy-start
  7.4 0.0 all-reduce.2.cloned.1.call-start
  7.4 0.7 iota_compare_fusion.1
  8.2 3.3 %broadcast_select_fusion = (bf16[4,24,128,128]{3,2,1,0:T(8,128)(2,1)S(1)}, bf16[4,24,128,128]{3,2,1,0:T(8,128)(2,1)}) fusion(bf16[4,24,128,128]{3,2,1,0:T(8,128)(2,1)} %param.9, pred[4,24]{1,0:T(4,128)(4,1)S(1)} %constant_dynamic-slice_fusion.1, pred[]{:T(512)S(6)} %eq.16), kind=kLoop, calls=%fused_computation.9 | loop fusion | flops 3145728 | bytes 9437281 | tf_op jit(solution)/shard_map/jit(_where)/select_n | solution.py:43
  11.5 0.0 all-reduce.2.cloned.1.call-update
  11.5 0.0 all-gather.3.cloned.1.call-start
  11.6 1.8 convert_element_type.19
  13.3 0.0 all-gather.3.cloned.1.call-update
  13.4 0.0 all-gather.5.cloned.1.call-start
  13.4 0.5 all-gather.5.cloned.1.call-update
  14.0 2.0 copy.25
  16.0 0.0 copy-done
  16.0 0.1 constant_dynamic-slice_fusion.2
  16.1 0.1 copy.17
  16.2 0.1 constant_dynamic-slice_fusion
  16.2 0.1 copy.20
  16.3 6.2 %convert_bitcast_fusion = bf16[64,128,4,128]{3,0,1,2:T(8,128)(2,1)} fusion(bf16[4,24,128,128]{3,2,1,0:T(8,128)(2,1)S(1)} %get-tuple-element.5, s32[4,24]{1,0:T(4,128)S(1)} %copy.20), kind=kOutput, calls=%fused_computation.3 | convolution fusion | flops 205527040 | bytes 11534720 | tf_op jit(solution)/shard_map/msk,msab->kamb/dot_general | solution.py:16
  22.5 0.0 copy-start.1
  22.5 13.6 %copy.22 = bf16[64,128,4,128]{1,0,3,2:T(8,128)(2,1)} copy(bf16[64,128,4,128]{3,0,1,2:T(8,128)(2,1)} %convert_bitcast_fusion) | data formatting | bytes 16777216 | tf_op jit(solution)/shard_map/convert_element_type | solution.py:16
  36.1 0.0 copy-done.1
  36.1 0.2 copy.24
  37.0 236.8 %all-reduce.2.cloned.1.call-done = bf16[4,24,128,128]{3,2,1,0:T(8,128)(2,1)} async-done(((bf16[4,24,128,128]{3,2,1,0:T(8,128)(2,1)}), bf16[4,24,128,128]{3,2,1,0:T(8,128)(2,1)}) %all-reduce.2.cloned.1.call-update) | async-done | bytes 3145744 | tf_op jit(solution)/shard_map/psum | solution.py:9
  273.8 1.6 dynamic-slice_select_fusion
  275.4 3.6 %convert_bitcast_fusion.1 = bf16[64,128,2,128]{3,0,1,2:T(8,128)(2,1)} fusion(bf16[2,24,128,128]{3,2,1,0:T(8,128)(2,1)S(1)} %dynamic-slice_select_fusion, s32[2,24]{1,0:T(2,128)S(1)} %copy.17), kind=kOutput, calls=%fused_computation.7 | convolution fusion | flops 102763520 | bytes 5767360 | tf_op jit(solution)/shard_map/msk,msab->kamb/dot_general | solution.py:16
  279.0 7.4 %copy.19 = bf16[64,128,2,128]{1,0,3,2:T(8,128)(2,1)} copy(bf16[64,128,2,128]{3,0,1,2:T(8,128)(2,1)} %convert_bitcast_fusion.1) | data formatting | bytes 8388608 | tf_op jit(solution)/shard_map/convert_element_type | solution.py:16
  286.4 0.0 all-gather.3.cloned.1.call-done
  286.4 0.0 copy-start.2
  286.4 9.2 %fusion.8 = f32[512,256]{0,1:T(8,128)S(1)} fusion(bf16[512,8192]{1,0:T(8,128)(2,1)} %all-gather.3.cloned.1.call-done, bf16[32,8,64,128]{3,2,1,0:T(8,128)(2,1)} %bitcast.45), kind=kOutput, calls=%fused_computation.13 | convolution fusion | flops 2147483648 | bytes 13107200 | tf_op jit(solution)/shard_map/dot_general | solution.py:46
  295.6 0.0 all-gather.5.cloned.1.call-done
  295.6 0.0 copy-done.2
  295.6 11.1 %fusion.20 = f32[512,256]{0,1:T(8,128)S(1)} fusion(f32[512,256]{0,1:T(8,128)S(1)} %fusion.8, bf16[8192,256]{1,0:T(8,128)(2,1)} %all-gather.5.cloned.1.call-done, bf16[64,8,64,128]{3,2,1,0:T(8,128)(2,1)} %bitcast.44, f32[512,256]{0,1:T(8,128)S(1)} %copy.24, f32[512,256]{0,1:T(8,128)S(1)} %copy-done.2, f32[]{:T(128)} %bitcast.43), kind=kOutput, calls=%fused_computation.17 | convolution fusion | flops 2148663296 | bytes 14680068 | tf_op jit(solution)/shard_map/dot_general | solution.py:53
  306.8 1.0 copy.28
  (2 shorter events, 0.0 us)
Async XLA Ops:
  7.4 8.7 %copy-start = (s32[64,24]{0,1:T(8,128)S(1)}, s32[64,24]{0,1:T(8,128)}, u32[]{:S(2)}) copy-start(s32[64,24]{0,1:T(8,128)} %param.10) | copy-start | bytes 18436
  7.4 266.4 %all-reduce.2.cloned.1.call-start = ((), (), s32[]{:S(2)}) async-start(), calls=%async_computation | async-start | bytes 6291456 | tf_op jit(solution)/shard_map/psum | solution.py:9
  11.5 274.9 %all-gather.3.cloned.1.call-start = ((), (), s32[]{:S(2)}) async-start(), calls=%async_computation.1 | async-start | bytes 8650752 | tf_op jit(solution)/shard_map/all_gather | solution.py:47
  13.4 282.2 %all-gather.5.cloned.1.call-start = ((), (), s32[]{:S(2)}) async-start(), calls=%async_computation.2 | async-start | bytes 4456448 | tf_op jit(solution)/shard_map/all_gather | solution.py:55
  22.5 13.6 %copy-start.1 = (f32[512,256]{1,0:T(8,128)S(1)}, f32[512,256]{1,0:T(8,128)}, u32[]{:S(2)}) copy-start(f32[512,256]{1,0:T(8,128)} %param.7) | copy-start | bytes 1572868
  286.4 9.2 %copy-start.2 = (f32[512,256]{0,1:T(8,128)S(1)}, f32[512,256]{0,1:T(8,128)}, u32[]{:S(2)}) copy-start(f32[512,256]{0,1:T(8,128)} %copy.25) | copy-start | bytes 1572868
Sparse Core Ops, SparseCore 0:
  11.6 262.1 all-reduce.1
Sparse Core Ops, SparseCore 1:
  15.0 137.6 all-gather.2
  154.7 115.3 all-gather.4
where the time goes:
time: 316 us; the launch traced here: 315 us
  waiting for transfers between devices  237 us (75%)
  matrix products  30.1 us (10%)
  local copies, waits for them, and re-layouts  24.6 us (8%)
  between operations  15.6 us (5%)
  other arithmetic  7.43 us (2%)
    psum x1, waiting for transfers between devices, broadcast(): return lax.psum(jnp.where(mine, value, jnp.zeros_like(value)), axis)  237 us
    convert_element_type x2, local copies, waits for them, and re-layouts, build_panel(): jnp.einsum('msk,msab->kamb', onehot, h_part, preferred_element_type=jnp.f...  21 us
    dot_general x1, matrix products, on_device(): lax.dot_general(panel_rows, lax.all_gather(coeff_half, 'row', axis=0, til...  11.1 us
    dot_general x2, matrix products, build_panel(): jnp.einsum('msk,msab->kamb', onehot, h_part, preferred_element_type=jnp.f...  9.74 us
    dot_general x1, matrix products, on_device(): jnp.dot(lax.all_gather(coeff_half, 'col', axis=1, tiled=True), panel_rows...  9.21 us
  transfers between devices with their start and end apart: 3, of which 1 were waited for; matrix products, arithmetic and copies ran while one was open for 15% of the time, Pallas kernels for 0%

commit v1 on v0

v1 whole, which is shorter than its diff:
```python
import functools

import jax
import jax.numpy as jnp
from jax import lax
from jax.experimental import pallas as pl
from jax.experimental.pallas import tpu as pltpu
from jax.sharding import Mesh, PartitionSpec as P

AXES = ("zl", "x", "zh", "y", "co")
ROW = ("zl", "x")
COL = ("zh", "y", "co")
W = 128
VMEM_LIMIT = 56 * 1024 * 1024


def shifted(value, axis, step):
    return lax.ppermute(value, axis, [(i, (i + step) % 4) for i in range(4)])


def swap_cores(value):
    return lax.ppermute(value, "co", [(0, 1), (1, 0)])


def panel_direct_kernel(pos, own_ref, other_ref, out_ref):
    out_ref[...] = jnp.zeros_like(out_ref)
    cols = own_ref.shape[0]
    for part, h_ref in enumerate((own_ref, other_ref)):
        for m in range(cols):
            column = part * cols + m

            def place(s, carry, h_ref=h_ref, m=m, column=column):
                at = pos[column, s]

                @pl.when(at >= 0)
                def _():
                    rows = pl.ds(pl.multiple_of(at * W, W), W)
                    out_ref[rows, column * W : (column + 1) * W] = h_ref[m, s]

                return carry

            lax.fori_loop(0, h_ref.shape[1], place, 0)


def panel_direct(pos, own, other):
    return pl.pallas_call(
        panel_direct_kernel,
        out_shape=jax.ShapeDtypeStruct((4096, 512), jnp.bfloat16),
        in_specs=[
            pl.BlockSpec(memory_space=pltpu.SMEM),
            pl.BlockSpec(memory_space=pltpu.VMEM),
            pl.BlockSpec(memory_space=pltpu.VMEM),
        ],
        out_specs=pl.BlockSpec(memory_space=pltpu.VMEM),
        compiler_params=pltpu.CompilerParams(vmem_limit_bytes=VMEM_LIMIT),
        name="panel_direct",
    )(pos, own, other)


def panel_mirror_kernel(pos, h_ref, out_ref):
    out_ref[...] = jnp.zeros_like(out_ref)
    for m in range(h_ref.shape[0]):

        def place(s, carry, m=m):
            at = pos[m, s]

            @pl.when(at >= 0)
            def _():
                lanes = pl.ds(pl.multiple_of(at * W, W), W)
                out_ref[m * W : (m + 1) * W, lanes] = h_ref[m, s].T

            return carry

        lax.fori_loop(0, h_ref.shape[1], place, 0)


def panel_mirror(pos, h):
    return pl.pallas_call(
        panel_mirror_kernel,
        out_shape=jax.ShapeDtypeStruct((512, 8192), jnp.bfloat16),
        in_specs=[
            pl.BlockSpec(memory_space=pltpu.SMEM),
            pl.BlockSpec(memory_space=pltpu.VMEM),
        ],
        out_specs=pl.BlockSpec(memory_space=pltpu.VMEM),
        compiler_params=pltpu.CompilerParams(vmem_limit_bytes=VMEM_LIMIT),
        name="panel_mirror",
    )(pos, h)


def direct_kernel(places, *refs):
    panel_ref, out_ref = refs[-2], refs[-1]
    total = None
    for where, ref in zip(places, refs[:-2]):
        for t, place in enumerate(where):
            term = jnp.dot(
                ref[t], panel_ref[place * 256 : (place + 1) * 256, :], preferred_element_type=jnp.float32
            )
            total = term if total is None else total + term
    out_ref[...] = total


def direct_part(places, arrays, panel):
    return pl.pallas_call(
        functools.partial(direct_kernel, places),
        out_shape=jax.ShapeDtypeStruct((512, 512), jnp.float32),
        in_specs=[pl.BlockSpec(memory_space=pltpu.VMEM)] * (len(arrays) + 1),
        out_specs=pl.BlockSpec(memory_space=pltpu.VMEM),
        compiler_params=pltpu.CompilerParams(vmem_limit_bytes=VMEM_LIMIT),
        name="direct_part",
    )(*arrays, panel)


def mirror_kernel(places, *refs):
    panel_ref, out_ref = refs[-2], refs[-1]
    total = None
    for where, ref in zip(places, refs[:-2]):
        for t, place in enumerate(where):
            term = jnp.dot(
                panel_ref[:, place * 512 : (place + 1) * 512], ref[t], preferred_element_type=jnp.float32
            )
            total = term if total is None else total + term
    out_ref[...] = total


def mirror_part(places, arrays, panel):
    return pl.pallas_call(
        functools.partial(mirror_kernel, places),
        out_shape=jax.ShapeDtypeStruct((512, 256), jnp.float32),
        in_specs=[pl.BlockSpec(memory_space=pltpu.VMEM)] * (len(arrays) + 1),
        out_specs=pl.BlockSpec(memory_space=pltpu.VMEM),
        compiler_params=pltpu.CompilerParams(vmem_limit_bytes=VMEM_LIMIT),
        name="mirror_part",
    )(*arrays, panel)


def on_device(coeffs, diag_energy, energy, h_blocks, pattern, counts):
    zl, x, zh, y, co = (lax.axis_index(a) for a in AXES)
    row_id = zl * 4 + x
    chip_col = zh * 4 + y
    slots = h_blocks.shape[1]

    half = coeffs.astype(jnp.bfloat16)[None]

    flat = h_blocks.reshape(2, 2 * slots, W, W)
    piece = lax.dynamic_slice(flat, (co, chip_col * 3, 0, 0), (1, 3, W, W))[0]
    turn = [((r * 16 + k) * 2 + c, (k * 16 + r) * 2 + c) for r in range(16) for k in range(16) for c in range(2)]
    piece = lax.ppermute(piece, AXES, turn)
    h_own = lax.all_gather(piece, ROW, axis=0, tiled=True).reshape(2, slots, W, W)
    h_other = swap_cores(h_own)

    filled = jnp.arange(slots, dtype=jnp.int32)[None, :] < counts[:, None]

    blk = lax.dynamic_slice_in_dim(pattern, chip_col * 4, 4, 0)
    live = lax.dynamic_slice_in_dim(filled, chip_col * 4, 4, 0)
    group = blk // 2
    at = (((zh - group // 8) % 4) * 4 + (y - (group // 2) % 4) % 4) * 2 + blk % 2
    at = jnp.where(live & (group % 2 == co), at, -1)
    pos_direct = jnp.where(co == 0, at, jnp.concatenate([at[2:], at[:2]], axis=0))

    blk = lax.dynamic_slice_in_dim(pattern, row_id * 4, 4, 0)
    live = lax.dynamic_slice_in_dim(filled, row_id * 4, 4, 0)
    owner = blk // 4
    at = (((zl - owner // 4) % 4) * 4 + (x - owner % 4) % 4) * 4 + blk % 4
    pos_mirror = jnp.where(live, at, -1)

    panel_m = panel_mirror(pos_mirror, h_blocks)
    panel_d = panel_direct(pos_direct, h_own, h_other)

    zh1, zh3 = shifted(half, "zh", 1), shifted(half, "zh", 3)
    zl_tiles = [shifted(half, "zl", d) for d in (1, 2, 3)]
    zh2 = shifted(half, "zh", 2)
    y0 = [half] + [shifted(half, "y", d) for d in (1, 2, 3)]
    x0 = [half] + [shifted(half, "x", d) for d in (1, 2, 3)]
    near = jnp.concatenate([zh1, zh3], axis=0)
    y13 = [near] + [shifted(near, "y", d) for d in (1, 2, 3)]
    mine = jnp.concatenate(zl_tiles, axis=0)
    x123 = [mine] + [shifted(mine, "x", d) for d in (1, 2, 3)]
    y2 = [zh2] + [shifted(zh2, "y", d) for d in (1, 2, 3)]

    mirror = mirror_part([(d,) for d in range(4)], x0, panel_m)
    direct = direct_part([(d,) for d in range(4)], y0, panel_d)
    direct = direct + direct_part([(4 + d, 12 + d) for d in range(4)], y13, panel_d)
    mirror = mirror + mirror_part([(4 + d, 8 + d, 12 + d) for d in range(4)], x123, panel_m)
    direct = direct + direct_part([(8 + d,) for d in range(4)], y2, panel_d)
    direct_term = direct[:, :256] + swap_cores(direct[:, 256:])
    sigma_full = direct_term + mirror + diag_energy * coeffs
    shift_value = energy[0]
    return (sigma_full - shift_value * coeffs) / jnp.maximum(jnp.abs(diag_energy - shift_value), 1.0)


def solution(mesh):
    fine = Mesh(mesh.devices.reshape(4, 4, 4, 4, 2), AXES)
    placed = (P(ROW, COL), P(ROW, COL), P(), P(ROW, None, None, None), P(), P())
    return jax.shard_map(on_device, mesh=fine, in_specs=placed, out_specs=P(ROW, COL), check_vma=False)
```

time: 316 us -> 321 us (1.016)
  the two profiles are of different devices: /device:TPU:16 before, /device:TPU:123 now
where the time goes in v1:
time: 321 us; the launch traced here: 320 us
  waiting for transfers between devices  149 us (46%)
  starting transfers between devices  100 us (31%)
  Pallas kernels  41.9 us (13%)
  between operations  14.6 us (5%)
  local copies, waits for them, and re-layouts  8.35 us (3%)
  other arithmetic  6.72 us (2%)
    all_gather x1, waiting for transfers between devices, on_device(): lax.all_gather(piece, ROW, axis=0, tiled=True).reshape(2, slots, W, W)  78.2 us
    ppermute x21, starting transfers between devices, shifted(): return lax.ppermute(value, axis, [(i, (i + step) % 4) for i in range(4)])  70.8 us
    ppermute x21, waiting for transfers between devices, shifted(): return lax.ppermute(value, axis, [(i, (i + step) % 4) for i in range(4)])  66.9 us
    ppermute x2, starting transfers between devices, swap_cores(): return lax.ppermute(value, 'co', [(0, 1), (1, 0)])  15.9 us
    pallas_call x3, Pallas kernels, direct_part(): pl.pallas_call(functools.partial(direct_kernel, places), out_shape=jax.Sh...  13.5 us
    ppermute x1, starting transfers between devices, on_device(): piece = lax.ppermute(piece, AXES, turn)  13.3 us
    pallas_call x2, Pallas kernels, mirror_part(): pl.pallas_call(functools.partial(mirror_kernel, places), out_shape=jax.Sh...  12.2 us
    pallas_call x1, Pallas kernels, panel_mirror(): pl.pallas_call(panel_mirror_kernel, out_shape=jax.ShapeDtypeStruct((512,...  10.1 us
  transfers between devices with their start and end apart: 25, of which 8 were waited for; matrix products, arithmetic and copies ran while one was open for 3% of the time, Pallas kernels for 13%

profile of v1, /device:TPU:123, one launch (start us, length us, event | category | flops | bytes accessed | tf_op | source)
XLA Modules:
  0.0 320.2 jit_solution(7466895050286970806)
XLA Ops:
  7.4 13.3 %collective-permute-start.3 = (bf16[3,128,128]{2,1,0:T(8,128)(2,1)S(1)}, bf16[3,128,128]{2,1,0:T(8,128)(2,1)S(1)}, u32[]{:S(2)}, u32[]{:S(2)}) collective-permute-start(bf16[3,128,128]{2,1,0:T(8,128)(2,1)S(1)} %dynamic-slice_bitcast_fusion), channel_id=1, source_target_pairs={{0,0},{1,1},{2,32},{3,33},{4,64},{5,65},{6,96},{7,97},{8,128},{9,1... | collective-permute-start | bytes 294920 | tf_op jit(solution)/shard_map/ppermute | solution.py:148
  20.8 3.5 %collective-permute-done.3 = bf16[3,128,128]{2,1,0:T(8,128)(2,1)S(1)} collective-permute-done((bf16[3,128,128]{2,1,0:T(8,128)(2,1)S(1)}, bf16[3,128,128]{2,1,0:T(8,128)(2,1)S(1)}, u32[]{:S(2)}, u32[]{:S(2)}) %collective-permute-start.3) | collective-permute-done | bytes 98336 | tf_op jit(solution)/shard_map/ppermute | solution.py:148
  24.9 78.2 %all-gather.2.cloned.1.call-done = bf16[48,128,128]{2,1,0:T(8,128)(2,1)} async-done(((bf16[3,128,128]{2,1,0:T(8,128)(2,1)}), bf16[48,128,128]{2,1,0:T(8,128)(2,1)}) %all-gather.2.cloned.1.call-update) | async-done | bytes 1572880 | tf_op jit(solution)/shard_map/all_gather | solution.py:149
  103.1 12.5 %collective-permute-start.4 = (bf16[2,24,128,128]{3,2,1,0:T(8,128)(2,1)}, bf16[2,24,128,128]{3,2,1,0:T(8,128)(2,1)S(1)}, u32[]{:S(2)}, u32[]{:S(2)}) collective-permute-start(bf16[2,24,128,128]{3,2,1,0:T(8,128)(2,1)} %bitcast.9), channel_id=1, source_target_pairs={{0,1},{1,0},{2,3},{3,2},{4,5},{5,4},{6,7},{7,6},{8,9},{9,8},{10,11... | collective-permute-start | bytes 4718600 | tf_op jit(solution)/shard_map/ppermute | solution.py:22
  116.7 10.0 %collective-permute-start.10 = (bf16[1,512,256]{2,1,0:T(8,128)(2,1)S(1)}, bf16[1,512,256]{2,1,0:T(8,128)(2,1)S(1)}, u32[]{:S(2)}, u32[]{:S(2)}) collective-permute-start(bf16[1,512,256]{2,1,0:T(8,128)(2,1)S(1)} %convert_bitcast_fusion.refs_0_), channel_id=1, source_target_pairs={{0,16},{8,24},{16,0},{24,8},{1,17},{9,25},{17,1},{25,9},{2,18},{10... | collective-permute-start | bytes 786440 | tf_op jit(solution)/shard_map/ppermute | solution.py:18
  128.8 2.6 collective-permute-start.5
  131.4 6.6 %collective-permute-start.6 = (bf16[1,512,256]{2,1,0:T(8,128)(2,1)S(1)}, bf16[1,512,256]{2,1,0:T(8,128)(2,1)S(1)}, u32[]{:S(2)}, u32[]{:S(2)}) collective-permute-start(bf16[1,512,256]{2,1,0:T(8,128)(2,1)S(1)} %convert_bitcast_fusion.refs_0_), channel_id=1, source_target_pairs={{0,24},{8,0},{16,8},{24,16},{1,25},{9,1},{17,9},{25,17},{2,26},{10... | collective-permute-start | bytes 786440 | tf_op jit(solution)/shard_map/ppermute | solution.py:18
  138.8 24.8 %collective-permute-done.10.refs_0_ = bf16[1,512,256]{2,1,0:T(8,128)(2,1)S(1)} collective-permute-done((bf16[1,512,256]{2,1,0:T(8,128)(2,1)S(1)}, bf16[1,512,256]{2,1,0:T(8,128)(2,1)S(1)}, u32[]{:S(2)}, u32[]{:S(2)}) %collective-permute-start.10) | collective-permute-done | bytes 262176 | tf_op jit(solution)/shard_map/ppermute | solution.py:18
  169.1 3.4 %collective-permute-start.20 = (bf16[1,512,256]{2,1,0:T(8,128)(2,1)S(1)}, bf16[1,512,256]{2,1,0:T(8,128)(2,1)}, u32[]{:S(2)}, u32[]{:S(2)}) collective-permute-start(bf16[1,512,256]{2,1,0:T(8,128)(2,1)S(1)} %convert_bitcast_fusion.refs_0_), channel_id=1, source_target_pairs={{0,384},{128,0},{256,128},{384,256},{1,385},{129,1},{257,129},{385... | collective-permute-start | bytes 786440 | tf_op jit(solution)/shard_map/ppermute | solution.py:18
  176.2 3.1 collective-permute-start.12
  180.3 12.9 %collective-permute-done.19 = bf16[1,512,256]{2,1,0:T(8,128)(2,1)} collective-permute-done((bf16[1,512,256]{2,1,0:T(8,128)(2,1)S(1)}, bf16[1,512,256]{2,1,0:T(8,128)(2,1)}, u32[]{:S(2)}, u32[]{:S(2)}) %collective-permute-start.19) | collective-permute-done | bytes 262176 | tf_op jit(solution)/shard_map/ppermute | solution.py:18
  193.2 2.5 collective-permute-start.13
  195.8 4.0 %collective-permute-start.7 = (bf16[2,512,256]{2,1,0:T(8,128)(2,1)S(1)}, bf16[2,512,256]{2,1,0:T(8,128)(2,1)S(1)}, u32[]{:S(2)}, u32[]{:S(2)}) collective-permute-start(bf16[2,512,256]{2,1,0:T(8,128)(2,1)S(1)} %constant_dynamic-update-slice_fusion.refs_0_), channel_id=1, source_target_pairs={{0,2},{2,4},{4,6},{6,0},{1,3},{3,5},{5,7},{7,1},{8,10},{10,12},{12... | collective-permute-start | bytes 1572872 | tf_op jit(solution)/shard_map/ppermute | solution.py:18
  201.8 2.5 collective-permute-start.9
  204.9 4.3 %collective-permute-start.1 = (bf16[1,512,256]{2,1,0:T(8,128)(2,1)S(1)}, bf16[1,512,256]{2,1,0:T(8,128)(2,1)S(1)}, u32[]{:S(2)}, u32[]{:S(2)}) collective-permute-start(bf16[1,512,256]{2,1,0:T(8,128)(2,1)S(1)} %convert_bitcast_fusion.refs_0_), channel_id=1, source_target_pairs={{0,4},{2,6},{4,0},{6,2},{1,5},{3,7},{5,1},{7,3},{8,12},{10,14},{12... | collective-permute-start | bytes 786440 | tf_op jit(solution)/shard_map/ppermute | solution.py:18
  209.2 2.2 collective-permute-start.2
  213.4 6.0 %panel_direct.1.refs_4_ = bf16[4096,512]{1,0:T(8,128)(2,1)} custom-call(s32[4,24]{1,0:T(4,128)} %add_select_fusion.14.pos, bf16[2,24,128,128]{3,2,1,0:T(8,128)(2,1)} %bitcast.10, bf16[2,24,128,128]{3,2,1,0:T(8,128)(2,1)} %copy-done.6), custom_call_target="tpu_custom_call" | custom-call | tf_op jit(solution)/shard_map/panel_direct/pallas_call | solution.py:46
  219.5 4.2 %direct_part.5 = f32[512,512]{1,0:T(8,128)} custom-call(bf16[1,512,256]{2,1,0:T(8,128)(2,1)} %copy-done.17, bf16[1,512,256]{2,1,0:T(8,128)(2,1)} %copy-done.18, bf16[1,512,256]{2,1,0:T(8,128)(2,1)} %copy-done.19, bf16[1,512,256]{2,1,0:T(8,128)(2,1)} %copy-done.21, bf16[4096,512]{1,0:T(8,128)(2,1)} %panel_direct.1.refs_4_), custom_call_target="tpu_custom_call" | custom-call | tf_op jit(solution)/shard_map/direct_part/pallas_call | solution.py:104
  223.7 8.8 %collective-permute-done.1.refs_2_ = bf16[1,512,256]{2,1,0:T(8,128)(2,1)S(1)} collective-permute-done((bf16[1,512,256]{2,1,0:T(8,128)(2,1)S(1)}, bf16[1,512,256]{2,1,0:T(8,128)(2,1)S(1)}, u32[]{:S(2)}, u32[]{:S(2)}) %collective-permute-start.1) | collective-permute-done | bytes 262176 | tf_op jit(solution)/shard_map/ppermute | solution.py:18
  232.5 3.2 %collective-permute-start.15 = (bf16[1,512,256]{2,1,0:T(8,128)(2,1)S(1)}, bf16[1,512,256]{2,1,0:T(8,128)(2,1)S(1)}, u32[]{:S(2)}, u32[]{:S(2)}) collective-permute-start(bf16[1,512,256]{2,1,0:T(8,128)(2,1)S(1)} %convert_bitcast_fusion.refs_0_), channel_id=1, source_target_pairs={{0,32},{32,64},{64,96},{96,0},{1,33},{33,65},{65,97},{97,1},{2,34}... | collective-permute-start | bytes 786440 | tf_op jit(solution)/shard_map/ppermute | solution.py:18
  235.7 3.8 %collective-permute-done.2.refs_3_ = bf16[1,512,256]{2,1,0:T(8,128)(2,1)S(1)} collective-permute-done((bf16[1,512,256]{2,1,0:T(8,128)(2,1)S(1)}, bf16[1,512,256]{2,1,0:T(8,128)(2,1)S(1)}, u32[]{:S(2)}, u32[]{:S(2)}) %collective-permute-start.2) | collective-permute-done | bytes 262176 | tf_op jit(solution)/shard_map/ppermute | solution.py:18
  239.5 5.0 %collective-permute-start.16 = (bf16[1,512,256]{2,1,0:T(8,128)(2,1)S(1)}, bf16[1,512,256]{2,1,0:T(8,128)(2,1)}, u32[]{:S(2)}, u32[]{:S(2)}) collective-permute-start(bf16[1,512,256]{2,1,0:T(8,128)(2,1)S(1)} %convert_bitcast_fusion.refs_0_), channel_id=1, source_target_pairs={{0,64},{32,96},{64,0},{96,32},{1,65},{33,97},{65,1},{97,33},{2,66}... | collective-permute-start | bytes 786440 | tf_op jit(solution)/shard_map/ppermute | solution.py:18
  244.5 4.2 %direct_part.3 = f32[512,512]{1,0:T(8,128)} custom-call(bf16[1,512,256]{2,1,0:T(8,128)(2,1)} %copy-done.2, bf16[1,512,256]{2,1,0:T(8,128)(2,1)} %copy-done.16, bf16[1,512,256]{2,1,0:T(8,128)(2,1)} %copy-done.22, bf16[1,512,256]{2,1,0:T(8,128)(2,1)} %copy-done.23, bf16[4096,512]{1,0:T(8,128)(2,1)} %panel_direct.1.refs_4_), custom_call_target="tpu_custom_call" | custom-call | tf_op jit(solution)/shard_map/direct_part/pallas_call | solution.py:104
  248.8 2.2 collective-permute-start.21
  251.0 3.7 %collective-permute-start.22 = (bf16[3,512,256]{2,1,0:T(8,128)(2,1)S(1)}, bf16[3,512,256]{2,1,0:T(8,128)(2,1)S(1)}, u32[]{:S(2)}, u32[]{:S(2)}) collective-permute-start(bf16[3,512,256]{2,1,0:T(8,128)(2,1)S(1)} %constant_dynamic-update-slice_fusion.2.refs_0_), channel_id=1, source_target_pairs={{0,64},{32,96},{64,0},{96,32},{1,65},{33,97},{65,1},{97,33},{2,66}... | collective-permute-start | bytes 2359304 | tf_op jit(solution)/shard_map/ppermute | solution.py:18
  256.9 5.1 %direct_part.4 = f32[512,512]{1,0:T(8,128)} custom-call(bf16[2,512,256]{2,1,0:T(8,128)(2,1)} %copy-done.8, bf16[2,512,256]{2,1,0:T(8,128)(2,1)} %copy-done.12, bf16[2,512,256]{2,1,0:T(8,128)(2,1)} %copy-done.13, bf16[2,512,256]{2,1,0:T(8,128)(2,1)} %copy-done.14, bf16[4096,512]{1,0:T(8,128)(2,1)} %panel_direct.1.refs_4_), custom_call_target="tpu_custom_call" | custom-call | tf_op jit(solution)/shard_map/direct_part/pallas_call | solution.py:104
  263.7 3.4 %collective-permute-start.14 = (f32[512,256]{1,0:T(8,128)S(1)}, f32[512,256]{1,0:T(8,128)S(1)}, u32[]{:S(2)}, u32[]{:S(2)}) collective-permute-start(f32[512,256]{1,0:T(8,128)S(1)} %slice.17), channel_id=1, source_target_pairs={{0,1},{1,0},{2,3},{3,2},{4,5},{5,4},{6,7},{7,6},{8,9},{9,8},{10,11... | collective-permute-start | bytes 1572872 | tf_op jit(solution)/shard_map/ppermute | solution.py:22
  267.1 3.5 %collective-permute-start.17 = (bf16[1,512,256]{2,1,0:T(8,128)(2,1)S(1)}, bf16[1,512,256]{2,1,0:T(8,128)(2,1)S(1)}, u32[]{:S(2)}, u32[]{:S(2)}) collective-permute-start(bf16[1,512,256]{2,1,0:T(8,128)(2,1)S(1)} %copy-done.3), channel_id=1, source_target_pairs={{0,96},{32,0},{64,32},{96,64},{1,97},{33,1},{65,33},{97,65},{2,98}... | collective-permute-start | bytes 786440 | tf_op jit(solution)/shard_map/ppermute | solution.py:18
  270.7 10.1 %panel_mirror.1.refs_4_ = bf16[512,8192]{1,0:T(8,128)(2,1)} custom-call(s32[4,24]{1,0:T(4,128)} %get-tuple-element.7.pos, bf16[4,24,128,128]{3,2,1,0:T(8,128)(2,1)} %h_ref.1), custom_call_target="tpu_custom_call" | custom-call | tf_op jit(solution)/shard_map/panel_mirror/pallas_call | solution.py:78
  281.5 14.8 %collective-permute-done.17.refs_3_ = bf16[1,512,256]{2,1,0:T(8,128)(2,1)S(1)} collective-permute-done((bf16[1,512,256]{2,1,0:T(8,128)(2,1)S(1)}, bf16[1,512,256]{2,1,0:T(8,128)(2,1)S(1)}, u32[]{:S(2)}, u32[]{:S(2)}) %collective-permute-start.17) | collective-permute-done | bytes 262176 | tf_op jit(solution)/shard_map/ppermute | solution.py:18
  297.0 5.2 %mirror_part.2 = f32[512,256]{1,0:T(8,128)} custom-call(bf16[1,512,256]{2,1,0:T(8,128)(2,1)} %copy-done.2, bf16[1,512,256]{2,1,0:T(8,128)(2,1)} %copy-done.20, bf16[1,512,256]{2,1,0:T(8,128)(2,1)} %collective-permute-done.16.refs_2_, bf16[1,512,256]{2,1,0:T(8,128)(2,1)} %copy-done.24, bf16[512,8192]{1,0:T(8,128)(2,1)} %panel_mirror.1.refs_4_), custom_call_target="tpu_custom_call" | custom-call | tf_op jit(solution)/shard_map/mirror_part/pallas_call | solution.py:127
  304.3 7.0 %mirror_part.3 = f32[512,256]{1,0:T(8,128)} custom-call(bf16[3,512,256]{2,1,0:T(8,128)(2,1)} %copy-done.7, bf16[3,512,256]{2,1,0:T(8,128)(2,1)} %copy-done.9, bf16[3,512,256]{2,1,0:T(8,128)(2,1)} %copy-done.10, bf16[3,512,256]{2,1,0:T(8,128)(2,1)} %copy-done.11, bf16[512,8192]{1,0:T(8,128)(2,1)} %panel_mirror.1.refs_4_), custom_call_target="tpu_custom_call" | custom-call | tf_op jit(solution)/shard_map/mirror_part/pallas_call | solution.py:127
  (97 shorter events, 28.9 us)
Async XLA Ops:
  6.5 96.6 %all-gather.2.cloned.1.call-start = ((), (), s32[]{:S(2)}) async-start(), calls=%async_computation | async-start | bytes 1671168 | tf_op jit(solution)/shard_map/all_gather | solution.py:149
  7.4 16.8 %collective-permute-start.3 = (bf16[3,128,128]{2,1,0:T(8,128)(2,1)S(1)}, bf16[3,128,128]{2,1,0:T(8,128)(2,1)S(1)}, u32[]{:S(2)}, u32[]{:S(2)}) collective-permute-start(bf16[3,128,128]{2,1,0:T(8,128)(2,1)S(1)} %dynamic-slice_bitcast_fusion), channel_id=1, source_target_pairs={{0,0},{1,1},{2,32},{3,33},{4,64},{5,65},{6,96},{7,97},{8,128},{9,1... | collective-permute-start | bytes 294920 | tf_op jit(solution)/shard_map/ppermute | solution.py:148
  103.1 106.0 %collective-permute-start.4 = (bf16[2,24,128,128]{3,2,1,0:T(8,128)(2,1)}, bf16[2,24,128,128]{3,2,1,0:T(8,128)(2,1)S(1)}, u32[]{:S(2)}, u32[]{:S(2)}) collective-permute-start(bf16[2,24,128,128]{3,2,1,0:T(8,128)(2,1)} %bitcast.9), channel_id=1, source_target_pairs={{0,1},{1,0},{2,3},{3,2},{4,5},{5,4},{6,7},{7,6},{8,9},{9,8},{10,11... | collective-permute-start | bytes 4718600 | tf_op jit(solution)/shard_map/ppermute | solution.py:22
  116.7 122.8 %copy-start.2 = (bf16[1,512,256]{2,1,0:T(8,128)(2,1)}, bf16[1,512,256]{2,1,0:T(8,128)(2,1)S(1)}, u32[]{:S(2)}) copy-start(bf16[1,512,256]{2,1,0:T(8,128)(2,1)S(1)} %convert_bitcast_fusion.refs_0_) | copy-start | bytes 786436
  116.7 46.9 %collective-permute-start.10 = (bf16[1,512,256]{2,1,0:T(8,128)(2,1)S(1)}, bf16[1,512,256]{2,1,0:T(8,128)(2,1)S(1)}, u32[]{:S(2)}, u32[]{:S(2)}) collective-permute-start(bf16[1,512,256]{2,1,0:T(8,128)(2,1)S(1)} %convert_bitcast_fusion.refs_0_), channel_id=1, source_target_pairs={{0,16},{8,24},{16,0},{24,8},{1,17},{9,25},{17,1},{25,9},{2,18},{10... | collective-permute-start | bytes 786440 | tf_op jit(solution)/shard_map/ppermute | solution.py:18
  126.7 40.5 %collective-permute-start = (bf16[1,512,256]{2,1,0:T(8,128)(2,1)S(1)}, bf16[1,512,256]{2,1,0:T(8,128)(2,1)S(1)}, u32[]{:S(2)}, u32[]{:S(2)}) collective-permute-start(bf16[1,512,256]{2,1,0:T(8,128)(2,1)S(1)} %convert_bitcast_fusion.refs_0_), channel_id=1, source_target_pairs={{0,2},{2,4},{4,6},{6,0},{1,3},{3,5},{5,7},{7,1},{8,10},{10,12},{12... | collective-permute-start | bytes 786440 | tf_op jit(solution)/shard_map/ppermute | solution.py:18
  128.8 40.3 %collective-permute-start.5 = (bf16[1,512,256]{2,1,0:T(8,128)(2,1)S(1)}, bf16[1,512,256]{2,1,0:T(8,128)(2,1)S(1)}, u32[]{:S(2)}, u32[]{:S(2)}) collective-permute-start(bf16[1,512,256]{2,1,0:T(8,128)(2,1)S(1)} %convert_bitcast_fusion.refs_0_), channel_id=1, source_target_pairs={{0,8},{8,16},{16,24},{24,0},{1,9},{9,17},{17,25},{25,1},{2,10},{10... | collective-permute-start | bytes 786440 | tf_op jit(solution)/shard_map/ppermute | solution.py:18
  131.4 41.1 %collective-permute-start.6 = (bf16[1,512,256]{2,1,0:T(8,128)(2,1)S(1)}, bf16[1,512,256]{2,1,0:T(8,128)(2,1)S(1)}, u32[]{:S(2)}, u32[]{:S(2)}) collective-permute-start(bf16[1,512,256]{2,1,0:T(8,128)(2,1)S(1)} %convert_bitcast_fusion.refs_0_), channel_id=1, source_target_pairs={{0,24},{8,0},{16,8},{24,16},{1,25},{9,1},{17,9},{25,17},{2,26},{10... | collective-permute-start | bytes 786440 | tf_op jit(solution)/shard_map/ppermute | solution.py:18
  163.6 55.8 %copy-start.17 = (bf16[1,512,256]{2,1,0:T(8,128)(2,1)}, bf16[1,512,256]{2,1,0:T(8,128)(2,1)S(1)}, u32[]{:S(2)}) copy-start(bf16[1,512,256]{2,1,0:T(8,128)(2,1)S(1)} %collective-permute-done.10.refs_0_) | copy-start | bytes 786436
  163.6 12.7 %collective-permute-start.18 = (bf16[1,512,256]{2,1,0:T(8,128)(2,1)S(1)}, bf16[1,512,256]{2,1,0:T(8,128)(2,1)S(1)}, u32[]{:S(2)}, u32[]{:S(2)}) collective-permute-start(bf16[1,512,256]{2,1,0:T(8,128)(2,1)S(1)} %convert_bitcast_fusion.refs_0_), channel_id=1, source_target_pairs={{0,128},{128,256},{256,384},{384,0},{1,129},{129,257},{257,385},{3... | collective-permute-start | bytes 786440 | tf_op jit(solution)/shard_map/ppermute | solution.py:18
  167.2 52.3 %copy-start.16 = (bf16[1,512,256]{2,1,0:T(8,128)(2,1)}, bf16[1,512,256]{2,1,0:T(8,128)(2,1)S(1)}, u32[]{:S(2)}) copy-start(bf16[1,512,256]{2,1,0:T(8,128)(2,1)S(1)} %collective-permute-done.refs_1_) | copy-start | bytes 786436
  167.2 26.1 %collective-permute-start.19 = (bf16[1,512,256]{2,1,0:T(8,128)(2,1)S(1)}, bf16[1,512,256]{2,1,0:T(8,128)(2,1)}, u32[]{:S(2)}, u32[]{:S(2)}) collective-permute-start(bf16[1,512,256]{2,1,0:T(8,128)(2,1)S(1)} %convert_bitcast_fusion.refs_0_), channel_id=1, source_target_pairs={{0,256},{128,384},{256,0},{384,128},{1,257},{129,385},{257,1},{385... | collective-permute-start | bytes 786440 | tf_op jit(solution)/shard_map/ppermute | solution.py:18
  169.1 26.7 %collective-permute-start.20 = (bf16[1,512,256]{2,1,0:T(8,128)(2,1)S(1)}, bf16[1,512,256]{2,1,0:T(8,128)(2,1)}, u32[]{:S(2)}, u32[]{:S(2)}) collective-permute-start(bf16[1,512,256]{2,1,0:T(8,128)(2,1)S(1)} %convert_bitcast_fusion.refs_0_), channel_id=1, source_target_pairs={{0,384},{128,0},{256,128},{384,256},{1,385},{129,1},{257,129},{385... | collective-permute-start | bytes 786440 | tf_op jit(solution)/shard_map/ppermute | solution.py:18
  172.5 27.3 %collective-permute-start.11 = (bf16[1,512,256]{2,1,0:T(8,128)(2,1)S(1)}, bf16[1,512,256]{2,1,0:T(8,128)(2,1)S(1)}, u32[]{:S(2)}, u32[]{:S(2)}) collective-permute-start(bf16[1,512,256]{2,1,0:T(8,128)(2,1)S(1)} %collective-permute-done.10.refs_0_), channel_id=1, source_target_pairs={{0,2},{2,4},{4,6},{6,0},{1,3},{3,5},{5,7},{7,1},{8,10},{10,12},{12... | collective-permute-start | bytes 786440 | tf_op jit(solution)/shard_map/ppermute | solution.py:18
  176.2 25.5 %collective-permute-start.12 = (bf16[1,512,256]{2,1,0:T(8,128)(2,1)S(1)}, bf16[1,512,256]{2,1,0:T(8,128)(2,1)S(1)}, u32[]{:S(2)}, u32[]{:S(2)}) collective-permute-start(bf16[1,512,256]{2,1,0:T(8,128)(2,1)S(1)} %collective-permute-done.10.refs_0_), channel_id=1, source_target_pairs={{0,4},{2,6},{4,0},{6,2},{1,5},{3,7},{5,1},{7,3},{8,12},{10,14},{12... | collective-permute-start | bytes 786440 | tf_op jit(solution)/shard_map/ppermute | solution.py:18
  193.2 11.6 %collective-permute-start.13 = (bf16[1,512,256]{2,1,0:T(8,128)(2,1)S(1)}, bf16[1,512,256]{2,1,0:T(8,128)(2,1)S(1)}, u32[]{:S(2)}, u32[]{:S(2)}) collective-permute-start(bf16[1,512,256]{2,1,0:T(8,128)(2,1)S(1)} %collective-permute-done.10.refs_0_), channel_id=1, source_target_pairs={{0,6},{2,0},{4,2},{6,4},{1,7},{3,1},{5,3},{7,5},{8,14},{10,8},{12,... | collective-permute-start | bytes 786440 | tf_op jit(solution)/shard_map/ppermute | solution.py:18
  195.7 23.7 %copy-start.8 = (bf16[2,512,256]{2,1,0:T(8,128)(2,1)}, bf16[2,512,256]{2,1,0:T(8,128)(2,1)S(1)}, u32[]{:S(2)}) copy-start(bf16[2,512,256]{2,1,0:T(8,128)(2,1)S(1)} %constant_dynamic-update-slice_fusion.refs_0_) | copy-start | bytes 1572868
  195.8 53.0 %collective-permute-start.7 = (bf16[2,512,256]{2,1,0:T(8,128)(2,1)S(1)}, bf16[2,512,256]{2,1,0:T(8,128)(2,1)S(1)}, u32[]{:S(2)}, u32[]{:S(2)}) collective-permute-start(bf16[2,512,256]{2,1,0:T(8,128)(2,1)S(1)} %constant_dynamic-update-slice_fusion.refs_0_), channel_id=1, source_target_pairs={{0,2},{2,4},{4,6},{6,0},{1,3},{3,5},{5,7},{7,1},{8,10},{10,12},{12... | collective-permute-start | bytes 1572872 | tf_op jit(solution)/shard_map/ppermute | solution.py:18
  199.8 19.6 %copy-start.18 = (bf16[1,512,256]{2,1,0:T(8,128)(2,1)}, bf16[1,512,256]{2,1,0:T(8,128)(2,1)S(1)}, u32[]{:S(2)}) copy-start(bf16[1,512,256]{2,1,0:T(8,128)(2,1)S(1)} %collective-permute-done.11.refs_1_) | copy-start | bytes 786436
  199.8 51.1 %collective-permute-start.8 = (bf16[2,512,256]{2,1,0:T(8,128)(2,1)S(1)}, bf16[2,512,256]{2,1,0:T(8,128)(2,1)S(1)}, u32[]{:S(2)}, u32[]{:S(2)}) collective-permute-start(bf16[2,512,256]{2,1,0:T(8,128)(2,1)S(1)} %constant_dynamic-update-slice_fusion.refs_0_), channel_id=1, source_target_pairs={{0,4},{2,6},{4,0},{6,2},{1,5},{3,7},{5,1},{7,3},{8,12},{10,14},{12... | collective-permute-start | bytes 1572872 | tf_op jit(solution)/shard_map/ppermute | solution.py:18
  201.8 17.7 %copy-start.19 = (bf16[1,512,256]{2,1,0:T(8,128)(2,1)}, bf16[1,512,256]{2,1,0:T(8,128)(2,1)S(1)}, u32[]{:S(2)}) copy-start(bf16[1,512,256]{2,1,0:T(8,128)(2,1)S(1)} %collective-permute-done.12.refs_2_) | copy-start | bytes 786436
  201.8 52.9 %collective-permute-start.9 = (bf16[2,512,256]{2,1,0:T(8,128)(2,1)S(1)}, bf16[2,512,256]{2,1,0:T(8,128)(2,1)S(1)}, u32[]{:S(2)}, u32[]{:S(2)}) collective-permute-start(bf16[2,512,256]{2,1,0:T(8,128)(2,1)S(1)} %constant_dynamic-update-slice_fusion.refs_0_), channel_id=1, source_target_pairs={{0,6},{2,0},{4,2},{6,4},{1,7},{3,1},{5,3},{7,5},{8,14},{10,8},{12,... | collective-permute-start | bytes 1572872 | tf_op jit(solution)/shard_map/ppermute | solution.py:18
  204.9 27.7 %collective-permute-start.1 = (bf16[1,512,256]{2,1,0:T(8,128)(2,1)S(1)}, bf16[1,512,256]{2,1,0:T(8,128)(2,1)S(1)}, u32[]{:S(2)}, u32[]{:S(2)}) collective-permute-start(bf16[1,512,256]{2,1,0:T(8,128)(2,1)S(1)} %convert_bitcast_fusion.refs_0_), channel_id=1, source_target_pairs={{0,4},{2,6},{4,0},{6,2},{1,5},{3,7},{5,1},{7,3},{8,12},{10,14},{12... | collective-permute-start | bytes 786440 | tf_op jit(solution)/shard_map/ppermute | solution.py:18
  209.2 30.3 %collective-permute-start.2 = (bf16[1,512,256]{2,1,0:T(8,128)(2,1)S(1)}, bf16[1,512,256]{2,1,0:T(8,128)(2,1)S(1)}, u32[]{:S(2)}, u32[]{:S(2)}) collective-permute-start(bf16[1,512,256]{2,1,0:T(8,128)(2,1)S(1)} %convert_bitcast_fusion.refs_0_), channel_id=1, source_target_pairs={{0,6},{2,0},{4,2},{6,4},{1,7},{3,1},{5,3},{7,5},{8,14},{10,8},{12,... | collective-permute-start | bytes 786440 | tf_op jit(solution)/shard_map/ppermute | solution.py:18
  213.4 41.3 %copy-start.7 = (bf16[3,512,256]{2,1,0:T(8,128)(2,1)}, bf16[3,512,256]{2,1,0:T(8,128)(2,1)S(1)}, u32[]{:S(2)}) copy-start(bf16[3,512,256]{2,1,0:T(8,128)(2,1)S(1)} %constant_dynamic-update-slice_fusion.2.refs_0_) | copy-start | bytes 2359300
  232.5 31.2 %collective-permute-start.15 = (bf16[1,512,256]{2,1,0:T(8,128)(2,1)S(1)}, bf16[1,512,256]{2,1,0:T(8,128)(2,1)S(1)}, u32[]{:S(2)}, u32[]{:S(2)}) collective-permute-start(bf16[1,512,256]{2,1,0:T(8,128)(2,1)S(1)} %convert_bitcast_fusion.refs_0_), channel_id=1, source_target_pairs={{0,32},{32,64},{64,96},{96,0},{1,33},{33,65},{65,97},{97,1},{2,34}... | collective-permute-start | bytes 786440 | tf_op jit(solution)/shard_map/ppermute | solution.py:18
  239.5 27.6 %collective-permute-start.16 = (bf16[1,512,256]{2,1,0:T(8,128)(2,1)S(1)}, bf16[1,512,256]{2,1,0:T(8,128)(2,1)}, u32[]{:S(2)}, u32[]{:S(2)}) collective-permute-start(bf16[1,512,256]{2,1,0:T(8,128)(2,1)S(1)} %convert_bitcast_fusion.refs_0_), channel_id=1, source_target_pairs={{0,64},{32,96},{64,0},{96,32},{1,65},{33,97},{65,1},{97,33},{2,66}... | collective-permute-start | bytes 786440 | tf_op jit(solution)/shard_map/ppermute | solution.py:18
  248.8 53.5 %collective-permute-start.21 = (bf16[3,512,256]{2,1,0:T(8,128)(2,1)S(1)}, bf16[3,512,256]{2,1,0:T(8,128)(2,1)S(1)}, u32[]{:S(2)}, u32[]{:S(2)}) collective-permute-start(bf16[3,512,256]{2,1,0:T(8,128)(2,1)S(1)} %constant_dynamic-update-slice_fusion.2.refs_0_), channel_id=1, source_target_pairs={{0,32},{32,64},{64,96},{96,0},{1,33},{33,65},{65,97},{97,1},{2,34}... | collective-permute-start | bytes 2359304 | tf_op jit(solution)/shard_map/ppermute | solution.py:18
  251.0 51.3 %collective-permute-start.22 = (bf16[3,512,256]{2,1,0:T(8,128)(2,1)S(1)}, bf16[3,512,256]{2,1,0:T(8,128)(2,1)S(1)}, u32[]{:S(2)}, u32[]{:S(2)}) collective-permute-start(bf16[3,512,256]{2,1,0:T(8,128)(2,1)S(1)} %constant_dynamic-update-slice_fusion.2.refs_0_), channel_id=1, source_target_pairs={{0,64},{32,96},{64,0},{96,32},{1,65},{33,97},{65,1},{97,33},{2,66}... | collective-permute-start | bytes 2359304 | tf_op jit(solution)/shard_map/ppermute | solution.py:18
  254.7 47.6 %collective-permute-start.23 = (bf16[3,512,256]{2,1,0:T(8,128)(2,1)S(1)}, bf16[3,512,256]{2,1,0:T(8,128)(2,1)S(1)}, u32[]{:S(2)}, u32[]{:S(2)}) collective-permute-start(bf16[3,512,256]{2,1,0:T(8,128)(2,1)S(1)} %constant_dynamic-update-slice_fusion.2.refs_0_), channel_id=1, source_target_pairs={{0,96},{32,0},{64,32},{96,64},{1,97},{33,1},{65,33},{97,65},{2,98}... | collective-permute-start | bytes 2359304 | tf_op jit(solution)/shard_map/ppermute | solution.py:18
  263.7 47.6 %collective-permute-start.14 = (f32[512,256]{1,0:T(8,128)S(1)}, f32[512,256]{1,0:T(8,128)S(1)}, u32[]{:S(2)}, u32[]{:S(2)}) collective-permute-start(f32[512,256]{1,0:T(8,128)S(1)} %slice.17), channel_id=1, source_target_pairs={{0,1},{1,0},{2,3},{3,2},{4,5},{5,4},{6,7},{7,6},{8,9},{9,8},{10,11... | collective-permute-start | bytes 1572872 | tf_op jit(solution)/shard_map/ppermute | solution.py:22
  267.1 29.2 %collective-permute-start.17 = (bf16[1,512,256]{2,1,0:T(8,128)(2,1)S(1)}, bf16[1,512,256]{2,1,0:T(8,128)(2,1)S(1)}, u32[]{:S(2)}, u32[]{:S(2)}) collective-permute-start(bf16[1,512,256]{2,1,0:T(8,128)(2,1)S(1)} %copy-done.3), channel_id=1, source_target_pairs={{0,96},{32,0},{64,32},{96,64},{1,97},{33,1},{65,33},{97,65},{2,98}... | collective-permute-start | bytes 786440 | tf_op jit(solution)/shard_map/ppermute | solution.py:18
  (20 other events, 135.5 us)
Sparse Core Ops, SparseCore 0:
  25.0 78.0 all-gather.1

commit v2 on v0

v2 whole, which is shorter than its diff:
```python
import jax
import jax.numpy as jnp
from jax import lax
from jax.experimental import pallas as pl
from jax.experimental.pallas import tpu as pltpu
from jax.sharding import Mesh, PartitionSpec as P

AXES = ("zl", "x", "zh", "y", "co")
ROW = ("zl", "x")
COL = ("zh", "y", "co")
W = 128
VMEM_LIMIT = 56 * 1024 * 1024
PARAMS = pltpu.CompilerParams(vmem_limit_bytes=VMEM_LIMIT)


def shifted(value, axis, step):
    return lax.ppermute(value, axis, [(i, (i + step) % 4) for i in range(4)])


def swap_cores(value):
    return lax.ppermute(value, "co", [(0, 1), (1, 0)])


def turned(value, cross):
    pairs = [
        ((r * 16 + k) * 2 + c, (k * 16 + r) * 2 + (c ^ cross))
        for r in range(16)
        for k in range(16)
        for c in range(2)
    ]
    return lax.ppermute(value, AXES, pairs)


def pack_kernel(pos, co, h_ref, out_ref):
    out_ref[...] = jnp.zeros_like(out_ref)
    for m in range(2):

        def place(s, carry, m=m):
            at = pos[m, s]

            @pl.when(at >= 0)
            def _():
                out_ref[at, :, m * W : (m + 1) * W] = h_ref[m, s]

            return carry

        lax.fori_loop(0, h_ref.shape[1], place, 0)


def pack(pos, co, h_blocks):
    slots = h_blocks.shape[1]
    return pl.pallas_call(
        pack_kernel,
        out_shape=jax.ShapeDtypeStruct((32, W, 2 * W), jnp.bfloat16),
        grid_spec=pltpu.PrefetchScalarGridSpec(
            num_scalar_prefetch=2,
            grid=(1,),
            in_specs=[pl.BlockSpec((2, slots, W, W), lambda i, pos, co: (co[0], 0, 0, 0))],
            out_specs=pl.BlockSpec((32, W, 2 * W), lambda i, pos, co: (0, 0, 0)),
        ),
        compiler_params=PARAMS,
        name="pack",
    )(pos, co, h_blocks)


def gathered(where, bits, tiles, h_ref, column, pair, take):
    zl = where[0]
    strings, blocks = [], []
    for d, tile in enumerate(tiles):
        owner = lax.rem(zl - d + 4, 4)
        for j in range(2):
            i = owner * 2 + j
            start = pl.multiple_of((2 * j + bits[pair, i]) * W, W)
            strings.append(take(tile, start))
            blocks.append(h_ref[column, i])
    return strings, jnp.concatenate(blocks, axis=0)


def direct_kernel(where, bits, t0, t1, t2, t3, own_ref, other_ref, out_ref, kept_ref):
    for column in range(4):
        for h_ref, half in ((own_ref, where[2]), (other_ref, 1 - where[2])):
            strings, blocks = gathered(
                where,
                bits,
                (t0, t1, t2, t3),
                h_ref,
                column,
                column * 2 + half,
                lambda tile, start: tile[:, pl.ds(start, W)],
            )
            part = jnp.dot(jnp.concatenate(strings, axis=1), blocks, preferred_element_type=jnp.float32)
            lanes = pl.ds(pl.multiple_of(half * 2 * W, 2 * W), 2 * W)
            out_ref[column, :, lanes] = part.astype(jnp.bfloat16)

            @pl.when(where[1] == column)
            def _():
                kept_ref[:, lanes] = part


def mirror_kernel(where, bits, t0, t1, t2, t3, own_ref, other_ref, out_ref, kept_ref):
    for column in range(4):
        for h_ref, half in ((own_ref, where[2]), (other_ref, 1 - where[2])):
            strings, blocks = gathered(
                where,
                bits,
                (t0, t1, t2, t3),
                h_ref,
                column,
                column * 2 + half,
                lambda tile, start: tile[pl.ds(start, W), :],
            )
            part = lax.dot_general(
                blocks,
                jnp.concatenate(strings, axis=0),
                (((0,), (0,)), ((), ())),
                preferred_element_type=jnp.float32,
            )
            rows = pl.ds(pl.multiple_of(half * 2 * W, 2 * W), 2 * W)
            out_ref[column, rows, :] = part.astype(jnp.bfloat16)

            @pl.when(where[1] == column)
            def _():
                kept_ref[rows, :] = part


def partial_sums(kernel, name, where, bits, tiles, own, other):
    shape = tiles[0].shape
    return pl.pallas_call(
        kernel,
        out_shape=(
            jax.ShapeDtypeStruct((4, *shape), jnp.bfloat16),
            jax.ShapeDtypeStruct(shape, jnp.float32),
        ),
        in_specs=[pl.BlockSpec(memory_space=pltpu.SMEM)] * 2 + [pl.BlockSpec(memory_space=pltpu.VMEM)] * 6,
        out_specs=(pl.BlockSpec(memory_space=pltpu.VMEM), pl.BlockSpec(memory_space=pltpu.VMEM)),
        compiler_params=PARAMS,
        name=name,
    )(where, bits, *tiles, own, other)


def summed(parts, kept, x):
    got = lax.all_to_all(parts, "x", 0, 0, tiled=True)
    others = (jnp.arange(4) != x)[:, None, None]
    return kept + jnp.sum(jnp.where(others, got, jnp.zeros_like(got)).astype(jnp.float32), axis=0)


def on_device(coeffs, diag_energy, energy, h_blocks, pattern, counts):
    zl, x, zh, y, co = (lax.axis_index(a).astype(jnp.int32) for a in AXES)
    row_id = zl * 4 + x
    slots = h_blocks.shape[1]

    half = coeffs.astype(jnp.bfloat16)

    first, last = half[:256], half[256:]
    here = turned(jnp.where(co == 0, first, last), 0)
    there = turned(jnp.where(co == 0, last, first), 1)
    tile = jnp.where(
        co == 0, jnp.concatenate([here, there], axis=1), jnp.concatenate([there, here], axis=1)
    )
    direct_tiles = [tile] + [shifted(tile, "zl", d) for d in (1, 2, 3)]
    mirror_tiles = [half] + [shifted(half, "zl", d) for d in (1, 2, 3)]

    filled = jnp.arange(slots, dtype=jnp.int32)[None, :] < counts[:, None]
    begin = row_id * 4 + co * 2
    blk = lax.dynamic_slice_in_dim(pattern, begin, 2, 0)
    live = lax.dynamic_slice_in_dim(filled, begin, 2, 0)
    owner = blk // 4
    at = (owner % 4) * 8 + (owner // 4) * 2 + (blk % 4) // 2
    packed = pack(jnp.where(live, at, -1), co[None], h_blocks)
    own = lax.all_to_all(packed.reshape(4, 8, W, 2 * W), "x", 0, 0, tiled=True)
    other = swap_cores(lax.optimization_barrier((own, tile))[0])

    names = lax.dynamic_slice_in_dim(pattern, zl * 16, 16, 0).reshape(8, 1, 2 * slots)
    i = jnp.arange(8, dtype=jnp.int32)
    odd = (8 * (i // 2) + 2 * x + i % 2) * 2 + 1
    bits = jnp.any(names == odd[None, :, None], axis=2).astype(jnp.int32)
    where = jnp.stack([zl, x, co])

    direct, kept_direct = partial_sums(direct_kernel, "direct", where, bits, direct_tiles, own, other)
    direct = summed(direct, kept_direct, x).astype(jnp.bfloat16)
    left, right = direct[:, :256], direct[:, 256:]
    here = turned(jnp.where(co == 0, left, right), 0)
    there = turned(jnp.where(co == 0, right, left), 1)
    direct_term = jnp.where(
        co == 0, jnp.concatenate([here, there], axis=0), jnp.concatenate([there, here], axis=0)
    ).astype(jnp.float32)

    mirror, kept_mirror = partial_sums(mirror_kernel, "mirror", where, bits, mirror_tiles, own, other)
    mirror_term = summed(mirror, kept_mirror, x)

    sigma_full = direct_term + mirror_term + diag_energy * coeffs
    shift_value = energy[0]
    return (sigma_full - shift_value * coeffs) / jnp.maximum(jnp.abs(diag_energy - shift_value), 1.0)


def solution(mesh):
    fine = Mesh(mesh.devices.reshape(4, 4, 4, 4, 2), AXES)
    placed = (P(ROW, COL), P(ROW, COL), P(), P(ROW, None, None, None), P(), P())
    return jax.shard_map(on_device, mesh=fine, in_specs=placed, out_specs=P(ROW, COL), check_vma=False)
```

time: 316 us -> 170 us (0.54)
  the two profiles are of different devices: /device:TPU:16 before, /device:TPU:102 now
where the time goes in v2:
time: 170 us
  waiting for transfers between devices  77.9 us (46%)
  starting transfers between devices  65.3 us (38%)
  Pallas kernels  18.8 us (11%)
  other arithmetic  4.09 us (2%)
  local copies, waits for them, and re-layouts  2.55 us (1%)
    ppermute x4, waiting for transfers between devices, turned(): return lax.ppermute(value, AXES, pairs)  42.1 us
    ppermute x6, waiting for transfers between devices, shifted(): return lax.ppermute(value, axis, [(i, (i + step) % 4) for i in range(4)])  35.8 us
    ppermute x4, starting transfers between devices, turned(): return lax.ppermute(value, AXES, pairs)  30.8 us
    ppermute x6, starting transfers between devices, shifted(): return lax.ppermute(value, axis, [(i, (i + step) % 4) for i in range(4)])  17.6 us
    pallas_call x2, Pallas kernels, partial_sums(): pl.pallas_call(kernel, out_shape=(jax.ShapeDtypeStruct((4, *shape), jnp.b...  14.4 us
    all_to_all x2, starting transfers between devices, summed(): got = lax.all_to_all(parts, 'x', 0, 0, tiled=True)  10.1 us
    all_to_all x1, starting transfers between devices, on_device(): own = lax.all_to_all(packed.reshape(4, 8, W, 2 * W), 'x', 0, 0, tiled=True)  4.92 us
    pallas_call x1, Pallas kernels, pack(): pl.pallas_call(pack_kernel, out_shape=jax.ShapeDtypeStruct((32, W, 2 * W)...  4.38 us
  transfers between devices with their start and end apart: 14, of which 9 were waited for; matrix products, arithmetic and copies ran while one was open for 2% of the time, Pallas kernels for 4%

profile of v2, /device:TPU:102, one launch (start us, length us, event | category | flops | bytes accessed | tf_op | source)
XLA Modules:
  0.0 169.6 jit_solution(6994984289893003882)
XLA Ops:
  0.0 0.7 copy-done
  0.9 0.7 dynamic-slice
  1.6 0.6 compare_select_fusion.pos
  2.2 4.4 %pack.1 = bf16[32,128,256]{2,1,0:T(8,128)(2,1)} custom-call(s32[2,24]{1,0:T(2,128)} %compare_select_fusion.pos, s32[1]{0:T(128)} %bitcast.2.co, bf16[4,24,128,128]{3,2,1,0:T(8,128)(2,1)} %h_ref.1), custom_call_target="tpu_custom_call" | custom-call | tf_op jit(solution)/shard_map/pack/pallas_call | solution.py:52
  6.6 4.9 %all-to-all-start = ((bf16[4,8,128,256]{3,2,1,0:T(8,128)(2,1)}), bf16[4,8,128,256]{3,2,1,0:T(8,128)(2,1)S(1)}, u32[]{:S(2)}, u32[]{:S(2)}) async-start(bf16[4,8,128,256]{3,2,1,0:T(8,128)(2,1)} %bitcast.6), calls=%async_computation | async-start | bytes 4194304 | tf_op jit(solution)/shard_map/all_to_all | solution.py:170
  11.6 13.2 %collective-permute-start = (bf16[256,256]{1,0:T(8,128)(2,1)S(1)}, bf16[256,256]{1,0:T(8,128)(2,1)S(1)}, u32[]{:S(2)}, u32[]{:S(2)}) collective-permute-start(bf16[256,256]{1,0:T(8,128)(2,1)S(1)} %get-tuple-element.17), channel_id=1, source_target_pairs={{0,0},{1,1},{2,32},{3,33},{4,64},{5,65},{6,96},{7,97},{8,128},{9,1... | collective-permute-start | bytes 393224 | tf_op jit(solution)/shard_map/ppermute | solution.py:31
  24.8 2.0 %collective-permute-start.1 = (bf16[256,256]{1,0:T(8,128)(2,1)S(1)}, bf16[256,256]{1,0:T(8,128)(2,1)S(1)}, u32[]{:S(2)}, u32[]{:S(2)}) collective-permute-start(bf16[256,256]{1,0:T(8,128)(2,1)S(1)} %get-tuple-element.18), channel_id=1, source_target_pairs={{0,1},{1,0},{2,33},{3,32},{4,65},{5,64},{6,97},{7,96},{8,129},{9,1... | collective-permute-start | bytes 393224 | tf_op jit(solution)/shard_map/ppermute | solution.py:31
  26.8 6.8 %collective-permute-done = bf16[256,256]{1,0:T(8,128)(2,1)S(1)} collective-permute-done((bf16[256,256]{1,0:T(8,128)(2,1)S(1)}, bf16[256,256]{1,0:T(8,128)(2,1)S(1)}, u32[]{:S(2)}, u32[]{:S(2)}) %collective-permute-start) | collective-permute-done | bytes 131104 | tf_op jit(solution)/shard_map/ppermute | solution.py:31
  33.7 13.6 %collective-permute-done.1 = bf16[256,256]{1,0:T(8,128)(2,1)S(1)} collective-permute-done((bf16[256,256]{1,0:T(8,128)(2,1)S(1)}, bf16[256,256]{1,0:T(8,128)(2,1)S(1)}, u32[]{:S(2)}, u32[]{:S(2)}) %collective-permute-start.1) | collective-permute-done | bytes 131104 | tf_op jit(solution)/shard_map/ppermute | solution.py:31
  47.4 1.9 %collective-permute-start.5 = (bf16[4,8,128,256]{3,2,1,0:T(8,128)(2,1)S(1)}, bf16[4,8,128,256]{3,2,1,0:T(8,128)(2,1)}, u32[]{:S(2)}, u32[]{:S(2)}) collective-permute-start(bf16[4,8,128,256]{3,2,1,0:T(8,128)(2,1)S(1)} %all-to-all-done.own_ref), channel_id=1, source_target_pairs={{0,1},{1,0},{2,3},{3,2},{4,5},{5,4},{6,7},{7,6},{8,9},{9,8},{10,11... | collective-permute-start | bytes 6291464 | tf_op jit(solution)/shard_map/ppermute | solution.py:21
  49.4 1.9 %collective-permute-start.2 = (bf16[256,512]{1,0:T(8,128)(2,1)S(1)}, bf16[256,512]{1,0:T(8,128)(2,1)S(1)}, u32[]{:S(2)}, u32[]{:S(2)}) collective-permute-start(bf16[256,512]{1,0:T(8,128)(2,1)S(1)} %maximum_select_fusion.t0), channel_id=1, source_target_pairs={{0,128},{128,256},{256,384},{384,0},{1,129},{129,257},{257,385},{3... | collective-permute-start | bytes 786440 | tf_op jit(solution)/shard_map/ppermute | solution.py:17
  51.4 4.3 %collective-permute-start.3 = (bf16[256,512]{1,0:T(8,128)(2,1)S(1)}, bf16[256,512]{1,0:T(8,128)(2,1)}, u32[]{:S(2)}, u32[]{:S(2)}) collective-permute-start(bf16[256,512]{1,0:T(8,128)(2,1)S(1)} %maximum_select_fusion.t0), channel_id=1, source_target_pairs={{0,256},{128,384},{256,0},{384,128},{1,257},{129,385},{257,1},{385... | collective-permute-start | bytes 786440 | tf_op jit(solution)/shard_map/ppermute | solution.py:17
  55.6 1.9 %collective-permute-start.4 = (bf16[256,512]{1,0:T(8,128)(2,1)S(1)}, bf16[256,512]{1,0:T(8,128)(2,1)}, u32[]{:S(2)}, u32[]{:S(2)}) collective-permute-start(bf16[256,512]{1,0:T(8,128)(2,1)S(1)} %maximum_select_fusion.t0), channel_id=1, source_target_pairs={{0,384},{128,0},{256,128},{384,256},{1,385},{129,1},{257,129},{385... | collective-permute-start | bytes 786440 | tf_op jit(solution)/shard_map/ppermute | solution.py:17
  58.6 0.6 pad_add_fusion.where
  59.2 0.8 collective-permute-done.2.t1
  60.0 17.3 %collective-permute-done.3.t2 = bf16[256,512]{1,0:T(8,128)(2,1)} collective-permute-done((bf16[256,512]{1,0:T(8,128)(2,1)S(1)}, bf16[256,512]{1,0:T(8,128)(2,1)}, u32[]{:S(2)}, u32[]{:S(2)}) %collective-permute-start.3) | collective-permute-done | bytes 262176 | tf_op jit(solution)/shard_map/ppermute | solution.py:17
  77.4 7.2 %direct.1 = (bf16[4,256,512]{2,1,0:T(8,128)(2,1)}, f32[256,512]{1,0:T(8,128)}) custom-call(s32[3]{0:T(128)} %pad_add_fusion.where, s32[8,8]{1,0:T(8,128)} %convert_element_type.18.bits, bf16[256,512]{1,0:T(8,128)(2,1)} %copy-done.4, bf16[256,512]{1,0:T(8,128)(2,1)} %copy-done.8, bf16[256,512]{1,0:T(8,128)(2,1)} %collective-permute-done.3.t2, ...), custom_call_target="tpu_custom_call" | custom-call | tf_op jit(solution)/shard_map/direct/pallas_call | solution.py:128
  84.5 5.1 %all-to-all-start.1 = ((bf16[4,256,512]{2,1,0:T(8,128)(2,1)}), bf16[4,256,512]{2,1,0:T(8,128)(2,1)S(1)}, u32[]{:S(2)}, u32[]{:S(2)}) async-start(bf16[4,256,512]{2,1,0:T(8,128)(2,1)} %get-tuple-element.12), calls=%async_computation.1 | async-start | bytes 2097152 | tf_op jit(solution)/shard_map/all_to_all | solution.py:142
  89.7 1.9 %collective-permute-start.10 = (bf16[512,256]{1,0:T(8,128)(2,1)S(1)}, bf16[512,256]{1,0:T(8,128)(2,1)S(1)}, u32[]{:S(2)}, u32[]{:S(2)}) collective-permute-start(bf16[512,256]{1,0:T(8,128)(2,1)S(1)} %convert_element_type.19.t0), channel_id=1, source_target_pairs={{0,384},{128,0},{256,128},{384,256},{1,385},{129,1},{257,129},{385... | collective-permute-start | bytes 786440 | tf_op jit(solution)/shard_map/ppermute | solution.py:17
  91.6 5.7 %collective-permute-start.8 = (bf16[512,256]{1,0:T(8,128)(2,1)S(1)}, bf16[512,256]{1,0:T(8,128)(2,1)S(1)}, u32[]{:S(2)}, u32[]{:S(2)}) collective-permute-start(bf16[512,256]{1,0:T(8,128)(2,1)S(1)} %convert_element_type.19.t0), channel_id=1, source_target_pairs={{0,128},{128,256},{256,384},{384,0},{1,129},{129,257},{257,385},{3... | collective-permute-start | bytes 786440 | tf_op jit(solution)/shard_map/ppermute | solution.py:17
  97.3 1.9 %collective-permute-start.9 = (bf16[512,256]{1,0:T(8,128)(2,1)S(1)}, bf16[512,256]{1,0:T(8,128)(2,1)S(1)}, u32[]{:S(2)}, u32[]{:S(2)}) collective-permute-start(bf16[512,256]{1,0:T(8,128)(2,1)S(1)} %convert_element_type.19.t0), channel_id=1, source_target_pairs={{0,256},{128,384},{256,0},{384,128},{1,257},{129,385},{257,1},{385... | collective-permute-start | bytes 786440 | tf_op jit(solution)/shard_map/ppermute | solution.py:17
  99.9 2.7 %collective-permute-done.10.t3 = bf16[512,256]{1,0:T(8,128)(2,1)S(1)} collective-permute-done((bf16[512,256]{1,0:T(8,128)(2,1)S(1)}, bf16[512,256]{1,0:T(8,128)(2,1)S(1)}, u32[]{:S(2)}, u32[]{:S(2)}) %collective-permute-start.10) | collective-permute-done | bytes 262176 | tf_op jit(solution)/shard_map/ppermute | solution.py:17
  102.6 3.7 %collective-permute-done.8.t1 = bf16[512,256]{1,0:T(8,128)(2,1)S(1)} collective-permute-done((bf16[512,256]{1,0:T(8,128)(2,1)S(1)}, bf16[512,256]{1,0:T(8,128)(2,1)S(1)}, u32[]{:S(2)}, u32[]{:S(2)}) %collective-permute-start.8) | collective-permute-done | bytes 262176 | tf_op jit(solution)/shard_map/ppermute | solution.py:17
  106.3 11.2 %collective-permute-done.9.t2 = bf16[512,256]{1,0:T(8,128)(2,1)S(1)} collective-permute-done((bf16[512,256]{1,0:T(8,128)(2,1)S(1)}, bf16[512,256]{1,0:T(8,128)(2,1)S(1)}, u32[]{:S(2)}, u32[]{:S(2)}) %collective-permute-start.9) | collective-permute-done | bytes 262176 | tf_op jit(solution)/shard_map/ppermute | solution.py:17
  117.6 0.7 copy-done.11
  118.3 7.3 %mirror.1 = (bf16[4,512,256]{2,1,0:T(8,128)(2,1)}, f32[512,256]{1,0:T(8,128)}) custom-call(s32[3]{0:T(128)} %pad_add_fusion.where, s32[8,8]{1,0:T(8,128)} %convert_element_type.18.bits, bf16[512,256]{1,0:T(8,128)(2,1)} %copy-done.2, bf16[512,256]{1,0:T(8,128)(2,1)} %copy-done.10, bf16[512,256]{1,0:T(8,128)(2,1)} %copy-done.11, bf16[512,256]{1,0:T(8,128)(2,1)} %copy-done.9, ...), custom_call_target="tpu_custom_call" | custom-call | tf_op jit(solution)/shard_map/mirror/pallas_call | solution.py:128
  125.5 4.9 %all-to-all-start.2 = ((bf16[4,512,256]{2,1,0:T(8,128)(2,1)}), bf16[4,512,256]{2,1,0:T(8,128)(2,1)S(1)}, u32[]{:S(2)}, u32[]{:S(2)}) async-start(bf16[4,512,256]{2,1,0:T(8,128)(2,1)} %get-tuple-element.14), calls=%async_computation.2 | async-start | bytes 2097152 | tf_op jit(solution)/shard_map/all_to_all | solution.py:142
  130.9 11.3 %collective-permute-start.6 = (bf16[256,256]{1,0:T(8,128)(2,1)S(1)}, bf16[256,256]{1,0:T(8,128)(2,1)S(1)}, u32[]{:S(2)}, u32[]{:S(2)}) collective-permute-start(bf16[256,256]{1,0:T(8,128)(2,1)S(1)} %get-tuple-element.15), channel_id=1, source_target_pairs={{0,0},{1,1},{2,32},{3,33},{4,64},{5,65},{6,96},{7,97},{8,128},{9,1... | collective-permute-start | bytes 393224 | tf_op jit(solution)/shard_map/ppermute | solution.py:31
  142.2 4.3 %collective-permute-start.7 = (bf16[256,256]{1,0:T(8,128)(2,1)S(1)}, bf16[256,256]{1,0:T(8,128)(2,1)S(1)}, u32[]{:S(2)}, u32[]{:S(2)}) collective-permute-start(bf16[256,256]{1,0:T(8,128)(2,1)S(1)} %get-tuple-element.16), channel_id=1, source_target_pairs={{0,1},{1,0},{2,33},{3,32},{4,65},{5,64},{6,97},{7,96},{8,129},{9,1... | collective-permute-start | bytes 393224 | tf_op jit(solution)/shard_map/ppermute | solution.py:31
  146.9 5.9 %collective-permute-done.6 = bf16[256,256]{1,0:T(8,128)(2,1)S(1)} collective-permute-done((bf16[256,256]{1,0:T(8,128)(2,1)S(1)}, bf16[256,256]{1,0:T(8,128)(2,1)S(1)}, u32[]{:S(2)}, u32[]{:S(2)}) %collective-permute-start.6) | collective-permute-done | bytes 131104 | tf_op jit(solution)/shard_map/ppermute | solution.py:31
  152.8 15.7 %collective-permute-done.7 = bf16[256,256]{1,0:T(8,128)(2,1)S(1)} collective-permute-done((bf16[256,256]{1,0:T(8,128)(2,1)S(1)}, bf16[256,256]{1,0:T(8,128)(2,1)S(1)}, u32[]{:S(2)}, u32[]{:S(2)}) %collective-permute-start.7) | collective-permute-done | bytes 131104 | tf_op jit(solution)/shard_map/ppermute | solution.py:31
  168.5 1.1 maximum_divide_fusion
  (43 shorter events, 2.2 us)
Async XLA Ops:
  0.0 0.7 copy-start
  6.6 4.9 %copy-start.3 = (f32[512,256]{1,0:T(8,128)S(1)}, f32[512,256]{1,0:T(8,128)}, u32[]{:S(2)}) copy-start(f32[512,256]{1,0:T(8,128)} %param.6) | copy-start | bytes 1572868
  6.6 40.8 %all-to-all-start = ((bf16[4,8,128,256]{3,2,1,0:T(8,128)(2,1)}), bf16[4,8,128,256]{3,2,1,0:T(8,128)(2,1)S(1)}, u32[]{:S(2)}, u32[]{:S(2)}) async-start(bf16[4,8,128,256]{3,2,1,0:T(8,128)(2,1)} %bitcast.6), calls=%async_computation | async-start | bytes 4194304 | tf_op jit(solution)/shard_map/all_to_all | solution.py:170
  11.6 85.8 %copy-start.2 = (bf16[512,256]{1,0:T(8,128)(2,1)}, bf16[512,256]{1,0:T(8,128)(2,1)S(1)}, u32[]{:S(2)}) copy-start(bf16[512,256]{1,0:T(8,128)(2,1)S(1)} %convert_element_type.19.t0) | copy-start | bytes 786436
  11.6 22.1 %collective-permute-start = (bf16[256,256]{1,0:T(8,128)(2,1)S(1)}, bf16[256,256]{1,0:T(8,128)(2,1)S(1)}, u32[]{:S(2)}, u32[]{:S(2)}) collective-permute-start(bf16[256,256]{1,0:T(8,128)(2,1)S(1)} %get-tuple-element.17), channel_id=1, source_target_pairs={{0,0},{1,1},{2,32},{3,33},{4,64},{5,65},{6,96},{7,97},{8,128},{9,1... | collective-permute-start | bytes 393224 | tf_op jit(solution)/shard_map/ppermute | solution.py:31
  24.8 22.5 %collective-permute-start.1 = (bf16[256,256]{1,0:T(8,128)(2,1)S(1)}, bf16[256,256]{1,0:T(8,128)(2,1)S(1)}, u32[]{:S(2)}, u32[]{:S(2)}) collective-permute-start(bf16[256,256]{1,0:T(8,128)(2,1)S(1)} %get-tuple-element.18), channel_id=1, source_target_pairs={{0,1},{1,0},{2,33},{3,32},{4,65},{5,64},{6,97},{7,96},{8,129},{9,1... | collective-permute-start | bytes 393224 | tf_op jit(solution)/shard_map/ppermute | solution.py:31
  47.4 29.9 %copy-start.4 = (bf16[256,512]{1,0:T(8,128)(2,1)}, bf16[256,512]{1,0:T(8,128)(2,1)S(1)}, u32[]{:S(2)}) copy-start(bf16[256,512]{1,0:T(8,128)(2,1)S(1)} %maximum_select_fusion.t0) | copy-start | bytes 786436
  47.4 29.9 %copy-start.1 = (bf16[4,8,128,256]{3,2,1,0:T(8,128)(2,1)}, bf16[4,8,128,256]{3,2,1,0:T(8,128)(2,1)S(1)}, u32[]{:S(2)}) copy-start(bf16[4,8,128,256]{3,2,1,0:T(8,128)(2,1)S(1)} %all-to-all-done.own_ref) | copy-start | bytes 6291460
  47.4 29.9 %collective-permute-start.5 = (bf16[4,8,128,256]{3,2,1,0:T(8,128)(2,1)S(1)}, bf16[4,8,128,256]{3,2,1,0:T(8,128)(2,1)}, u32[]{:S(2)}, u32[]{:S(2)}) collective-permute-start(bf16[4,8,128,256]{3,2,1,0:T(8,128)(2,1)S(1)} %all-to-all-done.own_ref), channel_id=1, source_target_pairs={{0,1},{1,0},{2,3},{3,2},{4,5},{5,4},{6,7},{7,6},{8,9},{9,8},{10,11... | collective-permute-start | bytes 6291464 | tf_op jit(solution)/shard_map/ppermute | solution.py:21
  49.4 10.6 %collective-permute-start.2 = (bf16[256,512]{1,0:T(8,128)(2,1)S(1)}, bf16[256,512]{1,0:T(8,128)(2,1)S(1)}, u32[]{:S(2)}, u32[]{:S(2)}) collective-permute-start(bf16[256,512]{1,0:T(8,128)(2,1)S(1)} %maximum_select_fusion.t0), channel_id=1, source_target_pairs={{0,128},{128,256},{256,384},{384,0},{1,129},{129,257},{257,385},{3... | collective-permute-start | bytes 786440 | tf_op jit(solution)/shard_map/ppermute | solution.py:17
  51.4 26.0 %collective-permute-start.3 = (bf16[256,512]{1,0:T(8,128)(2,1)S(1)}, bf16[256,512]{1,0:T(8,128)(2,1)}, u32[]{:S(2)}, u32[]{:S(2)}) collective-permute-start(bf16[256,512]{1,0:T(8,128)(2,1)S(1)} %maximum_select_fusion.t0), channel_id=1, source_target_pairs={{0,256},{128,384},{256,0},{384,128},{1,257},{129,385},{257,1},{385... | collective-permute-start | bytes 786440 | tf_op jit(solution)/shard_map/ppermute | solution.py:17
  55.6 21.7 %collective-permute-start.4 = (bf16[256,512]{1,0:T(8,128)(2,1)S(1)}, bf16[256,512]{1,0:T(8,128)(2,1)}, u32[]{:S(2)}, u32[]{:S(2)}) collective-permute-start(bf16[256,512]{1,0:T(8,128)(2,1)S(1)} %maximum_select_fusion.t0), channel_id=1, source_target_pairs={{0,384},{128,0},{256,128},{384,256},{1,385},{129,1},{257,129},{385... | collective-permute-start | bytes 786440 | tf_op jit(solution)/shard_map/ppermute | solution.py:17
  60.0 17.3 %copy-start.8 = (bf16[256,512]{1,0:T(8,128)(2,1)}, bf16[256,512]{1,0:T(8,128)(2,1)S(1)}, u32[]{:S(2)}) copy-start(bf16[256,512]{1,0:T(8,128)(2,1)S(1)} %collective-permute-done.2.t1) | copy-start | bytes 786436
  84.5 41.0 %all-to-all-start.1 = ((bf16[4,256,512]{2,1,0:T(8,128)(2,1)}), bf16[4,256,512]{2,1,0:T(8,128)(2,1)S(1)}, u32[]{:S(2)}, u32[]{:S(2)}) async-start(bf16[4,256,512]{2,1,0:T(8,128)(2,1)} %get-tuple-element.12), calls=%async_computation.1 | async-start | bytes 2097152 | tf_op jit(solution)/shard_map/all_to_all | solution.py:142
  89.7 13.0 %collective-permute-start.10 = (bf16[512,256]{1,0:T(8,128)(2,1)S(1)}, bf16[512,256]{1,0:T(8,128)(2,1)S(1)}, u32[]{:S(2)}, u32[]{:S(2)}) collective-permute-start(bf16[512,256]{1,0:T(8,128)(2,1)S(1)} %convert_element_type.19.t0), channel_id=1, source_target_pairs={{0,384},{128,0},{256,128},{384,256},{1,385},{129,1},{257,129},{385... | collective-permute-start | bytes 786440 | tf_op jit(solution)/shard_map/ppermute | solution.py:17
  91.6 14.7 %collective-permute-start.8 = (bf16[512,256]{1,0:T(8,128)(2,1)S(1)}, bf16[512,256]{1,0:T(8,128)(2,1)S(1)}, u32[]{:S(2)}, u32[]{:S(2)}) collective-permute-start(bf16[512,256]{1,0:T(8,128)(2,1)S(1)} %convert_element_type.19.t0), channel_id=1, source_target_pairs={{0,128},{128,256},{256,384},{384,0},{1,129},{129,257},{257,385},{3... | collective-permute-start | bytes 786440 | tf_op jit(solution)/shard_map/ppermute | solution.py:17
  97.3 20.2 %collective-permute-start.9 = (bf16[512,256]{1,0:T(8,128)(2,1)S(1)}, bf16[512,256]{1,0:T(8,128)(2,1)S(1)}, u32[]{:S(2)}, u32[]{:S(2)}) collective-permute-start(bf16[512,256]{1,0:T(8,128)(2,1)S(1)} %convert_element_type.19.t0), channel_id=1, source_target_pairs={{0,256},{128,384},{256,0},{384,128},{1,257},{129,385},{257,1},{385... | collective-permute-start | bytes 786440 | tf_op jit(solution)/shard_map/ppermute | solution.py:17
  102.6 14.9 %copy-start.9 = (bf16[512,256]{1,0:T(8,128)(2,1)}, bf16[512,256]{1,0:T(8,128)(2,1)S(1)}, u32[]{:S(2)}) copy-start(bf16[512,256]{1,0:T(8,128)(2,1)S(1)} %collective-permute-done.10.t3) | copy-start | bytes 786436
  106.3 11.2 %copy-start.10 = (bf16[512,256]{1,0:T(8,128)(2,1)}, bf16[512,256]{1,0:T(8,128)(2,1)S(1)}, u32[]{:S(2)}) copy-start(bf16[512,256]{1,0:T(8,128)(2,1)S(1)} %collective-permute-done.8.t1) | copy-start | bytes 786436
  117.6 0.7 copy-start.11
  125.5 5.3 %copy-start.5 = (f32[256,512]{1,0:T(8,128)S(1)}, f32[256,512]{1,0:T(8,128)}, u32[]{:S(2)}) copy-start(f32[256,512]{1,0:T(8,128)} %get-tuple-element.11) | copy-start | bytes 1572868
  125.5 21.0 %all-to-all-start.2 = ((bf16[4,512,256]{2,1,0:T(8,128)(2,1)}), bf16[4,512,256]{2,1,0:T(8,128)(2,1)S(1)}, u32[]{:S(2)}, u32[]{:S(2)}) async-start(bf16[4,512,256]{2,1,0:T(8,128)(2,1)} %get-tuple-element.14), calls=%async_computation.2 | async-start | bytes 2097152 | tf_op jit(solution)/shard_map/all_to_all | solution.py:142
  130.8 37.7 %copy-start.6 = (f32[512,256]{1,0:T(8,128)S(1)}, f32[512,256]{1,0:T(8,128)}, u32[]{:S(2)}) copy-start(f32[512,256]{1,0:T(8,128)} %param.7) | copy-start | bytes 1572868
  130.8 37.7 %copy-start.7 = (f32[512,256]{1,0:T(8,128)S(1)}, f32[512,256]{1,0:T(8,128)}, u32[]{:S(2)}) copy-start(f32[512,256]{1,0:T(8,128)} %get-tuple-element.13) | copy-start | bytes 1572868
  130.9 21.8 %collective-permute-start.6 = (bf16[256,256]{1,0:T(8,128)(2,1)S(1)}, bf16[256,256]{1,0:T(8,128)(2,1)S(1)}, u32[]{:S(2)}, u32[]{:S(2)}) collective-permute-start(bf16[256,256]{1,0:T(8,128)(2,1)S(1)} %get-tuple-element.15), channel_id=1, source_target_pairs={{0,0},{1,1},{2,32},{3,33},{4,64},{5,65},{6,96},{7,97},{8,128},{9,1... | collective-permute-start | bytes 393224 | tf_op jit(solution)/shard_map/ppermute | solution.py:31
  142.2 26.3 %collective-permute-start.7 = (bf16[256,256]{1,0:T(8,128)(2,1)S(1)}, bf16[256,256]{1,0:T(8,128)(2,1)S(1)}, u32[]{:S(2)}, u32[]{:S(2)}) collective-permute-start(bf16[256,256]{1,0:T(8,128)(2,1)S(1)} %get-tuple-element.16), channel_id=1, source_target_pairs={{0,1},{1,0},{2,33},{3,32},{4,65},{5,64},{6,97},{7,96},{8,129},{9,1... | collective-permute-start | bytes 393224 | tf_op jit(solution)/shard_map/ppermute | solution.py:31

commit v3 on v2

--- a/solution.py
+++ b/solution.py
@@ -63,11 +63,10 @@
     )(pos, co, h_blocks)
 
 
-def gathered(where, bits, tiles, h_ref, column, pair, take):
-    zl = where[0]
+def strings_and_blocks(where, bits, tiles, h_ref, column, pair, take):
     strings, blocks = [], []
     for d, tile in enumerate(tiles):
-        owner = lax.rem(zl - d + 4, 4)
+        owner = lax.rem(where[0] - d + 4, 4)
         for j in range(2):
             i = owner * 2 + j
             start = pl.multiple_of((2 * j + bits[pair, i]) * W, W)
@@ -76,31 +75,29 @@
     return strings, jnp.concatenate(blocks, axis=0)
 
 
-def direct_kernel(where, bits, t0, t1, t2, t3, own_ref, other_ref, out_ref, kept_ref):
+def direct_kernel(where, bits, t0, t1, t2, t3, h_ref, out_ref, kept_ref):
     for column in range(4):
-        for h_ref, half in ((own_ref, where[2]), (other_ref, 1 - where[2])):
-            strings, blocks = gathered(
-                where,
-                bits,
-                (t0, t1, t2, t3),
-                h_ref,
-                column,
-                column * 2 + half,
-                lambda tile, start: tile[:, pl.ds(start, W)],
-            )
-            part = jnp.dot(jnp.concatenate(strings, axis=1), blocks, preferred_element_type=jnp.float32)
-            lanes = pl.ds(pl.multiple_of(half * 2 * W, 2 * W), 2 * W)
-            out_ref[column, :, lanes] = part.astype(jnp.bfloat16)
-
-            @pl.when(where[1] == column)
-            def _():
-                kept_ref[:, lanes] = part
+        strings, blocks = strings_and_blocks(
+            where,
+            bits,
+            (t0, t1, t2, t3),
+            h_ref,
+            column,
+            column * 2 + where[2],
+            lambda tile, start: tile[:, pl.ds(start, W)],
+        )
+        part = jnp.dot(jnp.concatenate(strings, axis=1), blocks, preferred_element_type=jnp.float32)
+        out_ref[column] = part.astype(jnp.bfloat16)
+
+        @pl.when(where[1] == column)
+        def _():
+            kept_ref[...] = part
 
 
 def mirror_kernel(where, bits, t0, t1, t2, t3, own_ref, other_ref, out_ref, kept_ref):
     for column in range(4):
         for h_ref, half in ((own_ref, where[2]), (other_ref, 1 - where[2])):
-            strings, blocks = gathered(
+            strings, blocks = strings_and_blocks(
                 where,
                 bits,
                 (t0, t1, t2, t3),
@@ -123,23 +120,26 @@
                 kept_ref[rows, :] = part
 
 
-def partial_sums(kernel, name, where, bits, tiles, own, other):
-    shape = tiles[0].shape
+def partial_sums(kernel, name, shape, where, bits, tiles, *hams):
     return pl.pallas_call(
         kernel,
         out_shape=(
             jax.ShapeDtypeStruct((4, *shape), jnp.bfloat16),
             jax.ShapeDtypeStruct(shape, jnp.float32),
         ),
-        in_specs=[pl.BlockSpec(memory_space=pltpu.SMEM)] * 2 + [pl.BlockSpec(memory_space=pltpu.VMEM)] * 6,
+        in_specs=[pl.BlockSpec(memory_space=pltpu.SMEM)] * 2
+        + [pl.BlockSpec(memory_space=pltpu.VMEM)] * (4 + len(hams)),
         out_specs=(pl.BlockSpec(memory_space=pltpu.VMEM), pl.BlockSpec(memory_space=pltpu.VMEM)),
         compiler_params=PARAMS,
         name=name,
-    )(where, bits, *tiles, own, other)
-
-
-def summed(parts, kept, x):
-    got = lax.all_to_all(parts, "x", 0, 0, tiled=True)
+    )(where, bits, *tiles, *hams)
+
+
+def exchanged(parts):
+    return lax.all_to_all(parts, "x", 0, 0, tiled=True)
+
+
+def summed(got, kept, x):
     others = (jnp.arange(4) != x)[:, None, None]
     return kept + jnp.sum(jnp.where(others, got, jnp.zeros_like(got)).astype(jnp.float32), axis=0)
 
@@ -157,8 +157,9 @@
     tile = jnp.where(
         co == 0, jnp.concatenate([here, there], axis=1), jnp.concatenate([there, here], axis=1)
     )
+    mirror_tiles = [half] + [shifted(half, "zl", d) for d in (1, 2, 3)]
+    tile = lax.optimization_barrier((tile, *mirror_tiles[1:]))[0]
     direct_tiles = [tile] + [shifted(tile, "zl", d) for d in (1, 2, 3)]
-    mirror_tiles = [half] + [shifted(half, "zl", d) for d in (1, 2, 3)]
 
     filled = jnp.arange(slots, dtype=jnp.int32)[None, :] < counts[:, None]
     begin = row_id * 4 + co * 2
@@ -167,26 +168,34 @@
     owner = blk // 4
     at = (owner % 4) * 8 + (owner // 4) * 2 + (blk % 4) // 2
     packed = pack(jnp.where(live, at, -1), co[None], h_blocks)
+    packed = lax.optimization_barrier((packed, here, there, mirror_tiles[1]))[0]
     own = lax.all_to_all(packed.reshape(4, 8, W, 2 * W), "x", 0, 0, tiled=True)
-    other = swap_cores(lax.optimization_barrier((own, tile))[0])
+    other = swap_cores(lax.optimization_barrier((own, *direct_tiles[1:]))[0])
 
     names = lax.dynamic_slice_in_dim(pattern, zl * 16, 16, 0).reshape(8, 1, 2 * slots)
     i = jnp.arange(8, dtype=jnp.int32)
     odd = (8 * (i // 2) + 2 * x + i % 2) * 2 + 1
     bits = jnp.any(names == odd[None, :, None], axis=2).astype(jnp.int32)
-    where = jnp.stack([zl, x, co])
-
-    direct, kept_direct = partial_sums(direct_kernel, "direct", where, bits, direct_tiles, own, other)
-    direct = summed(direct, kept_direct, x).astype(jnp.bfloat16)
-    left, right = direct[:, :256], direct[:, 256:]
-    here = turned(jnp.where(co == 0, left, right), 0)
-    there = turned(jnp.where(co == 0, right, left), 1)
+    here_first = jnp.stack([zl, x, co])
+    there_first = jnp.stack([zl, x, 1 - co])
+
+    upper, kept_upper = partial_sums(direct_kernel, "direct", (256, 256), here_first, bits, direct_tiles, own)
+    got_upper = exchanged(upper)
+    direct_tiles[3], upper = lax.optimization_barrier((direct_tiles[3], upper))
+    lower, kept_lower = partial_sums(direct_kernel, "direct", (256, 256), there_first, bits, direct_tiles, other)
+    lower, got_upper = lax.optimization_barrier((lower, got_upper))
+    got_lower = exchanged(lower)
+    mirror_tiles[3], lower = lax.optimization_barrier((mirror_tiles[3], lower))
+    mirror, kept = partial_sums(
+        mirror_kernel, "mirror", (512, 256), here_first, bits, mirror_tiles, own, other
+    )
+    here = turned(summed(got_upper, kept_upper, x).astype(jnp.bfloat16), 0)
+    got_lower, mirror = lax.optimization_barrier((got_lower, mirror))
+    there = turned(summed(got_lower, kept_lower, x).astype(jnp.bfloat16), 1)
+    mirror_term = summed(exchanged(mirror), kept, x)
     direct_term = jnp.where(
         co == 0, jnp.concatenate([here, there], axis=0), jnp.concatenate([there, here], axis=0)
     ).astype(jnp.float32)
-
-    mirror, kept_mirror = partial_sums(mirror_kernel, "mirror", where, bits, mirror_tiles, own, other)
-    mirror_term = summed(mirror, kept_mirror, x)
 
     sigma_full = direct_term + mirror_term + diag_energy * coeffs
     shift_value = energy[0]

time: 170 us -> 167 us (0.982)
  the two profiles are of different devices: /device:TPU:102 before, /device:TPU:111 now
where the time goes in v3:
time: 167 us; the launch traced here: 166 us
  starting transfers between devices  70.5 us (42%)
  waiting for transfers between devices  64.8 us (39%)
  Pallas kernels  20.6 us (12%)
  other arithmetic  6.7 us (4%)
  local copies, waits for them, and re-layouts  2.6 us (2%)
    ppermute x4, starting transfers between devices, turned(): return lax.ppermute(value, AXES, pairs)  37 us
    ppermute x6, waiting for transfers between devices, shifted(): return lax.ppermute(value, axis, [(i, (i + step) % 4) for i in range(4)])  34.7 us
    ppermute x4, waiting for transfers between devices, turned(): return lax.ppermute(value, AXES, pairs)  27.6 us
    pallas_call x3, Pallas kernels, partial_sums(): pl.pallas_call(kernel, out_shape=(jax.ShapeDtypeStruct((4, *shape), jnp.b...  16.3 us
    all_to_all x3, starting transfers between devices, exchanged(): return lax.all_to_all(parts, 'x', 0, 0, tiled=True)  13.8 us
    ppermute x6, starting transfers between devices, shifted(): return lax.ppermute(value, axis, [(i, (i + step) % 4) for i in range(4)])  12.9 us
    pallas_call x1, Pallas kernels, pack(): pl.pallas_call(pack_kernel, out_shape=jax.ShapeDtypeStruct((32, W, 2 * W)...  4.3 us
    all_to_all x1, starting transfers between devices, on_device(): own = lax.all_to_all(packed.reshape(4, 8, W, 2 * W), 'x', 0, 0, tiled=True)  3.94 us
  transfers between devices with their start and end apart: 15, of which 7 were waited for; matrix products, arithmetic and copies ran while one was open for 3% of the time, Pallas kernels for 12%

profile of v3, /device:TPU:111, one launch (start us, length us, event | category | flops | bytes accessed | tf_op | source)
XLA Modules:
  0.0 166.2 jit_solution(3362441901015808948)
XLA Ops:
  0.0 1.1 convert_element_type.25.t0
  1.1 1.9 %collective-permute-start.2 = (bf16[512,256]{1,0:T(8,128)(2,1)S(1)}, bf16[512,256]{1,0:T(8,128)(2,1)S(1)}, u32[]{:S(2)}, u32[]{:S(2)}) collective-permute-start(bf16[512,256]{1,0:T(8,128)(2,1)S(1)} %convert_element_type.25.t0), channel_id=1, source_target_pairs={{0,128},{128,256},{256,384},{384,0},{1,129},{129,257},{257,385},{3... | collective-permute-start | bytes 786440 | tf_op jit(solution)/shard_map/ppermute | solution.py:17
  3.1 14.4 %collective-permute-start = (bf16[256,256]{1,0:T(8,128)(2,1)S(1)}, bf16[256,256]{1,0:T(8,128)(2,1)S(1)}, u32[]{:S(2)}, u32[]{:S(2)}) collective-permute-start(bf16[256,256]{1,0:T(8,128)(2,1)S(1)} %get-tuple-element.37), channel_id=1, source_target_pairs={{0,0},{1,1},{2,32},{3,33},{4,64},{5,65},{6,96},{7,97},{8,128},{9,1... | collective-permute-start | bytes 393224 | tf_op jit(solution)/shard_map/ppermute | solution.py:31
  17.5 3.1 %collective-permute-start.1 = (bf16[256,256]{1,0:T(8,128)(2,1)S(1)}, bf16[256,256]{1,0:T(8,128)(2,1)S(1)}, u32[]{:S(2)}, u32[]{:S(2)}) collective-permute-start(bf16[256,256]{1,0:T(8,128)(2,1)S(1)} %get-tuple-element.38), channel_id=1, source_target_pairs={{0,1},{1,0},{2,33},{3,32},{4,65},{5,64},{6,97},{7,96},{8,129},{9,1... | collective-permute-start | bytes 393224 | tf_op jit(solution)/shard_map/ppermute | solution.py:31
  20.8 0.7 dynamic-slice
  22.2 4.3 %pack.1 = bf16[32,128,256]{2,1,0:T(8,128)(2,1)} custom-call(s32[2,24]{1,0:T(2,128)} %compare_select_fusion.pos, s32[1]{0:T(128)} %bitcast.2.co, bf16[4,24,128,128]{3,2,1,0:T(8,128)(2,1)} %h_ref.1), custom_call_target="tpu_custom_call" | custom-call | tf_op jit(solution)/shard_map/pack/pallas_call | solution.py:52
  26.5 14.4 %collective-permute-done.1 = bf16[256,256]{1,0:T(8,128)(2,1)S(1)} collective-permute-done((bf16[256,256]{1,0:T(8,128)(2,1)S(1)}, bf16[256,256]{1,0:T(8,128)(2,1)S(1)}, u32[]{:S(2)}, u32[]{:S(2)}) %collective-permute-start.1) | collective-permute-done | bytes 131104 | tf_op jit(solution)/shard_map/ppermute | solution.py:31
  40.9 0.7 copy-done.10
  41.6 3.9 %all-to-all-start = ((bf16[4,8,128,256]{3,2,1,0:T(8,128)(2,1)}), bf16[4,8,128,256]{3,2,1,0:T(8,128)(2,1)S(1)}, u32[]{:S(2)}, u32[]{:S(2)}) async-start(bf16[4,8,128,256]{3,2,1,0:T(8,128)(2,1)} %bitcast.7), calls=%async_computation | async-start | bytes 4194304 | tf_op jit(solution)/shard_map/all_to_all | solution.py:172
  45.5 1.9 %collective-permute-start.3 = (bf16[512,256]{1,0:T(8,128)(2,1)S(1)}, bf16[512,256]{1,0:T(8,128)(2,1)S(1)}, u32[]{:S(2)}, u32[]{:S(2)}) collective-permute-start(bf16[512,256]{1,0:T(8,128)(2,1)S(1)} %convert_element_type.25.t0), channel_id=1, source_target_pairs={{0,256},{128,384},{256,0},{384,128},{1,257},{129,385},{257,1},{385... | collective-permute-start | bytes 786440 | tf_op jit(solution)/shard_map/ppermute | solution.py:17
  47.4 1.9 %collective-permute-start.4 = (bf16[512,256]{1,0:T(8,128)(2,1)S(1)}, bf16[512,256]{1,0:T(8,128)(2,1)S(1)}, u32[]{:S(2)}, u32[]{:S(2)}) collective-permute-start(bf16[512,256]{1,0:T(8,128)(2,1)S(1)} %convert_element_type.25.t0), channel_id=1, source_target_pairs={{0,384},{128,0},{256,128},{384,256},{1,385},{129,1},{257,129},{385... | collective-permute-start | bytes 786440 | tf_op jit(solution)/shard_map/ppermute | solution.py:17
  49.5 17.6 %collective-permute-done.3.t2 = bf16[512,256]{1,0:T(8,128)(2,1)S(1)} collective-permute-done((bf16[512,256]{1,0:T(8,128)(2,1)S(1)}, bf16[512,256]{1,0:T(8,128)(2,1)S(1)}, u32[]{:S(2)}, u32[]{:S(2)}) %collective-permute-start.3) | collective-permute-done | bytes 262176 | tf_op jit(solution)/shard_map/ppermute | solution.py:17
  67.1 0.7 copy-done.12
  67.9 1.9 %collective-permute-start.5 = (bf16[256,512]{1,0:T(8,128)(2,1)S(1)}, bf16[256,512]{1,0:T(8,128)(2,1)S(1)}, u32[]{:S(2)}, u32[]{:S(2)}) collective-permute-start(bf16[256,512]{1,0:T(8,128)(2,1)S(1)} %maximum_select_fusion.t0), channel_id=1, source_target_pairs={{0,128},{128,256},{256,384},{384,0},{1,129},{129,257},{257,385},{3... | collective-permute-start | bytes 786440 | tf_op jit(solution)/shard_map/ppermute | solution.py:17
  69.8 1.9 %collective-permute-start.6 = (bf16[256,512]{1,0:T(8,128)(2,1)S(1)}, bf16[256,512]{1,0:T(8,128)(2,1)S(1)}, u32[]{:S(2)}, u32[]{:S(2)}) collective-permute-start(bf16[256,512]{1,0:T(8,128)(2,1)S(1)} %maximum_select_fusion.t0), channel_id=1, source_target_pairs={{0,256},{128,384},{256,0},{384,128},{1,257},{129,385},{257,1},{385... | collective-permute-start | bytes 786440 | tf_op jit(solution)/shard_map/ppermute | solution.py:17
  71.7 3.4 %collective-permute-start.7 = (bf16[256,512]{1,0:T(8,128)(2,1)S(1)}, bf16[256,512]{1,0:T(8,128)(2,1)S(1)}, u32[]{:S(2)}, u32[]{:S(2)}) collective-permute-start(bf16[256,512]{1,0:T(8,128)(2,1)S(1)} %maximum_select_fusion.t0), channel_id=1, source_target_pairs={{0,384},{128,0},{256,128},{384,256},{1,385},{129,1},{257,129},{385... | collective-permute-start | bytes 786440 | tf_op jit(solution)/shard_map/ppermute | solution.py:17
  75.1 3.3 %collective-permute-done.5.t1 = bf16[256,512]{1,0:T(8,128)(2,1)S(1)} collective-permute-done((bf16[256,512]{1,0:T(8,128)(2,1)S(1)}, bf16[256,512]{1,0:T(8,128)(2,1)S(1)}, u32[]{:S(2)}, u32[]{:S(2)}) %collective-permute-start.5) | collective-permute-done | bytes 262176 | tf_op jit(solution)/shard_map/ppermute | solution.py:17
  78.4 13.8 %collective-permute-done.6.t2 = bf16[256,512]{1,0:T(8,128)(2,1)S(1)} collective-permute-done((bf16[256,512]{1,0:T(8,128)(2,1)S(1)}, bf16[256,512]{1,0:T(8,128)(2,1)S(1)}, u32[]{:S(2)}, u32[]{:S(2)}) %collective-permute-start.6) | collective-permute-done | bytes 262176 | tf_op jit(solution)/shard_map/ppermute | solution.py:17
  92.2 2.8 %collective-permute-start.8 = (bf16[4,8,128,256]{3,2,1,0:T(8,128)(2,1)S(1)}, bf16[4,8,128,256]{3,2,1,0:T(8,128)(2,1)}, u32[]{:S(2)}, u32[]{:S(2)}) collective-permute-start(bf16[4,8,128,256]{3,2,1,0:T(8,128)(2,1)S(1)} %all-to-all-done.h_ref.own_ref), channel_id=1, source_target_pairs={{0,1},{1,0},{2,3},{3,2},{4,5},{5,4},{6,7},{7,6},{8,9},{9,8},{10,11... | collective-permute-start | bytes 6291464 | tf_op jit(solution)/shard_map/ppermute | solution.py:21
  96.8 4.5 %direct.2 = (bf16[4,256,256]{2,1,0:T(8,128)(2,1)}, f32[256,256]{1,0:T(8,128)}) custom-call(s32[3]{0:T(128)} %pad_add_fusion.where, s32[8,8]{1,0:T(8,128)} %convert_element_type.24.bits, bf16[256,512]{1,0:T(8,128)(2,1)} %copy-done.3, bf16[256,512]{1,0:T(8,128)(2,1)} %copy-done.5, bf16[256,512]{1,0:T(8,128)(2,1)} %copy-done.6, bf16[256,512]{1,0:T(8,128)(2,1)} %copy-done.7, ...), custom_call_target="tpu_custom_call" | custom-call | tf_op jit(solution)/shard_map/direct/pallas_call | solution.py:124
  101.3 4.2 %all-to-all-start.1 = ((bf16[4,256,256]{2,1,0:T(8,128)(2,1)}), bf16[4,256,256]{2,1,0:T(8,128)(2,1)S(1)}, u32[]{:S(2)}, u32[]{:S(2)}) async-start(bf16[4,256,256]{2,1,0:T(8,128)(2,1)} %get-tuple-element.23), calls=%async_computation.1 | async-start | bytes 1048576 | tf_op jit(solution)/shard_map/all_to_all | solution.py:139
  106.2 4.5 %direct.3 = (bf16[4,256,256]{2,1,0:T(8,128)(2,1)}, f32[256,256]{1,0:T(8,128)}) custom-call(s32[3]{0:T(128)} %pad_add_fusion.2.where, s32[8,8]{1,0:T(8,128)} %convert_element_type.24.bits, bf16[256,512]{1,0:T(8,128)(2,1)} %copy-done.3, bf16[256,512]{1,0:T(8,128)(2,1)} %copy-done.5, bf16[256,512]{1,0:T(8,128)(2,1)} %copy-done.6, bf16[256,512]{1,0:T(8,128)(2,1)} %copy-done.7, ...), custom_call_target="tpu_custom_call" | custom-call | tf_op jit(solution)/shard_map/direct/pallas_call | solution.py:124
  110.7 2.4 %all-to-all-done.1 = bf16[4,256,256]{2,1,0:T(8,128)(2,1)S(1)} async-done(((bf16[4,256,256]{2,1,0:T(8,128)(2,1)}), bf16[4,256,256]{2,1,0:T(8,128)(2,1)S(1)}, u32[]{:S(2)}, u32[]{:S(2)}) %all-to-all-start.1) | async-done | bytes 524320 | tf_op jit(solution)/shard_map/all_to_all | solution.py:139
  113.1 5.2 %all-to-all-start.2 = ((bf16[4,256,256]{2,1,0:T(8,128)(2,1)}), bf16[4,256,256]{2,1,0:T(8,128)(2,1)S(1)}, u32[]{:S(2)}, u32[]{:S(2)}) async-start(bf16[4,256,256]{2,1,0:T(8,128)(2,1)} %get-tuple-element.29), calls=%async_computation.2 | async-start | bytes 1048576 | tf_op jit(solution)/shard_map/all_to_all | solution.py:139
  118.3 7.3 %mirror.1 = (bf16[4,512,256]{2,1,0:T(8,128)(2,1)}, f32[512,256]{1,0:T(8,128)}) custom-call(s32[3]{0:T(128)} %pad_add_fusion.where, s32[8,8]{1,0:T(8,128)} %convert_element_type.24.bits, bf16[512,256]{1,0:T(8,128)(2,1)} %copy-done.2, bf16[512,256]{1,0:T(8,128)(2,1)} %copy-done.10, bf16[512,256]{1,0:T(8,128)(2,1)} %copy-done.11, bf16[512,256]{1,0:T(8,128)(2,1)} %copy-done.12, ...), custom_call_target="tpu_custom_call" | custom-call | tf_op jit(solution)/shard_map/mirror/pallas_call | solution.py:124
  125.6 4.3 %all-to-all-start.3 = ((bf16[4,512,256]{2,1,0:T(8,128)(2,1)}), bf16[4,512,256]{2,1,0:T(8,128)(2,1)S(1)}, u32[]{:S(2)}, u32[]{:S(2)}) async-start(bf16[4,512,256]{2,1,0:T(8,128)(2,1)} %get-tuple-element.34), calls=%async_computation.3 | async-start | bytes 2097152 | tf_op jit(solution)/shard_map/all_to_all | solution.py:139
  131.0 1.1 add_convert_fusion.1
  132.0 2.2 %collective-permute-start.9 = (bf16[256,256]{1,0:T(8,128)(2,1)S(1)}, bf16[256,256]{1,0:T(8,128)(2,1)S(1)}, u32[]{:S(2)}, u32[]{:S(2)}) collective-permute-start(bf16[256,256]{1,0:T(8,128)(2,1)S(1)} %add_convert_fusion.1), channel_id=1, source_target_pairs={{0,0},{1,1},{2,32},{3,33},{4,64},{5,65},{6,96},{7,97},{8,128},{9,1... | collective-permute-start | bytes 393224 | tf_op jit(solution)/shard_map/ppermute | solution.py:31
  134.3 17.3 %collective-permute-start.10 = (bf16[256,256]{1,0:T(8,128)(2,1)S(1)}, bf16[256,256]{1,0:T(8,128)(2,1)S(1)}, u32[]{:S(2)}, u32[]{:S(2)}) collective-permute-start(bf16[256,256]{1,0:T(8,128)(2,1)S(1)} %add_convert_fusion), channel_id=1, source_target_pairs={{0,1},{1,0},{2,33},{3,32},{4,65},{5,64},{6,97},{7,96},{8,129},{9,1... | collective-permute-start | bytes 393224 | tf_op jit(solution)/shard_map/ppermute | solution.py:31
  151.9 5.6 %collective-permute-done.9 = bf16[256,256]{1,0:T(8,128)(2,1)S(1)} collective-permute-done((bf16[256,256]{1,0:T(8,128)(2,1)S(1)}, bf16[256,256]{1,0:T(8,128)(2,1)S(1)}, u32[]{:S(2)}, u32[]{:S(2)}) %collective-permute-start.9) | collective-permute-done | bytes 131104 | tf_op jit(solution)/shard_map/ppermute | solution.py:31
  157.5 7.6 %collective-permute-done.10 = bf16[256,256]{1,0:T(8,128)(2,1)S(1)} collective-permute-done((bf16[256,256]{1,0:T(8,128)(2,1)S(1)}, bf16[256,256]{1,0:T(8,128)(2,1)S(1)}, u32[]{:S(2)}, u32[]{:S(2)}) %collective-permute-start.10) | collective-permute-done | bytes 131104 | tf_op jit(solution)/shard_map/ppermute | solution.py:31
  165.1 1.1 maximum_divide_fusion
  (51 shorter events, 4.0 us)
Async XLA Ops:
  0.0 20.6 %copy-start = (s32[64,24]{0,1:T(8,128)S(1)}, s32[64,24]{0,1:T(8,128)}, u32[]{:S(2)}) copy-start(s32[64,24]{0,1:T(8,128)} %param.10) | copy-start | bytes 18436
  1.1 46.3 %copy-start.2 = (bf16[512,256]{1,0:T(8,128)(2,1)}, bf16[512,256]{1,0:T(8,128)(2,1)S(1)}, u32[]{:S(2)}) copy-start(bf16[512,256]{1,0:T(8,128)(2,1)S(1)} %convert_element_type.25.t0) | copy-start | bytes 786436
  1.1 39.8 %collective-permute-start.2 = (bf16[512,256]{1,0:T(8,128)(2,1)S(1)}, bf16[512,256]{1,0:T(8,128)(2,1)S(1)}, u32[]{:S(2)}, u32[]{:S(2)}) collective-permute-start(bf16[512,256]{1,0:T(8,128)(2,1)S(1)} %convert_element_type.25.t0), channel_id=1, source_target_pairs={{0,128},{128,256},{256,384},{384,0},{1,129},{129,257},{257,385},{3... | collective-permute-start | bytes 786440 | tf_op jit(solution)/shard_map/ppermute | solution.py:17
  3.1 23.4 %collective-permute-start = (bf16[256,256]{1,0:T(8,128)(2,1)S(1)}, bf16[256,256]{1,0:T(8,128)(2,1)S(1)}, u32[]{:S(2)}, u32[]{:S(2)}) collective-permute-start(bf16[256,256]{1,0:T(8,128)(2,1)S(1)} %get-tuple-element.37), channel_id=1, source_target_pairs={{0,0},{1,1},{2,32},{3,33},{4,64},{5,65},{6,96},{7,97},{8,128},{9,1... | collective-permute-start | bytes 393224 | tf_op jit(solution)/shard_map/ppermute | solution.py:31
  17.5 23.4 %collective-permute-start.1 = (bf16[256,256]{1,0:T(8,128)(2,1)S(1)}, bf16[256,256]{1,0:T(8,128)(2,1)S(1)}, u32[]{:S(2)}, u32[]{:S(2)}) collective-permute-start(bf16[256,256]{1,0:T(8,128)(2,1)S(1)} %get-tuple-element.38), channel_id=1, source_target_pairs={{0,1},{1,0},{2,33},{3,32},{4,65},{5,64},{6,97},{7,96},{8,129},{9,1... | collective-permute-start | bytes 393224 | tf_op jit(solution)/shard_map/ppermute | solution.py:31
  40.9 0.7 copy-start.10
  41.6 50.6 %all-to-all-start = ((bf16[4,8,128,256]{3,2,1,0:T(8,128)(2,1)}), bf16[4,8,128,256]{3,2,1,0:T(8,128)(2,1)S(1)}, u32[]{:S(2)}, u32[]{:S(2)}) async-start(bf16[4,8,128,256]{3,2,1,0:T(8,128)(2,1)} %bitcast.7), calls=%async_computation | async-start | bytes 4194304 | tf_op jit(solution)/shard_map/all_to_all | solution.py:172
  45.5 21.6 %collective-permute-start.3 = (bf16[512,256]{1,0:T(8,128)(2,1)S(1)}, bf16[512,256]{1,0:T(8,128)(2,1)S(1)}, u32[]{:S(2)}, u32[]{:S(2)}) collective-permute-start(bf16[512,256]{1,0:T(8,128)(2,1)S(1)} %convert_element_type.25.t0), channel_id=1, source_target_pairs={{0,256},{128,384},{256,0},{384,128},{1,257},{129,385},{257,1},{385... | collective-permute-start | bytes 786440 | tf_op jit(solution)/shard_map/ppermute | solution.py:17
  47.4 19.7 %collective-permute-start.4 = (bf16[512,256]{1,0:T(8,128)(2,1)S(1)}, bf16[512,256]{1,0:T(8,128)(2,1)S(1)}, u32[]{:S(2)}, u32[]{:S(2)}) collective-permute-start(bf16[512,256]{1,0:T(8,128)(2,1)S(1)} %convert_element_type.25.t0), channel_id=1, source_target_pairs={{0,384},{128,0},{256,128},{384,256},{1,385},{129,1},{257,129},{385... | collective-permute-start | bytes 786440 | tf_op jit(solution)/shard_map/ppermute | solution.py:17
  49.5 47.3 %copy-start.3 = (bf16[256,512]{1,0:T(8,128)(2,1)}, bf16[256,512]{1,0:T(8,128)(2,1)S(1)}, u32[]{:S(2)}) copy-start(bf16[256,512]{1,0:T(8,128)(2,1)S(1)} %maximum_select_fusion.t0) | copy-start | bytes 786436
  67.1 51.2 %copy-start.11 = (bf16[512,256]{1,0:T(8,128)(2,1)}, bf16[512,256]{1,0:T(8,128)(2,1)S(1)}, u32[]{:S(2)}) copy-start(bf16[512,256]{1,0:T(8,128)(2,1)S(1)} %collective-permute-done.3.t2) | copy-start | bytes 786436
  67.1 0.7 copy-start.12
  67.9 10.5 %collective-permute-start.5 = (bf16[256,512]{1,0:T(8,128)(2,1)S(1)}, bf16[256,512]{1,0:T(8,128)(2,1)S(1)}, u32[]{:S(2)}, u32[]{:S(2)}) collective-permute-start(bf16[256,512]{1,0:T(8,128)(2,1)S(1)} %maximum_select_fusion.t0), channel_id=1, source_target_pairs={{0,128},{128,256},{256,384},{384,0},{1,129},{129,257},{257,385},{3... | collective-permute-start | bytes 786440 | tf_op jit(solution)/shard_map/ppermute | solution.py:17
  69.8 22.4 %collective-permute-start.6 = (bf16[256,512]{1,0:T(8,128)(2,1)S(1)}, bf16[256,512]{1,0:T(8,128)(2,1)S(1)}, u32[]{:S(2)}, u32[]{:S(2)}) collective-permute-start(bf16[256,512]{1,0:T(8,128)(2,1)S(1)} %maximum_select_fusion.t0), channel_id=1, source_target_pairs={{0,256},{128,384},{256,0},{384,128},{1,257},{129,385},{257,1},{385... | collective-permute-start | bytes 786440 | tf_op jit(solution)/shard_map/ppermute | solution.py:17
  71.7 20.5 %collective-permute-start.7 = (bf16[256,512]{1,0:T(8,128)(2,1)S(1)}, bf16[256,512]{1,0:T(8,128)(2,1)S(1)}, u32[]{:S(2)}, u32[]{:S(2)}) collective-permute-start(bf16[256,512]{1,0:T(8,128)(2,1)S(1)} %maximum_select_fusion.t0), channel_id=1, source_target_pairs={{0,384},{128,0},{256,128},{384,256},{1,385},{129,1},{257,129},{385... | collective-permute-start | bytes 786440 | tf_op jit(solution)/shard_map/ppermute | solution.py:17
  78.4 18.4 %copy-start.5 = (bf16[256,512]{1,0:T(8,128)(2,1)}, bf16[256,512]{1,0:T(8,128)(2,1)S(1)}, u32[]{:S(2)}) copy-start(bf16[256,512]{1,0:T(8,128)(2,1)S(1)} %collective-permute-done.5.t1) | copy-start | bytes 786436
  92.2 4.6 %copy-start.6 = (bf16[256,512]{1,0:T(8,128)(2,1)}, bf16[256,512]{1,0:T(8,128)(2,1)S(1)}, u32[]{:S(2)}) copy-start(bf16[256,512]{1,0:T(8,128)(2,1)S(1)} %collective-permute-done.6.t2) | copy-start | bytes 786436
  92.2 4.6 %copy-start.7 = (bf16[256,512]{1,0:T(8,128)(2,1)}, bf16[256,512]{1,0:T(8,128)(2,1)S(1)}, u32[]{:S(2)}) copy-start(bf16[256,512]{1,0:T(8,128)(2,1)S(1)} %collective-permute-done.7.t3) | copy-start | bytes 786436
  92.2 4.6 %copy-start.1 = (bf16[4,8,128,256]{3,2,1,0:T(8,128)(2,1)}, bf16[4,8,128,256]{3,2,1,0:T(8,128)(2,1)S(1)}, u32[]{:S(2)}) copy-start(bf16[4,8,128,256]{3,2,1,0:T(8,128)(2,1)S(1)} %all-to-all-done.h_ref.own_ref) | copy-start | bytes 6291460
  92.2 14.0 %collective-permute-start.8 = (bf16[4,8,128,256]{3,2,1,0:T(8,128)(2,1)S(1)}, bf16[4,8,128,256]{3,2,1,0:T(8,128)(2,1)}, u32[]{:S(2)}, u32[]{:S(2)}) collective-permute-start(bf16[4,8,128,256]{3,2,1,0:T(8,128)(2,1)S(1)} %all-to-all-done.h_ref.own_ref), channel_id=1, source_target_pairs={{0,1},{1,0},{2,3},{3,2},{4,5},{5,4},{6,7},{7,6},{8,9},{9,8},{10,11... | collective-permute-start | bytes 6291464 | tf_op jit(solution)/shard_map/ppermute | solution.py:21
  101.3 11.8 %all-to-all-start.1 = ((bf16[4,256,256]{2,1,0:T(8,128)(2,1)}), bf16[4,256,256]{2,1,0:T(8,128)(2,1)S(1)}, u32[]{:S(2)}, u32[]{:S(2)}) async-start(bf16[4,256,256]{2,1,0:T(8,128)(2,1)} %get-tuple-element.23), calls=%async_computation.1 | async-start | bytes 1048576 | tf_op jit(solution)/shard_map/all_to_all | solution.py:139
  113.1 12.5 %all-to-all-start.2 = ((bf16[4,256,256]{2,1,0:T(8,128)(2,1)}), bf16[4,256,256]{2,1,0:T(8,128)(2,1)S(1)}, u32[]{:S(2)}, u32[]{:S(2)}) async-start(bf16[4,256,256]{2,1,0:T(8,128)(2,1)} %get-tuple-element.29), calls=%async_computation.2 | async-start | bytes 1048576 | tf_op jit(solution)/shard_map/all_to_all | solution.py:139
  125.6 26.0 %all-to-all-start.3 = ((bf16[4,512,256]{2,1,0:T(8,128)(2,1)}), bf16[4,512,256]{2,1,0:T(8,128)(2,1)S(1)}, u32[]{:S(2)}, u32[]{:S(2)}) async-start(bf16[4,512,256]{2,1,0:T(8,128)(2,1)} %get-tuple-element.34), calls=%async_computation.3 | async-start | bytes 2097152 | tf_op jit(solution)/shard_map/all_to_all | solution.py:139
  130.0 4.3 %copy-start.13 = (f32[256,256]{1,0:T(8,128)S(1)}, f32[256,256]{1,0:T(8,128)}, u32[]{:S(2)}) copy-start(f32[256,256]{1,0:T(8,128)} %get-tuple-element.28) | copy-start | bytes 786436
  130.7 34.4 %copy-start.4 = (f32[512,256]{1,0:T(8,128)S(1)}, f32[512,256]{1,0:T(8,128)}, u32[]{:S(2)}) copy-start(f32[512,256]{1,0:T(8,128)} %param.6) | copy-start | bytes 1572868
  130.7 34.4 %copy-start.8 = (f32[512,256]{1,0:T(8,128)S(1)}, f32[512,256]{1,0:T(8,128)}, u32[]{:S(2)}) copy-start(f32[512,256]{1,0:T(8,128)} %param.7) | copy-start | bytes 1572868
  131.0 34.1 %copy-start.9 = (f32[512,256]{1,0:T(8,128)S(1)}, f32[512,256]{1,0:T(8,128)}, u32[]{:S(2)}) copy-start(f32[512,256]{1,0:T(8,128)} %get-tuple-element.33) | copy-start | bytes 1572868
  132.0 25.5 %collective-permute-start.9 = (bf16[256,256]{1,0:T(8,128)(2,1)S(1)}, bf16[256,256]{1,0:T(8,128)(2,1)S(1)}, u32[]{:S(2)}, u32[]{:S(2)}) collective-permute-start(bf16[256,256]{1,0:T(8,128)(2,1)S(1)} %add_convert_fusion.1), channel_id=1, source_target_pairs={{0,0},{1,1},{2,32},{3,33},{4,64},{5,65},{6,96},{7,97},{8,128},{9,1... | collective-permute-start | bytes 393224 | tf_op jit(solution)/shard_map/ppermute | solution.py:31
  134.3 30.8 %collective-permute-start.10 = (bf16[256,256]{1,0:T(8,128)(2,1)S(1)}, bf16[256,256]{1,0:T(8,128)(2,1)S(1)}, u32[]{:S(2)}, u32[]{:S(2)}) collective-permute-start(bf16[256,256]{1,0:T(8,128)(2,1)S(1)} %add_convert_fusion), channel_id=1, source_target_pairs={{0,1},{1,0},{2,33},{3,32},{4,65},{5,64},{6,97},{7,96},{8,129},{9,1... | collective-permute-start | bytes 393224 | tf_op jit(solution)/shard_map/ppermute | solution.py:31

commit v4 on v3

--- a/solution.py
+++ b/solution.py
@@ -63,28 +63,24 @@
     )(pos, co, h_blocks)
 
 
-def strings_and_blocks(where, bits, tiles, h_ref, column, pair, take):
+def strings_and_blocks(bits, halves, h_ref, column, pair, take):
     strings, blocks = [], []
-    for d, tile in enumerate(tiles):
-        owner = lax.rem(where[0] - d + 4, 4)
-        for j in range(2):
-            i = owner * 2 + j
-            start = pl.multiple_of((2 * j + bits[pair, i]) * W, W)
-            strings.append(take(tile, start))
-            blocks.append(h_ref[column, i])
+    for i in range(8):
+        start = pl.multiple_of(bits[pair, i] * W, W)
+        strings.append(take(halves[i % 2], i // 2, start))
+        blocks.append(h_ref[column, i])
     return strings, jnp.concatenate(blocks, axis=0)
 
 
-def direct_kernel(where, bits, t0, t1, t2, t3, h_ref, out_ref, kept_ref):
+def direct_kernel(where, bits, low, high, h_ref, out_ref, kept_ref):
     for column in range(4):
         strings, blocks = strings_and_blocks(
-            where,
             bits,
-            (t0, t1, t2, t3),
+            (low, high),
             h_ref,
             column,
             column * 2 + where[2],
-            lambda tile, start: tile[:, pl.ds(start, W)],
+            lambda ref, t, start: ref[t, :, pl.ds(start, W)],
         )
         part = jnp.dot(jnp.concatenate(strings, axis=1), blocks, preferred_element_type=jnp.float32)
         out_ref[column] = part.astype(jnp.bfloat16)
@@ -94,17 +90,16 @@
             kept_ref[...] = part
 
 
-def mirror_kernel(where, bits, t0, t1, t2, t3, own_ref, other_ref, out_ref, kept_ref):
+def mirror_kernel(where, bits, low, high, own_ref, other_ref, out_ref, kept_ref):
     for column in range(4):
         for h_ref, half in ((own_ref, where[2]), (other_ref, 1 - where[2])):
             strings, blocks = strings_and_blocks(
-                where,
                 bits,
-                (t0, t1, t2, t3),
+                (low, high),
                 h_ref,
                 column,
                 column * 2 + half,
-                lambda tile, start: tile[pl.ds(start, W), :],
+                lambda ref, t, start: ref[t, pl.ds(start, W), :],
             )
             part = lax.dot_general(
                 blocks,
@@ -128,7 +123,7 @@
             jax.ShapeDtypeStruct(shape, jnp.float32),
         ),
         in_specs=[pl.BlockSpec(memory_space=pltpu.SMEM)] * 2
-        + [pl.BlockSpec(memory_space=pltpu.VMEM)] * (4 + len(hams)),
+        + [pl.BlockSpec(memory_space=pltpu.VMEM)] * (2 + len(hams)),
         out_specs=(pl.BlockSpec(memory_space=pltpu.VMEM), pl.BlockSpec(memory_space=pltpu.VMEM)),
         compiler_params=PARAMS,
         name=name,
@@ -154,12 +149,10 @@
     first, last = half[:256], half[256:]
     here = turned(jnp.where(co == 0, first, last), 0)
     there = turned(jnp.where(co == 0, last, first), 1)
-    tile = jnp.where(
-        co == 0, jnp.concatenate([here, there], axis=1), jnp.concatenate([there, here], axis=1)
-    )
-    mirror_tiles = [half] + [shifted(half, "zl", d) for d in (1, 2, 3)]
-    tile = lax.optimization_barrier((tile, *mirror_tiles[1:]))[0]
-    direct_tiles = [tile] + [shifted(tile, "zl", d) for d in (1, 2, 3)]
+    mirror_halves = [lax.all_gather(part, "zl") for part in (first, last)]
+    here, there, *mirror_halves = lax.optimization_barrier((here, there, *mirror_halves))
+    tile = (jnp.where(co == 0, here, there), jnp.where(co == 0, there, here))
+    direct_halves = [lax.all_gather(part, "zl") for part in tile]
 
     filled = jnp.arange(slots, dtype=jnp.int32)[None, :] < counts[:, None]
     begin = row_id * 4 + co * 2
@@ -168,9 +161,9 @@
     owner = blk // 4
     at = (owner % 4) * 8 + (owner // 4) * 2 + (blk % 4) // 2
     packed = pack(jnp.where(live, at, -1), co[None], h_blocks)
-    packed = lax.optimization_barrier((packed, here, there, mirror_tiles[1]))[0]
+    packed = lax.optimization_barrier((packed, *tile))[0]
     own = lax.all_to_all(packed.reshape(4, 8, W, 2 * W), "x", 0, 0, tiled=True)
-    other = swap_cores(lax.optimization_barrier((own, *direct_tiles[1:]))[0])
+    other = swap_cores(lax.optimization_barrier((own, direct_halves[0]))[0])
 
     names = lax.dynamic_slice_in_dim(pattern, zl * 16, 16, 0).reshape(8, 1, 2 * slots)
     i = jnp.arange(8, dtype=jnp.int32)
@@ -179,15 +172,15 @@
     here_first = jnp.stack([zl, x, co])
     there_first = jnp.stack([zl, x, 1 - co])
 
-    upper, kept_upper = partial_sums(direct_kernel, "direct", (256, 256), here_first, bits, direct_tiles, own)
+    upper, kept_upper = partial_sums(direct_kernel, "direct", (256, 256), here_first, bits, direct_halves, own)
     got_upper = exchanged(upper)
-    direct_tiles[3], upper = lax.optimization_barrier((direct_tiles[3], upper))
-    lower, kept_lower = partial_sums(direct_kernel, "direct", (256, 256), there_first, bits, direct_tiles, other)
+    direct_halves[1], upper = lax.optimization_barrier((direct_halves[1], upper))
+    lower, kept_lower = partial_sums(direct_kernel, "direct", (256, 256), there_first, bits, direct_halves, other)
     lower, got_upper = lax.optimization_barrier((lower, got_upper))
     got_lower = exchanged(lower)
-    mirror_tiles[3], lower = lax.optimization_barrier((mirror_tiles[3], lower))
+    mirror_halves[1], lower = lax.optimization_barrier((mirror_halves[1], lower))
     mirror, kept = partial_sums(
-        mirror_kernel, "mirror", (512, 256), here_first, bits, mirror_tiles, own, other
+        mirror_kernel, "mirror", (512, 256), here_first, bits, mirror_halves, own, other
     )
     here = turned(summed(got_upper, kept_upper, x).astype(jnp.bfloat16), 0)
     got_lower, mirror = lax.optimization_barrier((got_lower, mirror))

time: 167 us -> 177 us (1.060)
  the two profiles are of different devices: /device:TPU:111 before, /device:TPU:110 now
where the time goes in v4:
time: 177 us
  blocking collectives  72 us (41%)
  starting transfers between devices  53.4 us (30%)
  waiting for transfers between devices  23 us (13%)
  Pallas kernels  20.7 us (12%)
  other arithmetic  5.64 us (3%)
    all_gather x2, blocking collectives, on_device(): mirror_halves = [lax.all_gather(part, 'zl') for part in (first, last)]  38.6 us
    all_gather x2, blocking collectives, on_device(): direct_halves = [lax.all_gather(part, 'zl') for part in tile]  33.4 us
    ppermute x4, starting transfers between devices, turned(): return lax.ppermute(value, AXES, pairs)  31.1 us
    ppermute x4, waiting for transfers between devices, turned(): return lax.ppermute(value, AXES, pairs)  18.1 us
    pallas_call x3, Pallas kernels, partial_sums(): pl.pallas_call(kernel, out_shape=(jax.ShapeDtypeStruct((4, *shape), jnp.b...  16.3 us
    all_to_all x3, starting transfers between devices, exchanged(): return lax.all_to_all(parts, 'x', 0, 0, tiled=True)  15.9 us
    all_to_all x1, starting transfers between devices, on_device(): own = lax.all_to_all(packed.reshape(4, 8, W, 2 * W), 'x', 0, 0, tiled=True)  4.52 us
    pallas_call x1, Pallas kernels, pack(): pl.pallas_call(pack_kernel, out_shape=jax.ShapeDtypeStruct((32, W, 2 * W)...  4.4 us
  transfers between devices with their start and end apart: 9, of which 4 were waited for; matrix products, arithmetic and copies ran while one was open for 3% of the time, Pallas kernels for 12%

profile of v4, /device:TPU:110, one launch (start us, length us, event | category | flops | bytes accessed | tf_op | source)
XLA Modules:
  0.0 176.8 jit_solution(7163193932634679863)
XLA Ops:
  0.0 1.1 convert_element_type.25
  1.1 13.9 %collective-permute-start = (bf16[256,256]{1,0:T(8,128)(2,1)S(1)}, bf16[256,256]{1,0:T(8,128)(2,1)S(1)}, u32[]{:S(2)}, u32[]{:S(2)}) collective-permute-start(bf16[256,256]{1,0:T(8,128)(2,1)S(1)} %get-tuple-element.46), channel_id=1, source_target_pairs={{0,0},{1,1},{2,32},{3,33},{4,64},{5,65},{6,96},{7,97},{8,128},{9,1... | collective-permute-start | bytes 393224 | tf_op jit(solution)/shard_map/ppermute | solution.py:31
  15.1 2.5 %collective-permute-start.1 = (bf16[256,256]{1,0:T(8,128)(2,1)S(1)}, bf16[256,256]{1,0:T(8,128)(2,1)S(1)}, u32[]{:S(2)}, u32[]{:S(2)}) collective-permute-start(bf16[256,256]{1,0:T(8,128)(2,1)S(1)} %get-tuple-element.47), channel_id=1, source_target_pairs={{0,1},{1,0},{2,33},{3,32},{4,65},{5,64},{6,97},{7,96},{8,129},{9,1... | collective-permute-start | bytes 393224 | tf_op jit(solution)/shard_map/ppermute | solution.py:31
  17.7 0.1 copy.12
  17.7 0.7 dynamic-slice
  18.5 21.8 %all-gather = bf16[1024,256]{1,0:T(8,128)(2,1)} all-gather(bf16[256,256]{1,0:T(8,128)(2,1)S(1)} %get-tuple-element.48), channel_id=2, replica_groups=mesh['zl'=4,'x'=4,'zh'=4,'y'=4,'co'=2] {'zl'}, dimensions={0}, use_global_device_ids=true | all-gather | bytes 655360 | tf_op jit(solution)/shard_map/all_gather | solution.py:152
  40.3 0.6 compare_select_fusion.pos
  40.9 4.4 %pack.1 = bf16[32,128,256]{2,1,0:T(8,128)(2,1)} custom-call(s32[2,24]{1,0:T(2,128)} %compare_select_fusion.pos, s32[1]{0:T(128)} %bitcast.2.co, bf16[4,24,128,128]{3,2,1,0:T(8,128)(2,1)} %h_ref.1), custom_call_target="tpu_custom_call" | custom-call | tf_op jit(solution)/shard_map/pack/pallas_call | solution.py:52
  45.3 16.8 %all-gather.1 = bf16[1024,256]{1,0:T(8,128)(2,1)} all-gather(bf16[256,256]{1,0:T(8,128)(2,1)S(1)} %get-tuple-element.45), channel_id=3, replica_groups=mesh['zl'=4,'x'=4,'zh'=4,'y'=4,'co'=2] {'zl'}, dimensions={0}, use_global_device_ids=true | all-gather | bytes 655360 | tf_op jit(solution)/shard_map/all_gather | solution.py:152
  62.2 4.5 %all-to-all-start = ((bf16[4,8,128,256]{3,2,1,0:T(8,128)(2,1)}), bf16[4,8,128,256]{3,2,1,0:T(8,128)(2,1)S(1)}, u32[]{:S(2)}, u32[]{:S(2)}) async-start(bf16[4,8,128,256]{3,2,1,0:T(8,128)(2,1)} %bitcast.11), calls=%async_computation | async-start | bytes 4194304 | tf_op jit(solution)/shard_map/all_to_all | solution.py:165
  66.7 16.6 %all-gather.2 = bf16[1024,256]{1,0:T(8,128)(2,1)} all-gather(bf16[256,256]{1,0:T(8,128)(2,1)S(1)} %get-tuple-element.44), channel_id=4, replica_groups=mesh['zl'=4,'x'=4,'zh'=4,'y'=4,'co'=2] {'zl'}, dimensions={0}, use_global_device_ids=true | all-gather | bytes 655360 | tf_op jit(solution)/shard_map/all_gather | solution.py:155
  83.3 3.5 %all-to-all-done.h_ref.own_ref = bf16[4,8,128,256]{3,2,1,0:T(8,128)(2,1)S(1)} async-done(((bf16[4,8,128,256]{3,2,1,0:T(8,128)(2,1)}), bf16[4,8,128,256]{3,2,1,0:T(8,128)(2,1)S(1)}, u32[]{:S(2)}, u32[]{:S(2)}) %all-to-all-start) | async-done | bytes 2097184 | tf_op jit(solution)/shard_map/all_to_all | solution.py:165
  86.8 1.9 %collective-permute-start.2 = (bf16[4,8,128,256]{3,2,1,0:T(8,128)(2,1)S(1)}, bf16[4,8,128,256]{3,2,1,0:T(8,128)(2,1)}, u32[]{:S(2)}, u32[]{:S(2)}) collective-permute-start(bf16[4,8,128,256]{3,2,1,0:T(8,128)(2,1)S(1)} %all-to-all-done.h_ref.own_ref), channel_id=1, source_target_pairs={{0,1},{1,0},{2,3},{3,2},{4,5},{5,4},{6,7},{7,6},{8,9},{9,8},{10,11... | collective-permute-start | bytes 6291464 | tf_op jit(solution)/shard_map/ppermute | solution.py:21
  88.9 0.3 compare_reduce_fusion
  89.2 0.6 convert_element_type.24.bits
  89.8 0.6 pad_add_fusion.where
  90.4 16.8 %all-gather.3 = bf16[1024,256]{1,0:T(8,128)(2,1)} all-gather(bf16[256,256]{1,0:T(8,128)(2,1)S(1)} %get-tuple-element.43), channel_id=5, replica_groups=mesh['zl'=4,'x'=4,'zh'=4,'y'=4,'co'=2] {'zl'}, dimensions={0}, use_global_device_ids=true | all-gather | bytes 655360 | tf_op jit(solution)/shard_map/all_gather | solution.py:155
  107.2 4.5 %direct.2 = (bf16[4,256,256]{2,1,0:T(8,128)(2,1)}, f32[256,256]{1,0:T(8,128)}) custom-call(s32[3]{0:T(128)} %pad_add_fusion.where, s32[8,8]{1,0:T(8,128)} %convert_element_type.24.bits, bf16[4,256,256]{2,1,0:T(8,128)(2,1)} %bitcast.12, bf16[4,256,256]{2,1,0:T(8,128)(2,1)} %bitcast.14, bf16[4,8,128,256]{3,2,1,0:T(8,128)(2,1)} %copy-done.1), custom_call_target="tpu_custom_call" | custom-call | tf_op jit(solution)/shard_map/direct/pallas_call | solution.py:119
  111.8 5.5 %all-to-all-start.1 = ((bf16[4,256,256]{2,1,0:T(8,128)(2,1)}), bf16[4,256,256]{2,1,0:T(8,128)(2,1)S(1)}, u32[]{:S(2)}, u32[]{:S(2)}) async-start(bf16[4,256,256]{2,1,0:T(8,128)(2,1)} %get-tuple-element.27), calls=%async_computation.1 | async-start | bytes 1048576 | tf_op jit(solution)/shard_map/all_to_all | solution.py:134
  117.3 0.6 pad_add_fusion.2.where
  117.9 4.5 %direct.3 = (bf16[4,256,256]{2,1,0:T(8,128)(2,1)}, f32[256,256]{1,0:T(8,128)}) custom-call(s32[3]{0:T(128)} %pad_add_fusion.2.where, s32[8,8]{1,0:T(8,128)} %convert_element_type.24.bits, bf16[4,256,256]{2,1,0:T(8,128)(2,1)} %bitcast.13, bf16[4,256,256]{2,1,0:T(8,128)(2,1)} %bitcast.15, bf16[4,8,128,256]{3,2,1,0:T(8,128)(2,1)} %collective-permute-done.2.h_ref.other_ref), custom_call_target="tpu_custom_call" | custom-call | tf_op jit(solution)/shard_map/direct/pallas_call | solution.py:119
  122.4 1.4 all-to-all-done.1
  123.8 5.5 %all-to-all-start.2 = ((bf16[4,256,256]{2,1,0:T(8,128)(2,1)}), bf16[4,256,256]{2,1,0:T(8,128)(2,1)S(1)}, u32[]{:S(2)}, u32[]{:S(2)}) async-start(bf16[4,256,256]{2,1,0:T(8,128)(2,1)} %get-tuple-element.33), calls=%async_computation.2 | async-start | bytes 1048576 | tf_op jit(solution)/shard_map/all_to_all | solution.py:134
  129.3 7.2 %mirror.1 = (bf16[4,512,256]{2,1,0:T(8,128)(2,1)}, f32[512,256]{1,0:T(8,128)}) custom-call(s32[3]{0:T(128)} %pad_add_fusion.where, s32[8,8]{1,0:T(8,128)} %convert_element_type.24.bits, bf16[4,256,256]{2,1,0:T(8,128)(2,1)} %bitcast.16, bf16[4,256,256]{2,1,0:T(8,128)(2,1)} %bitcast.17, bf16[4,8,128,256]{3,2,1,0:T(8,128)(2,1)} %copy-done.1, ...), custom_call_target="tpu_custom_call" | custom-call | tf_op jit(solution)/shard_map/mirror/pallas_call | solution.py:119
  136.5 4.9 %all-to-all-start.3 = ((bf16[4,512,256]{2,1,0:T(8,128)(2,1)}), bf16[4,512,256]{2,1,0:T(8,128)(2,1)S(1)}, u32[]{:S(2)}, u32[]{:S(2)}) async-start(bf16[4,512,256]{2,1,0:T(8,128)(2,1)} %get-tuple-element.40), calls=%async_computation.3 | async-start | bytes 2097152 | tf_op jit(solution)/shard_map/all_to_all | solution.py:134
  142.2 0.3 convert_reduce_fusion.2
  142.5 12.8 %collective-permute-start.3 = (bf16[256,256]{1,0:T(8,128)(2,1)S(1)}, bf16[256,256]{1,0:T(8,128)(2,1)S(1)}, u32[]{:S(2)}, u32[]{:S(2)}) collective-permute-start(bf16[256,256]{1,0:T(8,128)(2,1)S(1)} %add_convert_fusion.1), channel_id=1, source_target_pairs={{0,0},{1,1},{2,32},{3,33},{4,64},{5,65},{6,96},{7,97},{8,128},{9,1... | collective-permute-start | bytes 393224 | tf_op jit(solution)/shard_map/ppermute | solution.py:31
  155.4 1.9 %collective-permute-start.4 = (bf16[256,256]{1,0:T(8,128)(2,1)S(1)}, bf16[256,256]{1,0:T(8,128)(2,1)S(1)}, u32[]{:S(2)}, u32[]{:S(2)}) collective-permute-start(bf16[256,256]{1,0:T(8,128)(2,1)S(1)} %add_convert_fusion), channel_id=1, source_target_pairs={{0,1},{1,0},{2,33},{3,32},{4,65},{5,64},{6,97},{7,96},{8,129},{9,1... | collective-permute-start | bytes 393224 | tf_op jit(solution)/shard_map/ppermute | solution.py:31
  157.3 0.3 convert_reduce_fusion
  157.6 4.7 %collective-permute-done.3 = bf16[256,256]{1,0:T(8,128)(2,1)S(1)} collective-permute-done((bf16[256,256]{1,0:T(8,128)(2,1)S(1)}, bf16[256,256]{1,0:T(8,128)(2,1)S(1)}, u32[]{:S(2)}, u32[]{:S(2)}) %collective-permute-start.3) | collective-permute-done | bytes 131104 | tf_op jit(solution)/shard_map/ppermute | solution.py:31
  162.3 13.4 %collective-permute-done.4 = bf16[256,256]{1,0:T(8,128)(2,1)S(1)} collective-permute-done((bf16[256,256]{1,0:T(8,128)(2,1)S(1)}, bf16[256,256]{1,0:T(8,128)(2,1)S(1)}, u32[]{:S(2)}, u32[]{:S(2)}) %collective-permute-start.4) | collective-permute-done | bytes 131104 | tf_op jit(solution)/shard_map/ppermute | solution.py:31
  175.7 1.1 maximum_divide_fusion
  (29 shorter events, 0.5 us)
Async XLA Ops:
  0.0 17.6 %copy-start = (s32[64,24]{0,1:T(8,128)S(1)}, s32[64,24]{0,1:T(8,128)}, u32[]{:S(2)}) copy-start(s32[64,24]{0,1:T(8,128)} %param.10) | copy-start | bytes 18436
  1.1 61.0 %collective-permute-start = (bf16[256,256]{1,0:T(8,128)(2,1)S(1)}, bf16[256,256]{1,0:T(8,128)(2,1)S(1)}, u32[]{:S(2)}, u32[]{:S(2)}) collective-permute-start(bf16[256,256]{1,0:T(8,128)(2,1)S(1)} %get-tuple-element.46), channel_id=1, source_target_pairs={{0,0},{1,1},{2,32},{3,33},{4,64},{5,65},{6,96},{7,97},{8,128},{9,1... | collective-permute-start | bytes 393224 | tf_op jit(solution)/shard_map/ppermute | solution.py:31
  15.1 47.1 %collective-permute-start.1 = (bf16[256,256]{1,0:T(8,128)(2,1)S(1)}, bf16[256,256]{1,0:T(8,128)(2,1)S(1)}, u32[]{:S(2)}, u32[]{:S(2)}) collective-permute-start(bf16[256,256]{1,0:T(8,128)(2,1)S(1)} %get-tuple-element.47), channel_id=1, source_target_pairs={{0,1},{1,0},{2,33},{3,32},{4,65},{5,64},{6,97},{7,96},{8,129},{9,1... | collective-permute-start | bytes 393224 | tf_op jit(solution)/shard_map/ppermute | solution.py:31
  62.2 24.6 %all-to-all-start = ((bf16[4,8,128,256]{3,2,1,0:T(8,128)(2,1)}), bf16[4,8,128,256]{3,2,1,0:T(8,128)(2,1)S(1)}, u32[]{:S(2)}, u32[]{:S(2)}) async-start(bf16[4,8,128,256]{3,2,1,0:T(8,128)(2,1)} %bitcast.11), calls=%async_computation | async-start | bytes 4194304 | tf_op jit(solution)/shard_map/all_to_all | solution.py:165
  86.8 20.5 %copy-start.1 = (bf16[4,8,128,256]{3,2,1,0:T(8,128)(2,1)}, bf16[4,8,128,256]{3,2,1,0:T(8,128)(2,1)S(1)}, u32[]{:S(2)}) copy-start(bf16[4,8,128,256]{3,2,1,0:T(8,128)(2,1)S(1)} %all-to-all-done.h_ref.own_ref) | copy-start | bytes 6291460
  86.8 31.1 %collective-permute-start.2 = (bf16[4,8,128,256]{3,2,1,0:T(8,128)(2,1)S(1)}, bf16[4,8,128,256]{3,2,1,0:T(8,128)(2,1)}, u32[]{:S(2)}, u32[]{:S(2)}) collective-permute-start(bf16[4,8,128,256]{3,2,1,0:T(8,128)(2,1)S(1)} %all-to-all-done.h_ref.own_ref), channel_id=1, source_target_pairs={{0,1},{1,0},{2,3},{3,2},{4,5},{5,4},{6,7},{7,6},{8,9},{9,8},{10,11... | collective-permute-start | bytes 6291464 | tf_op jit(solution)/shard_map/ppermute | solution.py:21
  111.8 12.0 %all-to-all-start.1 = ((bf16[4,256,256]{2,1,0:T(8,128)(2,1)}), bf16[4,256,256]{2,1,0:T(8,128)(2,1)S(1)}, u32[]{:S(2)}, u32[]{:S(2)}) async-start(bf16[4,256,256]{2,1,0:T(8,128)(2,1)} %get-tuple-element.27), calls=%async_computation.1 | async-start | bytes 1048576 | tf_op jit(solution)/shard_map/all_to_all | solution.py:134
  123.8 12.7 %all-to-all-start.2 = ((bf16[4,256,256]{2,1,0:T(8,128)(2,1)}), bf16[4,256,256]{2,1,0:T(8,128)(2,1)S(1)}, u32[]{:S(2)}, u32[]{:S(2)}) async-start(bf16[4,256,256]{2,1,0:T(8,128)(2,1)} %get-tuple-element.33), calls=%async_computation.2 | async-start | bytes 1048576 | tf_op jit(solution)/shard_map/all_to_all | solution.py:134
  136.5 6.0 %copy-start.5 = (f32[256,256]{1,0:T(8,128)S(1)}, f32[256,256]{1,0:T(8,128)}, u32[]{:S(2)}) copy-start(f32[256,256]{1,0:T(8,128)} %get-tuple-element.26) | copy-start | bytes 786436
  136.5 20.8 %all-to-all-start.3 = ((bf16[4,512,256]{2,1,0:T(8,128)(2,1)}), bf16[4,512,256]{2,1,0:T(8,128)(2,1)S(1)}, u32[]{:S(2)}, u32[]{:S(2)}) async-start(bf16[4,512,256]{2,1,0:T(8,128)(2,1)} %get-tuple-element.40), calls=%async_computation.3 | async-start | bytes 2097152 | tf_op jit(solution)/shard_map/all_to_all | solution.py:134
  141.5 13.8 %copy-start.6 = (f32[256,256]{1,0:T(8,128)S(1)}, f32[256,256]{1,0:T(8,128)}, u32[]{:S(2)}) copy-start(f32[256,256]{1,0:T(8,128)} %get-tuple-element.32) | copy-start | bytes 786436
  142.2 33.6 %copy-start.2 = (f32[512,256]{1,0:T(8,128)S(1)}, f32[512,256]{1,0:T(8,128)}, u32[]{:S(2)}) copy-start(f32[512,256]{1,0:T(8,128)} %param.6) | copy-start | bytes 1572868
  142.2 33.6 %copy-start.3 = (f32[512,256]{1,0:T(8,128)S(1)}, f32[512,256]{1,0:T(8,128)}, u32[]{:S(2)}) copy-start(f32[512,256]{1,0:T(8,128)} %param.7) | copy-start | bytes 1572868
  142.5 33.3 %copy-start.4 = (f32[512,256]{1,0:T(8,128)S(1)}, f32[512,256]{1,0:T(8,128)}, u32[]{:S(2)}) copy-start(f32[512,256]{1,0:T(8,128)} %get-tuple-element.39) | copy-start | bytes 1572868
  142.5 19.8 %collective-permute-start.3 = (bf16[256,256]{1,0:T(8,128)(2,1)S(1)}, bf16[256,256]{1,0:T(8,128)(2,1)S(1)}, u32[]{:S(2)}, u32[]{:S(2)}) collective-permute-start(bf16[256,256]{1,0:T(8,128)(2,1)S(1)} %add_convert_fusion.1), channel_id=1, source_target_pairs={{0,0},{1,1},{2,32},{3,33},{4,64},{5,65},{6,96},{7,97},{8,128},{9,1... | collective-permute-start | bytes 393224 | tf_op jit(solution)/shard_map/ppermute | solution.py:31
  155.4 20.4 %collective-permute-start.4 = (bf16[256,256]{1,0:T(8,128)(2,1)S(1)}, bf16[256,256]{1,0:T(8,128)(2,1)S(1)}, u32[]{:S(2)}, u32[]{:S(2)}) collective-permute-start(bf16[256,256]{1,0:T(8,128)(2,1)S(1)} %add_convert_fusion), channel_id=1, source_target_pairs={{0,1},{1,0},{2,33},{3,32},{4,65},{5,64},{6,97},{7,96},{8,129},{9,1... | collective-permute-start | bytes 393224 | tf_op jit(solution)/shard_map/ppermute | solution.py:31

commit v5 on v3

--- a/solution.py
+++ b/solution.py
@@ -131,6 +131,7 @@
         + [pl.BlockSpec(memory_space=pltpu.VMEM)] * (4 + len(hams)),
         out_specs=(pl.BlockSpec(memory_space=pltpu.VMEM), pl.BlockSpec(memory_space=pltpu.VMEM)),
         compiler_params=PARAMS,
+        cost_estimate=pl.CostEstimate(flops=20_000_000_000, bytes_accessed=40_000_000, transcendentals=0),
         name=name,
     )(where, bits, *tiles, *hams)
 
@@ -168,9 +169,8 @@
     owner = blk // 4
     at = (owner % 4) * 8 + (owner // 4) * 2 + (blk % 4) // 2
     packed = pack(jnp.where(live, at, -1), co[None], h_blocks)
-    packed = lax.optimization_barrier((packed, here, there, mirror_tiles[1]))[0]
     own = lax.all_to_all(packed.reshape(4, 8, W, 2 * W), "x", 0, 0, tiled=True)
-    other = swap_cores(lax.optimization_barrier((own, *direct_tiles[1:]))[0])
+    other = swap_cores(lax.optimization_barrier((own, tile))[0])
 
     names = lax.dynamic_slice_in_dim(pattern, zl * 16, 16, 0).reshape(8, 1, 2 * slots)
     i = jnp.arange(8, dtype=jnp.int32)
@@ -179,20 +179,21 @@
     here_first = jnp.stack([zl, x, co])
     there_first = jnp.stack([zl, x, 1 - co])
 
+    mirror, kept = partial_sums(
+        mirror_kernel, "mirror", (512, 256), here_first, bits, mirror_tiles, own, other
+    )
+    got = exchanged(mirror)
+    direct_tiles[3], mirror = lax.optimization_barrier((direct_tiles[3], mirror))
     upper, kept_upper = partial_sums(direct_kernel, "direct", (256, 256), here_first, bits, direct_tiles, own)
+    upper, got = lax.optimization_barrier((upper, got))
     got_upper = exchanged(upper)
     direct_tiles[3], upper = lax.optimization_barrier((direct_tiles[3], upper))
     lower, kept_lower = partial_sums(direct_kernel, "direct", (256, 256), there_first, bits, direct_tiles, other)
     lower, got_upper = lax.optimization_barrier((lower, got_upper))
     got_lower = exchanged(lower)
-    mirror_tiles[3], lower = lax.optimization_barrier((mirror_tiles[3], lower))
-    mirror, kept = partial_sums(
-        mirror_kernel, "mirror", (512, 256), here_first, bits, mirror_tiles, own, other
-    )
     here = turned(summed(got_upper, kept_upper, x).astype(jnp.bfloat16), 0)
-    got_lower, mirror = lax.optimization_barrier((got_lower, mirror))
     there = turned(summed(got_lower, kept_lower, x).astype(jnp.bfloat16), 1)
-    mirror_term = summed(exchanged(mirror), kept, x)
+    mirror_term = summed(got, kept, x)
     direct_term = jnp.where(
         co == 0, jnp.concatenate([here, there], axis=0), jnp.concatenate([there, here], axis=0)
     ).astype(jnp.float32)

time: 167 us -> 162 us (0.970)
  the two profiles are of different devices: /device:TPU:111 before, /device:TPU:79 now
where the time goes in v5:
time: 162 us
  starting transfers between devices  79.7 us (49%)
  waiting for transfers between devices  52.6 us (32%)
  Pallas kernels  20.8 us (13%)
  other arithmetic  5.69 us (4%)
  local copies, waits for them, and re-layouts  1.86 us (1%)
    ppermute x4, starting transfers between devices, turned(): return lax.ppermute(value, AXES, pairs)  40.9 us
    ppermute x4, waiting for transfers between devices, turned(): return lax.ppermute(value, AXES, pairs)  38.9 us
    ppermute x6, starting transfers between devices, shifted(): return lax.ppermute(value, axis, [(i, (i + step) % 4) for i in range(4)])  17.6 us
    pallas_call x3, Pallas kernels, partial_sums(): pl.pallas_call(kernel, out_shape=(jax.ShapeDtypeStruct((4, *shape), jnp.b...  16.3 us
    all_to_all x3, starting transfers between devices, exchanged(): return lax.all_to_all(parts, 'x', 0, 0, tiled=True)  14.4 us
    all_to_all x3, waiting for transfers between devices, exchanged(): return lax.all_to_all(parts, 'x', 0, 0, tiled=True)  7.31 us
    ppermute x6, waiting for transfers between devices, shifted(): return lax.ppermute(value, axis, [(i, (i + step) % 4) for i in range(4)])  6.36 us
    pallas_call x1, Pallas kernels, pack(): pl.pallas_call(pack_kernel, out_shape=jax.ShapeDtypeStruct((32, W, 2 * W)...  4.43 us
  transfers between devices with their start and end apart: 15, of which 8 were waited for; matrix products, arithmetic and copies ran while one was open for 2% of the time, Pallas kernels for 10%

profile of v5, /device:TPU:79, one launch (start us, length us, event | category | flops | bytes accessed | tf_op | source)
XLA Modules:
  0.0 161.5 jit_solution(2650545380689361059)
XLA Ops:
  0.0 0.7 copy-done
  0.9 0.7 dynamic-slice
  2.2 4.4 %pack.1 = bf16[32,128,256]{2,1,0:T(8,128)(2,1)} custom-call(s32[2,24]{1,0:T(2,128)} %compare_select_fusion.pos, s32[1]{0:T(128)} %bitcast.2.co, bf16[4,24,128,128]{3,2,1,0:T(8,128)(2,1)} %h_ref.1), custom_call_target="tpu_custom_call" | custom-call | tf_op jit(solution)/shard_map/pack/pallas_call | solution.py:52
  6.7 4.3 %all-to-all-start = ((bf16[4,8,128,256]{3,2,1,0:T(8,128)(2,1)}), bf16[4,8,128,256]{3,2,1,0:T(8,128)(2,1)S(1)}, u32[]{:S(2)}, u32[]{:S(2)}) async-start(bf16[4,8,128,256]{3,2,1,0:T(8,128)(2,1)} %bitcast.7), calls=%async_computation | async-start | bytes 4194304 | tf_op jit(solution)/shard_map/all_to_all | solution.py:172
  11.0 3.6 %collective-permute-start.2 = (bf16[512,256]{1,0:T(8,128)(2,1)S(1)}, bf16[512,256]{1,0:T(8,128)(2,1)S(1)}, u32[]{:S(2)}, u32[]{:S(2)}) collective-permute-start(bf16[512,256]{1,0:T(8,128)(2,1)S(1)} %convert_element_type.25.t0), channel_id=1, source_target_pairs={{0,128},{128,256},{256,384},{384,0},{1,129},{129,257},{257,385},{3... | collective-permute-start | bytes 786440 | tf_op jit(solution)/shard_map/ppermute | solution.py:17
  14.6 1.9 %collective-permute-start.3 = (bf16[512,256]{1,0:T(8,128)(2,1)S(1)}, bf16[512,256]{1,0:T(8,128)(2,1)S(1)}, u32[]{:S(2)}, u32[]{:S(2)}) collective-permute-start(bf16[512,256]{1,0:T(8,128)(2,1)S(1)} %convert_element_type.25.t0), channel_id=1, source_target_pairs={{0,256},{128,384},{256,0},{384,128},{1,257},{129,385},{257,1},{385... | collective-permute-start | bytes 786440 | tf_op jit(solution)/shard_map/ppermute | solution.py:17
  16.5 3.1 %collective-permute-start.4 = (bf16[512,256]{1,0:T(8,128)(2,1)S(1)}, bf16[512,256]{1,0:T(8,128)(2,1)S(1)}, u32[]{:S(2)}, u32[]{:S(2)}) collective-permute-start(bf16[512,256]{1,0:T(8,128)(2,1)S(1)} %convert_element_type.25.t0), channel_id=1, source_target_pairs={{0,384},{128,0},{256,128},{384,256},{1,385},{129,1},{257,129},{385... | collective-permute-start | bytes 786440 | tf_op jit(solution)/shard_map/ppermute | solution.py:17
  19.6 18.0 %collective-permute-start.1 = (bf16[256,256]{1,0:T(8,128)(2,1)S(1)}, bf16[256,256]{1,0:T(8,128)(2,1)S(1)}, u32[]{:S(2)}, u32[]{:S(2)}) collective-permute-start(bf16[256,256]{1,0:T(8,128)(2,1)S(1)} %get-tuple-element.36), channel_id=1, source_target_pairs={{0,1},{1,0},{2,33},{3,32},{4,65},{5,64},{6,97},{7,96},{8,129},{9,1... | collective-permute-start | bytes 393224 | tf_op jit(solution)/shard_map/ppermute | solution.py:31
  37.7 1.9 %collective-permute-start = (bf16[256,256]{1,0:T(8,128)(2,1)S(1)}, bf16[256,256]{1,0:T(8,128)(2,1)S(1)}, u32[]{:S(2)}, u32[]{:S(2)}) collective-permute-start(bf16[256,256]{1,0:T(8,128)(2,1)S(1)} %get-tuple-element.35), channel_id=1, source_target_pairs={{0,0},{1,1},{2,32},{3,33},{4,64},{5,65},{6,96},{7,97},{8,128},{9,1... | collective-permute-start | bytes 393224 | tf_op jit(solution)/shard_map/ppermute | solution.py:31
  39.6 7.0 %collective-permute-done.1 = bf16[256,256]{1,0:T(8,128)(2,1)S(1)} collective-permute-done((bf16[256,256]{1,0:T(8,128)(2,1)S(1)}, bf16[256,256]{1,0:T(8,128)(2,1)S(1)}, u32[]{:S(2)}, u32[]{:S(2)}) %collective-permute-start.1) | collective-permute-done | bytes 131104 | tf_op jit(solution)/shard_map/ppermute | solution.py:31
  46.6 16.7 %collective-permute-done = bf16[256,256]{1,0:T(8,128)(2,1)S(1)} collective-permute-done((bf16[256,256]{1,0:T(8,128)(2,1)S(1)}, bf16[256,256]{1,0:T(8,128)(2,1)S(1)}, u32[]{:S(2)}, u32[]{:S(2)}) %collective-permute-start) | collective-permute-done | bytes 131104 | tf_op jit(solution)/shard_map/ppermute | solution.py:31
  63.6 2.5 %collective-permute-start.8 = (bf16[4,8,128,256]{3,2,1,0:T(8,128)(2,1)S(1)}, bf16[4,8,128,256]{3,2,1,0:T(8,128)(2,1)}, u32[]{:S(2)}, u32[]{:S(2)}) collective-permute-start(bf16[4,8,128,256]{3,2,1,0:T(8,128)(2,1)S(1)} %all-to-all-done.own_ref.h_ref), channel_id=1, source_target_pairs={{0,1},{1,0},{2,3},{3,2},{4,5},{5,4},{6,7},{7,6},{8,9},{9,8},{10,11... | collective-permute-start | bytes 6291464 | tf_op jit(solution)/shard_map/ppermute | solution.py:21
  67.2 0.7 pad_add_fusion.where
  68.5 4.0 %collective-permute-start.5 = (bf16[256,512]{1,0:T(8,128)(2,1)S(1)}, bf16[256,512]{1,0:T(8,128)(2,1)}, u32[]{:S(2)}, u32[]{:S(2)}) collective-permute-start(bf16[256,512]{1,0:T(8,128)(2,1)S(1)} %maximum_select_fusion.t0), channel_id=1, source_target_pairs={{0,128},{128,256},{256,384},{384,0},{1,129},{129,257},{257,385},{3... | collective-permute-start | bytes 786440 | tf_op jit(solution)/shard_map/ppermute | solution.py:17
  72.6 1.9 %collective-permute-start.6 = (bf16[256,512]{1,0:T(8,128)(2,1)S(1)}, bf16[256,512]{1,0:T(8,128)(2,1)}, u32[]{:S(2)}, u32[]{:S(2)}) collective-permute-start(bf16[256,512]{1,0:T(8,128)(2,1)S(1)} %maximum_select_fusion.t0), channel_id=1, source_target_pairs={{0,256},{128,384},{256,0},{384,128},{1,257},{129,385},{257,1},{385... | collective-permute-start | bytes 786440 | tf_op jit(solution)/shard_map/ppermute | solution.py:17
  74.5 3.1 %collective-permute-start.7 = (bf16[256,512]{1,0:T(8,128)(2,1)S(1)}, bf16[256,512]{1,0:T(8,128)(2,1)}, u32[]{:S(2)}, u32[]{:S(2)}) collective-permute-start(bf16[256,512]{1,0:T(8,128)(2,1)S(1)} %maximum_select_fusion.t0), channel_id=1, source_target_pairs={{0,384},{128,0},{256,128},{384,256},{1,385},{129,1},{257,129},{385... | collective-permute-start | bytes 786440 | tf_op jit(solution)/shard_map/ppermute | solution.py:17
  77.6 7.3 %mirror.1 = (bf16[4,512,256]{2,1,0:T(8,128)(2,1)}, f32[512,256]{1,0:T(8,128)}) custom-call(s32[3]{0:T(128)} %pad_add_fusion.where, s32[8,8]{1,0:T(8,128)} %convert_element_type.24.bits, bf16[512,256]{1,0:T(8,128)(2,1)} %copy-done.4, bf16[512,256]{1,0:T(8,128)(2,1)} %copy-done.9, bf16[512,256]{1,0:T(8,128)(2,1)} %copy-done.10, bf16[512,256]{1,0:T(8,128)(2,1)} %copy-done.11, ...), custom_call_target="tpu_custom_call" | custom-call | flops 20000000000 | bytes 40000000 | tf_op jit(solution)/shard_map/mirror/pallas_call | solution.py:124
  84.9 3.9 %all-to-all-start.1 = ((bf16[4,512,256]{2,1,0:T(8,128)(2,1)}), bf16[4,512,256]{2,1,0:T(8,128)(2,1)S(1)}, u32[]{:S(2)}, u32[]{:S(2)}) async-start(bf16[4,512,256]{2,1,0:T(8,128)(2,1)} %get-tuple-element.21), calls=%async_computation.1 | async-start | bytes 2097152 | tf_op jit(solution)/shard_map/all_to_all | solution.py:140
  88.9 6.3 %collective-permute-done.7.t3 = bf16[256,512]{1,0:T(8,128)(2,1)} collective-permute-done((bf16[256,512]{1,0:T(8,128)(2,1)S(1)}, bf16[256,512]{1,0:T(8,128)(2,1)}, u32[]{:S(2)}, u32[]{:S(2)}) %collective-permute-start.7) | collective-permute-done | bytes 262176 | tf_op jit(solution)/shard_map/ppermute | solution.py:17
  95.2 4.5 %direct.2 = (bf16[4,256,256]{2,1,0:T(8,128)(2,1)}, f32[256,256]{1,0:T(8,128)}) custom-call(s32[3]{0:T(128)} %pad_add_fusion.where, s32[8,8]{1,0:T(8,128)} %convert_element_type.24.bits, bf16[256,512]{1,0:T(8,128)(2,1)} %copy-done.7, bf16[256,512]{1,0:T(8,128)(2,1)} %collective-permute-done.5.t1, bf16[256,512]{1,0:T(8,128)(2,1)} %collective-permute-done.6.t2, ...), custom_call_target="tpu_custom_call" | custom-call | flops 20000000000 | bytes 40000000 | tf_op jit(solution)/shard_map/direct/pallas_call | solution.py:124
  99.7 1.6 %all-to-all-done.1 = bf16[4,512,256]{2,1,0:T(8,128)(2,1)S(1)} async-done(((bf16[4,512,256]{2,1,0:T(8,128)(2,1)}), bf16[4,512,256]{2,1,0:T(8,128)(2,1)S(1)}, u32[]{:S(2)}, u32[]{:S(2)}) %all-to-all-start.1) | async-done | bytes 1048608 | tf_op jit(solution)/shard_map/all_to_all | solution.py:140
  101.4 5.2 %all-to-all-start.2 = ((bf16[4,256,256]{2,1,0:T(8,128)(2,1)}), bf16[4,256,256]{2,1,0:T(8,128)(2,1)S(1)}, u32[]{:S(2)}, u32[]{:S(2)}) async-start(bf16[4,256,256]{2,1,0:T(8,128)(2,1)} %get-tuple-element.25), calls=%async_computation.2 | async-start | bytes 1048576 | tf_op jit(solution)/shard_map/all_to_all | solution.py:140
  106.6 4.5 %direct.3 = (bf16[4,256,256]{2,1,0:T(8,128)(2,1)}, f32[256,256]{1,0:T(8,128)}) custom-call(s32[3]{0:T(128)} %pad_add_fusion.2.where, s32[8,8]{1,0:T(8,128)} %convert_element_type.24.bits, bf16[256,512]{1,0:T(8,128)(2,1)} %copy-done.7, bf16[256,512]{1,0:T(8,128)(2,1)} %collective-permute-done.5.t1, bf16[256,512]{1,0:T(8,128)(2,1)} %collective-permute-done.6.t2, ...), custom_call_target="tpu_custom_call" | custom-call | flops 20000000000 | bytes 40000000 | tf_op jit(solution)/shard_map/direct/pallas_call | solution.py:124
  111.1 1.1 all-to-all-done.2
  112.3 5.2 %all-to-all-start.3 = ((bf16[4,256,256]{2,1,0:T(8,128)(2,1)}), bf16[4,256,256]{2,1,0:T(8,128)(2,1)S(1)}, u32[]{:S(2)}, u32[]{:S(2)}) async-start(bf16[4,256,256]{2,1,0:T(8,128)(2,1)} %get-tuple-element.30), calls=%async_computation.3 | async-start | bytes 1048576 | tf_op jit(solution)/shard_map/all_to_all | solution.py:140
  118.2 4.5 %all-to-all-done.3 = bf16[4,256,256]{2,1,0:T(8,128)(2,1)S(1)} async-done(((bf16[4,256,256]{2,1,0:T(8,128)(2,1)}), bf16[4,256,256]{2,1,0:T(8,128)(2,1)S(1)}, u32[]{:S(2)}, u32[]{:S(2)}) %all-to-all-start.3) | async-done | bytes 524320 | tf_op jit(solution)/shard_map/all_to_all | solution.py:140
  123.0 1.0 add_convert_fusion
  124.0 14.4 %collective-permute-start.10 = (bf16[256,256]{1,0:T(8,128)(2,1)S(1)}, bf16[256,256]{1,0:T(8,128)(2,1)S(1)}, u32[]{:S(2)}, u32[]{:S(2)}) collective-permute-start(bf16[256,256]{1,0:T(8,128)(2,1)S(1)} %add_convert_fusion), channel_id=1, source_target_pairs={{0,1},{1,0},{2,33},{3,32},{4,65},{5,64},{6,97},{7,96},{8,129},{9,1... | collective-permute-start | bytes 393224 | tf_op jit(solution)/shard_map/ppermute | solution.py:31
  138.4 6.6 %collective-permute-start.9 = (bf16[256,256]{1,0:T(8,128)(2,1)S(1)}, bf16[256,256]{1,0:T(8,128)(2,1)S(1)}, u32[]{:S(2)}, u32[]{:S(2)}) collective-permute-start(bf16[256,256]{1,0:T(8,128)(2,1)S(1)} %add_convert_fusion.1), channel_id=1, source_target_pairs={{0,0},{1,1},{2,32},{3,33},{4,64},{5,65},{6,96},{7,97},{8,128},{9,1... | collective-permute-start | bytes 393224 | tf_op jit(solution)/shard_map/ppermute | solution.py:31
  145.3 4.1 %collective-permute-done.10 = bf16[256,256]{1,0:T(8,128)(2,1)S(1)} collective-permute-done((bf16[256,256]{1,0:T(8,128)(2,1)S(1)}, bf16[256,256]{1,0:T(8,128)(2,1)S(1)}, u32[]{:S(2)}, u32[]{:S(2)}) %collective-permute-start.10) | collective-permute-done | bytes 131104 | tf_op jit(solution)/shard_map/ppermute | solution.py:31
  149.4 11.0 %collective-permute-done.9 = bf16[256,256]{1,0:T(8,128)(2,1)S(1)} collective-permute-done((bf16[256,256]{1,0:T(8,128)(2,1)S(1)}, bf16[256,256]{1,0:T(8,128)(2,1)S(1)}, u32[]{:S(2)}, u32[]{:S(2)}) %collective-permute-start.9) | collective-permute-done | bytes 131104 | tf_op jit(solution)/shard_map/ppermute | solution.py:31
  160.5 1.1 maximum_divide_fusion
  (47 shorter events, 3.4 us)
Async XLA Ops:
  0.0 0.7 copy-start
  6.7 4.3 %copy-start.2 = (f32[512,256]{1,0:T(8,128)S(1)}, f32[512,256]{1,0:T(8,128)}, u32[]{:S(2)}) copy-start(f32[512,256]{1,0:T(8,128)} %param.6) | copy-start | bytes 1572868
  6.7 56.9 %all-to-all-start = ((bf16[4,8,128,256]{3,2,1,0:T(8,128)(2,1)}), bf16[4,8,128,256]{3,2,1,0:T(8,128)(2,1)S(1)}, u32[]{:S(2)}, u32[]{:S(2)}) async-start(bf16[4,8,128,256]{3,2,1,0:T(8,128)(2,1)} %bitcast.7), calls=%async_computation | async-start | bytes 4194304 | tf_op jit(solution)/shard_map/all_to_all | solution.py:172
  11.0 66.6 %copy-start.4 = (bf16[512,256]{1,0:T(8,128)(2,1)}, bf16[512,256]{1,0:T(8,128)(2,1)S(1)}, u32[]{:S(2)}) copy-start(bf16[512,256]{1,0:T(8,128)(2,1)S(1)} %convert_element_type.25.t0) | copy-start | bytes 786436
  11.0 52.5 %collective-permute-start.2 = (bf16[512,256]{1,0:T(8,128)(2,1)S(1)}, bf16[512,256]{1,0:T(8,128)(2,1)S(1)}, u32[]{:S(2)}, u32[]{:S(2)}) collective-permute-start(bf16[512,256]{1,0:T(8,128)(2,1)S(1)} %convert_element_type.25.t0), channel_id=1, source_target_pairs={{0,128},{128,256},{256,384},{384,0},{1,129},{129,257},{257,385},{3... | collective-permute-start | bytes 786440 | tf_op jit(solution)/shard_map/ppermute | solution.py:17
  14.6 49.0 %collective-permute-start.3 = (bf16[512,256]{1,0:T(8,128)(2,1)S(1)}, bf16[512,256]{1,0:T(8,128)(2,1)S(1)}, u32[]{:S(2)}, u32[]{:S(2)}) collective-permute-start(bf16[512,256]{1,0:T(8,128)(2,1)S(1)} %convert_element_type.25.t0), channel_id=1, source_target_pairs={{0,256},{128,384},{256,0},{384,128},{1,257},{129,385},{257,1},{385... | collective-permute-start | bytes 786440 | tf_op jit(solution)/shard_map/ppermute | solution.py:17
  16.5 47.1 %collective-permute-start.4 = (bf16[512,256]{1,0:T(8,128)(2,1)S(1)}, bf16[512,256]{1,0:T(8,128)(2,1)S(1)}, u32[]{:S(2)}, u32[]{:S(2)}) collective-permute-start(bf16[512,256]{1,0:T(8,128)(2,1)S(1)} %convert_element_type.25.t0), channel_id=1, source_target_pairs={{0,384},{128,0},{256,128},{384,256},{1,385},{129,1},{257,129},{385... | collective-permute-start | bytes 786440 | tf_op jit(solution)/shard_map/ppermute | solution.py:17
  19.6 27.0 %collective-permute-start.1 = (bf16[256,256]{1,0:T(8,128)(2,1)S(1)}, bf16[256,256]{1,0:T(8,128)(2,1)S(1)}, u32[]{:S(2)}, u32[]{:S(2)}) collective-permute-start(bf16[256,256]{1,0:T(8,128)(2,1)S(1)} %get-tuple-element.36), channel_id=1, source_target_pairs={{0,1},{1,0},{2,33},{3,32},{4,65},{5,64},{6,97},{7,96},{8,129},{9,1... | collective-permute-start | bytes 393224 | tf_op jit(solution)/shard_map/ppermute | solution.py:31
  37.7 25.7 %collective-permute-start = (bf16[256,256]{1,0:T(8,128)(2,1)S(1)}, bf16[256,256]{1,0:T(8,128)(2,1)S(1)}, u32[]{:S(2)}, u32[]{:S(2)}) collective-permute-start(bf16[256,256]{1,0:T(8,128)(2,1)S(1)} %get-tuple-element.35), channel_id=1, source_target_pairs={{0,0},{1,1},{2,32},{3,33},{4,64},{5,65},{6,96},{7,97},{8,128},{9,1... | collective-permute-start | bytes 393224 | tf_op jit(solution)/shard_map/ppermute | solution.py:31
  63.5 21.4 %copy-start.7 = (bf16[256,512]{1,0:T(8,128)(2,1)}, bf16[256,512]{1,0:T(8,128)(2,1)S(1)}, u32[]{:S(2)}) copy-start(bf16[256,512]{1,0:T(8,128)(2,1)S(1)} %maximum_select_fusion.t0) | copy-start | bytes 786436
  63.5 14.1 %copy-start.9 = (bf16[512,256]{1,0:T(8,128)(2,1)}, bf16[512,256]{1,0:T(8,128)(2,1)S(1)}, u32[]{:S(2)}) copy-start(bf16[512,256]{1,0:T(8,128)(2,1)S(1)} %collective-permute-done.2.t1) | copy-start | bytes 786436
  63.5 14.1 %copy-start.10 = (bf16[512,256]{1,0:T(8,128)(2,1)}, bf16[512,256]{1,0:T(8,128)(2,1)S(1)}, u32[]{:S(2)}) copy-start(bf16[512,256]{1,0:T(8,128)(2,1)S(1)} %collective-permute-done.3.t2) | copy-start | bytes 786436
  63.6 14.1 %copy-start.11 = (bf16[512,256]{1,0:T(8,128)(2,1)}, bf16[512,256]{1,0:T(8,128)(2,1)S(1)}, u32[]{:S(2)}) copy-start(bf16[512,256]{1,0:T(8,128)(2,1)S(1)} %collective-permute-done.4.t3) | copy-start | bytes 786436
  63.6 14.1 %copy-start.1 = (bf16[4,8,128,256]{3,2,1,0:T(8,128)(2,1)}, bf16[4,8,128,256]{3,2,1,0:T(8,128)(2,1)S(1)}, u32[]{:S(2)}) copy-start(bf16[4,8,128,256]{3,2,1,0:T(8,128)(2,1)S(1)} %all-to-all-done.own_ref.h_ref) | copy-start | bytes 6291460
  63.6 14.0 %collective-permute-start.8 = (bf16[4,8,128,256]{3,2,1,0:T(8,128)(2,1)S(1)}, bf16[4,8,128,256]{3,2,1,0:T(8,128)(2,1)}, u32[]{:S(2)}, u32[]{:S(2)}) collective-permute-start(bf16[4,8,128,256]{3,2,1,0:T(8,128)(2,1)S(1)} %all-to-all-done.own_ref.h_ref), channel_id=1, source_target_pairs={{0,1},{1,0},{2,3},{3,2},{4,5},{5,4},{6,7},{7,6},{8,9},{9,8},{10,11... | collective-permute-start | bytes 6291464 | tf_op jit(solution)/shard_map/ppermute | solution.py:21
  68.5 26.7 %collective-permute-start.5 = (bf16[256,512]{1,0:T(8,128)(2,1)S(1)}, bf16[256,512]{1,0:T(8,128)(2,1)}, u32[]{:S(2)}, u32[]{:S(2)}) collective-permute-start(bf16[256,512]{1,0:T(8,128)(2,1)S(1)} %maximum_select_fusion.t0), channel_id=1, source_target_pairs={{0,128},{128,256},{256,384},{384,0},{1,129},{129,257},{257,385},{3... | collective-permute-start | bytes 786440 | tf_op jit(solution)/shard_map/ppermute | solution.py:17
  72.6 22.6 %collective-permute-start.6 = (bf16[256,512]{1,0:T(8,128)(2,1)S(1)}, bf16[256,512]{1,0:T(8,128)(2,1)}, u32[]{:S(2)}, u32[]{:S(2)}) collective-permute-start(bf16[256,512]{1,0:T(8,128)(2,1)S(1)} %maximum_select_fusion.t0), channel_id=1, source_target_pairs={{0,256},{128,384},{256,0},{384,128},{1,257},{129,385},{257,1},{385... | collective-permute-start | bytes 786440 | tf_op jit(solution)/shard_map/ppermute | solution.py:17
  74.5 20.7 %collective-permute-start.7 = (bf16[256,512]{1,0:T(8,128)(2,1)S(1)}, bf16[256,512]{1,0:T(8,128)(2,1)}, u32[]{:S(2)}, u32[]{:S(2)}) collective-permute-start(bf16[256,512]{1,0:T(8,128)(2,1)S(1)} %maximum_select_fusion.t0), channel_id=1, source_target_pairs={{0,384},{128,0},{256,128},{384,256},{1,385},{129,1},{257,129},{385... | collective-permute-start | bytes 786440 | tf_op jit(solution)/shard_map/ppermute | solution.py:17
  84.9 16.5 %all-to-all-start.1 = ((bf16[4,512,256]{2,1,0:T(8,128)(2,1)}), bf16[4,512,256]{2,1,0:T(8,128)(2,1)S(1)}, u32[]{:S(2)}, u32[]{:S(2)}) async-start(bf16[4,512,256]{2,1,0:T(8,128)(2,1)} %get-tuple-element.21), calls=%async_computation.1 | async-start | bytes 2097152 | tf_op jit(solution)/shard_map/all_to_all | solution.py:140
  101.4 10.9 %all-to-all-start.2 = ((bf16[4,256,256]{2,1,0:T(8,128)(2,1)}), bf16[4,256,256]{2,1,0:T(8,128)(2,1)S(1)}, u32[]{:S(2)}, u32[]{:S(2)}) async-start(bf16[4,256,256]{2,1,0:T(8,128)(2,1)} %get-tuple-element.25), calls=%async_computation.2 | async-start | bytes 1048576 | tf_op jit(solution)/shard_map/all_to_all | solution.py:140
  111.1 27.3 %copy-start.8 = (f32[256,256]{1,0:T(8,128)S(1)}, f32[256,256]{1,0:T(8,128)}, u32[]{:S(2)}) copy-start(f32[256,256]{1,0:T(8,128)} %get-tuple-element.23) | copy-start | bytes 786436
  112.3 10.5 %all-to-all-start.3 = ((bf16[4,256,256]{2,1,0:T(8,128)(2,1)}), bf16[4,256,256]{2,1,0:T(8,128)(2,1)S(1)}, u32[]{:S(2)}, u32[]{:S(2)}) async-start(bf16[4,256,256]{2,1,0:T(8,128)(2,1)} %get-tuple-element.30), calls=%async_computation.3 | async-start | bytes 1048576 | tf_op jit(solution)/shard_map/all_to_all | solution.py:140
  118.2 42.3 %copy-start.3 = (f32[512,256]{1,0:T(8,128)S(1)}, f32[512,256]{1,0:T(8,128)}, u32[]{:S(2)}) copy-start(f32[512,256]{1,0:T(8,128)} %param.6) | copy-start | bytes 1572868
  118.2 42.3 %copy-start.5 = (f32[512,256]{1,0:T(8,128)S(1)}, f32[512,256]{1,0:T(8,128)}, u32[]{:S(2)}) copy-start(f32[512,256]{1,0:T(8,128)} %param.7) | copy-start | bytes 1572868
  122.7 37.7 %copy-start.6 = (f32[512,256]{1,0:T(8,128)S(1)}, f32[512,256]{1,0:T(8,128)}, u32[]{:S(2)}) copy-start(f32[512,256]{1,0:T(8,128)} %get-tuple-element.31) | copy-start | bytes 1572868
  124.0 25.4 %collective-permute-start.10 = (bf16[256,256]{1,0:T(8,128)(2,1)S(1)}, bf16[256,256]{1,0:T(8,128)(2,1)S(1)}, u32[]{:S(2)}, u32[]{:S(2)}) collective-permute-start(bf16[256,256]{1,0:T(8,128)(2,1)S(1)} %add_convert_fusion), channel_id=1, source_target_pairs={{0,1},{1,0},{2,33},{3,32},{4,65},{5,64},{6,97},{7,96},{8,129},{9,1... | collective-permute-start | bytes 393224 | tf_op jit(solution)/shard_map/ppermute | solution.py:31
  138.4 22.0 %collective-permute-start.9 = (bf16[256,256]{1,0:T(8,128)(2,1)S(1)}, bf16[256,256]{1,0:T(8,128)(2,1)S(1)}, u32[]{:S(2)}, u32[]{:S(2)}) collective-permute-start(bf16[256,256]{1,0:T(8,128)(2,1)S(1)} %add_convert_fusion.1), channel_id=1, source_target_pairs={{0,0},{1,1},{2,32},{3,33},{4,64},{5,65},{6,96},{7,97},{8,128},{9,1... | collective-permute-start | bytes 393224 | tf_op jit(solution)/shard_map/ppermute | solution.py:31

commit v6 on v3

--- a/solution.py
+++ b/solution.py
@@ -131,8 +131,28 @@
         + [pl.BlockSpec(memory_space=pltpu.VMEM)] * (4 + len(hams)),
         out_specs=(pl.BlockSpec(memory_space=pltpu.VMEM), pl.BlockSpec(memory_space=pltpu.VMEM)),
         compiler_params=PARAMS,
+        cost_estimate=pl.CostEstimate(flops=20_000_000_000, bytes_accessed=40_000_000, transcendentals=0),
         name=name,
     )(where, bits, *tiles, *hams)
+
+
+def base_kernel(co, energy, here_ref, there_ref, coeffs_ref, diag_ref, out_ref):
+    for at, ref in ((co[0], here_ref), (1 - co[0], there_ref)):
+        rows = pl.ds(pl.multiple_of(at * 256, 256), 256)
+        coeffs = coeffs_ref[rows, :]
+        out_ref[rows, :] = ref[...].astype(jnp.float32) + diag_ref[rows, :] * coeffs - energy[0] * coeffs
+
+
+def direct_base(co, energy, here, there, coeffs, diag_energy):
+    return pl.pallas_call(
+        base_kernel,
+        out_shape=jax.ShapeDtypeStruct(coeffs.shape, jnp.float32),
+        in_specs=[pl.BlockSpec(memory_space=pltpu.SMEM)] * 2 + [pl.BlockSpec(memory_space=pltpu.VMEM)] * 4,
+        out_specs=pl.BlockSpec(memory_space=pltpu.VMEM),
+        compiler_params=PARAMS,
+        cost_estimate=pl.CostEstimate(flops=20_000_000_000, bytes_accessed=40_000_000, transcendentals=0),
+        name="base",
+    )(co, energy, here, there, coeffs, diag_energy)
 
 
 def exchanged(parts):
@@ -157,9 +177,9 @@
     tile = jnp.where(
         co == 0, jnp.concatenate([here, there], axis=1), jnp.concatenate([there, here], axis=1)
     )
-    mirror_tiles = [half] + [shifted(half, "zl", d) for d in (1, 2, 3)]
-    tile = lax.optimization_barrier((tile, *mirror_tiles[1:]))[0]
     direct_tiles = [tile] + [shifted(tile, "zl", d) for d in (1, 2, 3)]
+    later = lax.optimization_barrier((half, *direct_tiles[1:]))[0]
+    mirror_tiles = [half] + [shifted(later, "zl", d) for d in (1, 2, 3)]
 
     filled = jnp.arange(slots, dtype=jnp.int32)[None, :] < counts[:, None]
     begin = row_id * 4 + co * 2
@@ -168,7 +188,7 @@
     owner = blk // 4
     at = (owner % 4) * 8 + (owner // 4) * 2 + (blk % 4) // 2
     packed = pack(jnp.where(live, at, -1), co[None], h_blocks)
-    packed = lax.optimization_barrier((packed, here, there, mirror_tiles[1]))[0]
+    packed = lax.optimization_barrier((packed, tile))[0]
     own = lax.all_to_all(packed.reshape(4, 8, W, 2 * W), "x", 0, 0, tiled=True)
     other = swap_cores(lax.optimization_barrier((own, *direct_tiles[1:]))[0])
 
@@ -183,23 +203,20 @@
     got_upper = exchanged(upper)
     direct_tiles[3], upper = lax.optimization_barrier((direct_tiles[3], upper))
     lower, kept_lower = partial_sums(direct_kernel, "direct", (256, 256), there_first, bits, direct_tiles, other)
-    lower, got_upper = lax.optimization_barrier((lower, got_upper))
+    lower, got_upper, mirror_tiles[1], mirror_tiles[3] = lax.optimization_barrier(
+        (lower, got_upper, mirror_tiles[1], mirror_tiles[3])
+    )
     got_lower = exchanged(lower)
+    upper = summed(got_upper, kept_upper, x).astype(jnp.bfloat16)
+    lower = summed(got_lower, kept_lower, x).astype(jnp.bfloat16)
+    here, there = turned(upper, 0), turned(lower, 1)
     mirror_tiles[3], lower = lax.optimization_barrier((mirror_tiles[3], lower))
     mirror, kept = partial_sums(
         mirror_kernel, "mirror", (512, 256), here_first, bits, mirror_tiles, own, other
     )
-    here = turned(summed(got_upper, kept_upper, x).astype(jnp.bfloat16), 0)
-    got_lower, mirror = lax.optimization_barrier((got_lower, mirror))
-    there = turned(summed(got_lower, kept_lower, x).astype(jnp.bfloat16), 1)
     mirror_term = summed(exchanged(mirror), kept, x)
-    direct_term = jnp.where(
-        co == 0, jnp.concatenate([here, there], axis=0), jnp.concatenate([there, here], axis=0)
-    ).astype(jnp.float32)
-
-    sigma_full = direct_term + mirror_term + diag_energy * coeffs
-    shift_value = energy[0]
-    return (sigma_full - shift_value * coeffs) / jnp.maximum(jnp.abs(diag_energy - shift_value), 1.0)
+    base = direct_base(co[None], energy, here, there, coeffs, diag_energy)
+    return (base + mirror_term) / jnp.maximum(jnp.abs(diag_energy - energy[0]), 1.0)
 
 
 def solution(mesh):

time: 167 us -> 159 us (0.952)
  the two profiles are of different devices: /device:TPU:111 before, /device:TPU:24 now
where the time goes in v6:
time: 159 us; the launch traced here: 158 us
  starting transfers between devices  86.1 us (54%)
  waiting for transfers between devices  38.4 us (24%)
  Pallas kernels  23 us (14%)
  other arithmetic  6.64 us (4%)
  local copies, waits for them, and re-layouts  3.13 us (2%)
    ppermute x6, starting transfers between devices, shifted(): return lax.ppermute(value, axis, [(i, (i + step) % 4) for i in range(4)])  44.3 us
    all_to_all x3, waiting for transfers between devices, exchanged(): return lax.all_to_all(parts, 'x', 0, 0, tiled=True)  22.8 us
    all_to_all x3, starting transfers between devices, exchanged(): return lax.all_to_all(parts, 'x', 0, 0, tiled=True)  21.3 us
    pallas_call x3, Pallas kernels, partial_sums(): pl.pallas_call(kernel, out_shape=(jax.ShapeDtypeStruct((4, *shape), jnp.b...  16.4 us
    ppermute x4, starting transfers between devices, turned(): return lax.ppermute(value, AXES, pairs)  15 us
    ppermute x6, waiting for transfers between devices, shifted(): return lax.ppermute(value, axis, [(i, (i + step) % 4) for i in range(4)])  10.6 us
    ppermute x4, waiting for transfers between devices, turned(): return lax.ppermute(value, AXES, pairs)  4.91 us
    pallas_call x1, Pallas kernels, pack(): pl.pallas_call(pack_kernel, out_shape=jax.ShapeDtypeStruct((32, W, 2 * W)...  4.37 us
  transfers between devices with their start and end apart: 15, of which 8 were waited for; matrix products, arithmetic and copies ran while one was open for 3% of the time, Pallas kernels for 15%

profile of v6, /device:TPU:24, one launch (start us, length us, event | category | flops | bytes accessed | tf_op | source)
XLA Modules:
  0.0 158.2 jit_solution(7471148595672135715)
XLA Ops:
  0.0 1.1 convert_element_type.22.t0
  1.1 3.8 %collective-permute-start.1 = (bf16[256,256]{1,0:T(8,128)(2,1)S(1)}, bf16[256,256]{1,0:T(8,128)(2,1)S(1)}, u32[]{:S(2)}, u32[]{:S(2)}) collective-permute-start(bf16[256,256]{1,0:T(8,128)(2,1)S(1)} %get-tuple-element.38), channel_id=1, source_target_pairs={{0,1},{1,0},{2,33},{3,32},{4,65},{5,64},{6,97},{7,96},{8,129},{9,1... | collective-permute-start | bytes 393224 | tf_op jit(solution)/shard_map/ppermute | solution.py:31
  4.9 4.8 %collective-permute-start = (bf16[256,256]{1,0:T(8,128)(2,1)S(1)}, bf16[256,256]{1,0:T(8,128)(2,1)S(1)}, u32[]{:S(2)}, u32[]{:S(2)}) collective-permute-start(bf16[256,256]{1,0:T(8,128)(2,1)S(1)} %get-tuple-element.37), channel_id=1, source_target_pairs={{0,0},{1,1},{2,32},{3,33},{4,64},{5,65},{6,96},{7,97},{8,128},{9,1... | collective-permute-start | bytes 393224 | tf_op jit(solution)/shard_map/ppermute | solution.py:31
  9.9 0.7 dynamic-slice
  11.3 4.4 %pack.1 = bf16[32,128,256]{2,1,0:T(8,128)(2,1)} custom-call(s32[2,24]{1,0:T(2,128)} %compare_select_fusion.pos, s32[1]{0:T(128)} %bitcast.co, bf16[4,24,128,128]{3,2,1,0:T(8,128)(2,1)} %h_ref.1), custom_call_target="tpu_custom_call" | custom-call | tf_op jit(solution)/shard_map/pack/pallas_call | solution.py:52
  15.7 1.4 collective-permute-done.1
  17.1 3.5 %collective-permute-done = bf16[256,256]{1,0:T(8,128)(2,1)S(1)} collective-permute-done((bf16[256,256]{1,0:T(8,128)(2,1)S(1)}, bf16[256,256]{1,0:T(8,128)(2,1)S(1)}, u32[]{:S(2)}, u32[]{:S(2)}) %collective-permute-start) | collective-permute-done | bytes 131104 | tf_op jit(solution)/shard_map/ppermute | solution.py:31
  20.7 3.6 %all-to-all-start = ((bf16[4,8,128,256]{3,2,1,0:T(8,128)(2,1)}), bf16[4,8,128,256]{3,2,1,0:T(8,128)(2,1)S(1)}, u32[]{:S(2)}, u32[]{:S(2)}) async-start(bf16[4,8,128,256]{3,2,1,0:T(8,128)(2,1)} %bitcast.7), calls=%async_computation | async-start | bytes 4194304 | tf_op jit(solution)/shard_map/all_to_all | solution.py:192
  24.3 10.8 %collective-permute-start.2 = (bf16[256,512]{1,0:T(8,128)(2,1)S(1)}, bf16[256,512]{1,0:T(8,128)(2,1)S(1)}, u32[]{:S(2)}, u32[]{:S(2)}) collective-permute-start(bf16[256,512]{1,0:T(8,128)(2,1)S(1)} %maximum_select_fusion.t0), channel_id=1, source_target_pairs={{0,128},{128,256},{256,384},{384,0},{1,129},{129,257},{257,385},{3... | collective-permute-start | bytes 786440 | tf_op jit(solution)/shard_map/ppermute | solution.py:17
  35.1 14.5 %collective-permute-start.3 = (bf16[256,512]{1,0:T(8,128)(2,1)S(1)}, bf16[256,512]{1,0:T(8,128)(2,1)S(1)}, u32[]{:S(2)}, u32[]{:S(2)}) collective-permute-start(bf16[256,512]{1,0:T(8,128)(2,1)S(1)} %maximum_select_fusion.t0), channel_id=1, source_target_pairs={{0,256},{128,384},{256,0},{384,128},{1,257},{129,385},{257,1},{385... | collective-permute-start | bytes 786440 | tf_op jit(solution)/shard_map/ppermute | solution.py:17
  49.7 4.6 %collective-permute-start.4 = (bf16[256,512]{1,0:T(8,128)(2,1)S(1)}, bf16[256,512]{1,0:T(8,128)(2,1)}, u32[]{:S(2)}, u32[]{:S(2)}) collective-permute-start(bf16[256,512]{1,0:T(8,128)(2,1)S(1)} %maximum_select_fusion.t0), channel_id=1, source_target_pairs={{0,384},{128,0},{256,128},{384,256},{1,385},{129,1},{257,129},{385... | collective-permute-start | bytes 786440 | tf_op jit(solution)/shard_map/ppermute | solution.py:17
  55.4 9.4 %collective-permute-done.3.t2 = bf16[256,512]{1,0:T(8,128)(2,1)S(1)} collective-permute-done((bf16[256,512]{1,0:T(8,128)(2,1)S(1)}, bf16[256,512]{1,0:T(8,128)(2,1)S(1)}, u32[]{:S(2)}, u32[]{:S(2)}) %collective-permute-start.3) | collective-permute-done | bytes 262176 | tf_op jit(solution)/shard_map/ppermute | solution.py:17
  65.2 1.9 %collective-permute-start.5 = (bf16[4,8,128,256]{3,2,1,0:T(8,128)(2,1)S(1)}, bf16[4,8,128,256]{3,2,1,0:T(8,128)(2,1)}, u32[]{:S(2)}, u32[]{:S(2)}) collective-permute-start(bf16[4,8,128,256]{3,2,1,0:T(8,128)(2,1)S(1)} %all-to-all-done.h_ref.own_ref), channel_id=1, source_target_pairs={{0,1},{1,0},{2,3},{3,2},{4,5},{5,4},{6,7},{7,6},{8,9},{9,8},{10,11... | collective-permute-start | bytes 6291464 | tf_op jit(solution)/shard_map/ppermute | solution.py:21
  67.7 0.7 pad_add_fusion.2.where
  68.3 7.7 %collective-permute-start.6 = (bf16[512,256]{1,0:T(8,128)(2,1)S(1)}, bf16[512,256]{1,0:T(8,128)(2,1)S(1)}, u32[]{:S(2)}, u32[]{:S(2)}) collective-permute-start(bf16[512,256]{1,0:T(8,128)(2,1)S(1)} %convert_element_type.22.t0), channel_id=1, source_target_pairs={{0,128},{128,256},{256,384},{384,0},{1,129},{129,257},{257,385},{3... | collective-permute-start | bytes 786440 | tf_op jit(solution)/shard_map/ppermute | solution.py:17
  76.0 4.2 %collective-permute-start.7 = (bf16[512,256]{1,0:T(8,128)(2,1)S(1)}, bf16[512,256]{1,0:T(8,128)(2,1)S(1)}, u32[]{:S(2)}, u32[]{:S(2)}) collective-permute-start(bf16[512,256]{1,0:T(8,128)(2,1)S(1)} %convert_element_type.22.t0), channel_id=1, source_target_pairs={{0,384},{128,0},{256,128},{384,256},{1,385},{129,1},{257,129},{385... | collective-permute-start | bytes 786440 | tf_op jit(solution)/shard_map/ppermute | solution.py:17
  80.3 4.5 %direct.2 = (bf16[4,256,256]{2,1,0:T(8,128)(2,1)}, f32[256,256]{1,0:T(8,128)}) custom-call(s32[3]{0:T(128)} %pad_add_fusion.where, s32[8,8]{1,0:T(8,128)} %convert_element_type.21.bits, bf16[256,512]{1,0:T(8,128)(2,1)} %copy-done.5, bf16[256,512]{1,0:T(8,128)(2,1)} %copy-done.10, bf16[256,512]{1,0:T(8,128)(2,1)} %copy-done.11, ...), custom_call_target="tpu_custom_call" | custom-call | flops 20000000000 | bytes 40000000 | tf_op jit(solution)/shard_map/direct/pallas_call | solution.py:124
  84.8 4.5 %all-to-all-start.1 = ((bf16[4,256,256]{2,1,0:T(8,128)(2,1)}), bf16[4,256,256]{2,1,0:T(8,128)(2,1)S(1)}, u32[]{:S(2)}, u32[]{:S(2)}) async-start(bf16[4,256,256]{2,1,0:T(8,128)(2,1)} %get-tuple-element.22), calls=%async_computation.1 | async-start | bytes 1048576 | tf_op jit(solution)/shard_map/all_to_all | solution.py:159
  89.2 4.5 %direct.3 = (bf16[4,256,256]{2,1,0:T(8,128)(2,1)}, f32[256,256]{1,0:T(8,128)}) custom-call(s32[3]{0:T(128)} %pad_add_fusion.2.where, s32[8,8]{1,0:T(8,128)} %convert_element_type.21.bits, bf16[256,512]{1,0:T(8,128)(2,1)} %copy-done.5, bf16[256,512]{1,0:T(8,128)(2,1)} %copy-done.10, bf16[256,512]{1,0:T(8,128)(2,1)} %copy-done.11, ...), custom_call_target="tpu_custom_call" | custom-call | flops 20000000000 | bytes 40000000 | tf_op jit(solution)/shard_map/direct/pallas_call | solution.py:124
  93.8 5.3 %all-to-all-done.1 = bf16[4,256,256]{2,1,0:T(8,128)(2,1)S(1)} async-done(((bf16[4,256,256]{2,1,0:T(8,128)(2,1)}), bf16[4,256,256]{2,1,0:T(8,128)(2,1)S(1)}, u32[]{:S(2)}, u32[]{:S(2)}) %all-to-all-start.1) | async-done | bytes 524320 | tf_op jit(solution)/shard_map/all_to_all | solution.py:159
  99.1 3.5 %all-to-all-start.2 = ((bf16[4,256,256]{2,1,0:T(8,128)(2,1)}), bf16[4,256,256]{2,1,0:T(8,128)(2,1)S(1)}, u32[]{:S(2)}, u32[]{:S(2)}) async-start(bf16[4,256,256]{2,1,0:T(8,128)(2,1)} %get-tuple-element.29), calls=%async_computation.2 | async-start | bytes 1048576 | tf_op jit(solution)/shard_map/all_to_all | solution.py:159
  103.3 2.5 %collective-permute-start.10 = (bf16[512,256]{1,0:T(8,128)(2,1)S(1)}, bf16[512,256]{1,0:T(8,128)(2,1)S(1)}, u32[]{:S(2)}, u32[]{:S(2)}) collective-permute-start(bf16[512,256]{1,0:T(8,128)(2,1)S(1)} %convert_element_type.22.t0), channel_id=1, source_target_pairs={{0,256},{128,384},{256,0},{384,128},{1,257},{129,385},{257,1},{385... | collective-permute-start | bytes 786440 | tf_op jit(solution)/shard_map/ppermute | solution.py:17
  105.7 5.8 %all-to-all-done.2 = bf16[4,256,256]{2,1,0:T(8,128)(2,1)S(1)} async-done(((bf16[4,256,256]{2,1,0:T(8,128)(2,1)}), bf16[4,256,256]{2,1,0:T(8,128)(2,1)S(1)}, u32[]{:S(2)}, u32[]{:S(2)}) %all-to-all-start.2) | async-done | bytes 524320 | tf_op jit(solution)/shard_map/all_to_all | solution.py:159
  111.9 2.8 %collective-permute-start.8 = (bf16[256,256]{1,0:T(8,128)(2,1)S(1)}, bf16[256,256]{1,0:T(8,128)(2,1)S(1)}, u32[]{:S(2)}, u32[]{:S(2)}) collective-permute-start(bf16[256,256]{1,0:T(8,128)(2,1)S(1)} %add_convert_fusion.1), channel_id=1, source_target_pairs={{0,0},{1,1},{2,32},{3,33},{4,64},{5,65},{6,96},{7,97},{8,128},{9,1... | collective-permute-start | bytes 393224 | tf_op jit(solution)/shard_map/ppermute | solution.py:31
  114.7 3.6 %collective-permute-start.9 = (bf16[256,256]{1,0:T(8,128)(2,1)S(1)}, bf16[256,256]{1,0:T(8,128)(2,1)S(1)}, u32[]{:S(2)}, u32[]{:S(2)}) collective-permute-start(bf16[256,256]{1,0:T(8,128)(2,1)S(1)} %add_convert_fusion), channel_id=1, source_target_pairs={{0,1},{1,0},{2,33},{3,32},{4,65},{5,64},{6,97},{7,96},{8,129},{9,1... | collective-permute-start | bytes 393224 | tf_op jit(solution)/shard_map/ppermute | solution.py:31
  118.3 0.8 collective-permute-done.10.t2
  119.1 0.7 copy-done.12
  119.8 7.3 %mirror.1 = (bf16[4,512,256]{2,1,0:T(8,128)(2,1)}, f32[512,256]{1,0:T(8,128)}) custom-call(s32[3]{0:T(128)} %pad_add_fusion.where, s32[8,8]{1,0:T(8,128)} %convert_element_type.21.bits, bf16[512,256]{1,0:T(8,128)(2,1)} %copy-done.2, bf16[512,256]{1,0:T(8,128)(2,1)} %copy-done.8, bf16[512,256]{1,0:T(8,128)(2,1)} %copy-done.12, bf16[512,256]{1,0:T(8,128)(2,1)} %copy-done.9, ...), custom_call_target="tpu_custom_call" | custom-call | flops 20000000000 | bytes 40000000 | tf_op jit(solution)/shard_map/mirror/pallas_call | solution.py:124
  127.1 13.4 %all-to-all-start.3 = ((bf16[4,512,256]{2,1,0:T(8,128)(2,1)}), bf16[4,512,256]{2,1,0:T(8,128)(2,1)S(1)}, u32[]{:S(2)}, u32[]{:S(2)}) async-start(bf16[4,512,256]{2,1,0:T(8,128)(2,1)} %get-tuple-element.34), calls=%async_computation.3 | async-start | bytes 2097152 | tf_op jit(solution)/shard_map/all_to_all | solution.py:159
  141.8 2.2 %base.1 = f32[512,256]{1,0:T(8,128)} custom-call(s32[1]{0:T(128)} %bitcast.co, f32[1]{0:T(128)} %copy.13.energy, bf16[256,256]{1,0:T(8,128)(2,1)} %copy-done.13, bf16[256,256]{1,0:T(8,128)(2,1)} %copy-done.14, f32[512,256]{1,0:T(8,128)} %coeffs_ref.1, f32[512,256]{1,0:T(8,128)} %diag_ref.1), custom_call_target="tpu_custom_call" | custom-call | flops 20000000000 | bytes 40000000 | tf_op jit(solution)/shard_map/base/pallas_call | solution.py:147
  144.1 11.7 %all-to-all-done.3 = bf16[4,512,256]{2,1,0:T(8,128)(2,1)S(1)} async-done(((bf16[4,512,256]{2,1,0:T(8,128)(2,1)}), bf16[4,512,256]{2,1,0:T(8,128)(2,1)S(1)}, u32[]{:S(2)}, u32[]{:S(2)}) %all-to-all-start.3) | async-done | bytes 1048608 | tf_op jit(solution)/shard_map/all_to_all | solution.py:159
  156.2 2.0 %maximum_divide_fusion = f32[512,256]{1,0:T(8,128)} fusion(f32[512,256]{1,0:T(8,128)S(1)} %copy-done.3, f32[512,256]{1,0:T(8,128)} %base.1, f32[512,256]{1,0:T(8,128)S(1)} %copy-done.4, f32[512,256]{1,0:T(8,128)S(1)} %convert_reduce_fusion, f32[]{:T(128)} %bitcast.6), kind=kLoop, calls=%fused_computation.3 | loop fusion | flops 786432 | bytes 2621444 | tf_op jit(solution)/shard_map/div | solution.py:219
  (54 shorter events, 5.0 us)
Async XLA Ops:
  0.0 9.8 %copy-start = (s32[64,24]{0,1:T(8,128)S(1)}, s32[64,24]{0,1:T(8,128)}, u32[]{:S(2)}) copy-start(s32[64,24]{0,1:T(8,128)} %param.10) | copy-start | bytes 18436
  1.1 102.2 %copy-start.2 = (bf16[512,256]{1,0:T(8,128)(2,1)}, bf16[512,256]{1,0:T(8,128)(2,1)S(1)}, u32[]{:S(2)}) copy-start(bf16[512,256]{1,0:T(8,128)(2,1)S(1)} %convert_element_type.22.t0) | copy-start | bytes 786436
  1.1 16.0 %collective-permute-start.1 = (bf16[256,256]{1,0:T(8,128)(2,1)S(1)}, bf16[256,256]{1,0:T(8,128)(2,1)S(1)}, u32[]{:S(2)}, u32[]{:S(2)}) collective-permute-start(bf16[256,256]{1,0:T(8,128)(2,1)S(1)} %get-tuple-element.38), channel_id=1, source_target_pairs={{0,1},{1,0},{2,33},{3,32},{4,65},{5,64},{6,97},{7,96},{8,129},{9,1... | collective-permute-start | bytes 393224 | tf_op jit(solution)/shard_map/ppermute | solution.py:31
  4.9 15.7 %collective-permute-start = (bf16[256,256]{1,0:T(8,128)(2,1)S(1)}, bf16[256,256]{1,0:T(8,128)(2,1)S(1)}, u32[]{:S(2)}, u32[]{:S(2)}) collective-permute-start(bf16[256,256]{1,0:T(8,128)(2,1)S(1)} %get-tuple-element.37), channel_id=1, source_target_pairs={{0,0},{1,1},{2,32},{3,33},{4,64},{5,65},{6,96},{7,97},{8,128},{9,1... | collective-permute-start | bytes 393224 | tf_op jit(solution)/shard_map/ppermute | solution.py:31
  20.7 29.0 %copy-start.5 = (bf16[256,512]{1,0:T(8,128)(2,1)}, bf16[256,512]{1,0:T(8,128)(2,1)S(1)}, u32[]{:S(2)}) copy-start(bf16[256,512]{1,0:T(8,128)(2,1)S(1)} %maximum_select_fusion.t0) | copy-start | bytes 786436
  20.7 44.5 %all-to-all-start = ((bf16[4,8,128,256]{3,2,1,0:T(8,128)(2,1)}), bf16[4,8,128,256]{3,2,1,0:T(8,128)(2,1)S(1)}, u32[]{:S(2)}, u32[]{:S(2)}) async-start(bf16[4,8,128,256]{3,2,1,0:T(8,128)(2,1)} %bitcast.7), calls=%async_computation | async-start | bytes 4194304 | tf_op jit(solution)/shard_map/all_to_all | solution.py:192
  24.3 31.1 %collective-permute-start.2 = (bf16[256,512]{1,0:T(8,128)(2,1)S(1)}, bf16[256,512]{1,0:T(8,128)(2,1)S(1)}, u32[]{:S(2)}, u32[]{:S(2)}) collective-permute-start(bf16[256,512]{1,0:T(8,128)(2,1)S(1)} %maximum_select_fusion.t0), channel_id=1, source_target_pairs={{0,128},{128,256},{256,384},{384,0},{1,129},{129,257},{257,385},{3... | collective-permute-start | bytes 786440 | tf_op jit(solution)/shard_map/ppermute | solution.py:17
  35.1 29.6 %collective-permute-start.3 = (bf16[256,512]{1,0:T(8,128)(2,1)S(1)}, bf16[256,512]{1,0:T(8,128)(2,1)S(1)}, u32[]{:S(2)}, u32[]{:S(2)}) collective-permute-start(bf16[256,512]{1,0:T(8,128)(2,1)S(1)} %maximum_select_fusion.t0), channel_id=1, source_target_pairs={{0,256},{128,384},{256,0},{384,128},{1,257},{129,385},{257,1},{385... | collective-permute-start | bytes 786440 | tf_op jit(solution)/shard_map/ppermute | solution.py:17
  49.7 15.5 %collective-permute-start.4 = (bf16[256,512]{1,0:T(8,128)(2,1)S(1)}, bf16[256,512]{1,0:T(8,128)(2,1)}, u32[]{:S(2)}, u32[]{:S(2)}) collective-permute-start(bf16[256,512]{1,0:T(8,128)(2,1)S(1)} %maximum_select_fusion.t0), channel_id=1, source_target_pairs={{0,384},{128,0},{256,128},{384,256},{1,385},{129,1},{257,129},{385... | collective-permute-start | bytes 786440 | tf_op jit(solution)/shard_map/ppermute | solution.py:17
  55.4 24.8 %copy-start.10 = (bf16[256,512]{1,0:T(8,128)(2,1)}, bf16[256,512]{1,0:T(8,128)(2,1)S(1)}, u32[]{:S(2)}) copy-start(bf16[256,512]{1,0:T(8,128)(2,1)S(1)} %collective-permute-done.2.t1) | copy-start | bytes 786436
  64.8 2.9 %copy-start.11 = (bf16[256,512]{1,0:T(8,128)(2,1)}, bf16[256,512]{1,0:T(8,128)(2,1)S(1)}, u32[]{:S(2)}) copy-start(bf16[256,512]{1,0:T(8,128)(2,1)S(1)} %collective-permute-done.3.t2) | copy-start | bytes 786436
  65.2 15.1 %copy-start.1 = (bf16[4,8,128,256]{3,2,1,0:T(8,128)(2,1)}, bf16[4,8,128,256]{3,2,1,0:T(8,128)(2,1)S(1)}, u32[]{:S(2)}) copy-start(bf16[4,8,128,256]{3,2,1,0:T(8,128)(2,1)S(1)} %all-to-all-done.h_ref.own_ref) | copy-start | bytes 6291460
  65.2 24.1 %collective-permute-start.5 = (bf16[4,8,128,256]{3,2,1,0:T(8,128)(2,1)S(1)}, bf16[4,8,128,256]{3,2,1,0:T(8,128)(2,1)}, u32[]{:S(2)}, u32[]{:S(2)}) collective-permute-start(bf16[4,8,128,256]{3,2,1,0:T(8,128)(2,1)S(1)} %all-to-all-done.h_ref.own_ref), channel_id=1, source_target_pairs={{0,1},{1,0},{2,3},{3,2},{4,5},{5,4},{6,7},{7,6},{8,9},{9,8},{10,11... | collective-permute-start | bytes 6291464 | tf_op jit(solution)/shard_map/ppermute | solution.py:21
  68.3 25.5 %collective-permute-start.6 = (bf16[512,256]{1,0:T(8,128)(2,1)S(1)}, bf16[512,256]{1,0:T(8,128)(2,1)S(1)}, u32[]{:S(2)}, u32[]{:S(2)}) collective-permute-start(bf16[512,256]{1,0:T(8,128)(2,1)S(1)} %convert_element_type.22.t0), channel_id=1, source_target_pairs={{0,128},{128,256},{256,384},{384,0},{1,129},{129,257},{257,385},{3... | collective-permute-start | bytes 786440 | tf_op jit(solution)/shard_map/ppermute | solution.py:17
  76.0 17.8 %collective-permute-start.7 = (bf16[512,256]{1,0:T(8,128)(2,1)S(1)}, bf16[512,256]{1,0:T(8,128)(2,1)S(1)}, u32[]{:S(2)}, u32[]{:S(2)}) collective-permute-start(bf16[512,256]{1,0:T(8,128)(2,1)S(1)} %convert_element_type.22.t0), channel_id=1, source_target_pairs={{0,384},{128,0},{256,128},{384,256},{1,385},{129,1},{257,129},{385... | collective-permute-start | bytes 786440 | tf_op jit(solution)/shard_map/ppermute | solution.py:17
  84.8 14.3 %all-to-all-start.1 = ((bf16[4,256,256]{2,1,0:T(8,128)(2,1)}), bf16[4,256,256]{2,1,0:T(8,128)(2,1)S(1)}, u32[]{:S(2)}, u32[]{:S(2)}) async-start(bf16[4,256,256]{2,1,0:T(8,128)(2,1)} %get-tuple-element.22), calls=%async_computation.1 | async-start | bytes 1048576 | tf_op jit(solution)/shard_map/all_to_all | solution.py:159
  93.8 18.1 %copy-start.6 = (f32[256,256]{1,0:T(8,128)S(1)}, f32[256,256]{1,0:T(8,128)}, u32[]{:S(2)}) copy-start(f32[256,256]{1,0:T(8,128)} %get-tuple-element.21) | copy-start | bytes 786436
  93.8 20.9 %copy-start.7 = (f32[256,256]{1,0:T(8,128)S(1)}, f32[256,256]{1,0:T(8,128)}, u32[]{:S(2)}) copy-start(f32[256,256]{1,0:T(8,128)} %get-tuple-element.28) | copy-start | bytes 786436
  93.8 25.3 %copy-start.8 = (bf16[512,256]{1,0:T(8,128)(2,1)}, bf16[512,256]{1,0:T(8,128)(2,1)S(1)}, u32[]{:S(2)}) copy-start(bf16[512,256]{1,0:T(8,128)(2,1)S(1)} %collective-permute-done.6.t1) | copy-start | bytes 786436
  93.8 25.3 %copy-start.9 = (bf16[512,256]{1,0:T(8,128)(2,1)}, bf16[512,256]{1,0:T(8,128)(2,1)S(1)}, u32[]{:S(2)}) copy-start(bf16[512,256]{1,0:T(8,128)(2,1)S(1)} %collective-permute-done.7.t3) | copy-start | bytes 786436
  99.1 12.4 %all-to-all-start.2 = ((bf16[4,256,256]{2,1,0:T(8,128)(2,1)}), bf16[4,256,256]{2,1,0:T(8,128)(2,1)S(1)}, u32[]{:S(2)}, u32[]{:S(2)}) async-start(bf16[4,256,256]{2,1,0:T(8,128)(2,1)} %get-tuple-element.29), calls=%async_computation.2 | async-start | bytes 1048576 | tf_op jit(solution)/shard_map/all_to_all | solution.py:159
  103.3 15.9 %collective-permute-start.10 = (bf16[512,256]{1,0:T(8,128)(2,1)S(1)}, bf16[512,256]{1,0:T(8,128)(2,1)S(1)}, u32[]{:S(2)}, u32[]{:S(2)}) collective-permute-start(bf16[512,256]{1,0:T(8,128)(2,1)S(1)} %convert_element_type.22.t0), channel_id=1, source_target_pairs={{0,256},{128,384},{256,0},{384,128},{1,257},{129,385},{257,1},{385... | collective-permute-start | bytes 786440 | tf_op jit(solution)/shard_map/ppermute | solution.py:17
  111.9 28.7 %collective-permute-start.8 = (bf16[256,256]{1,0:T(8,128)(2,1)S(1)}, bf16[256,256]{1,0:T(8,128)(2,1)S(1)}, u32[]{:S(2)}, u32[]{:S(2)}) collective-permute-start(bf16[256,256]{1,0:T(8,128)(2,1)S(1)} %add_convert_fusion.1), channel_id=1, source_target_pairs={{0,0},{1,1},{2,32},{3,33},{4,64},{5,65},{6,96},{7,97},{8,128},{9,1... | collective-permute-start | bytes 393224 | tf_op jit(solution)/shard_map/ppermute | solution.py:31
  114.7 25.9 %collective-permute-start.9 = (bf16[256,256]{1,0:T(8,128)(2,1)S(1)}, bf16[256,256]{1,0:T(8,128)(2,1)S(1)}, u32[]{:S(2)}, u32[]{:S(2)}) collective-permute-start(bf16[256,256]{1,0:T(8,128)(2,1)S(1)} %add_convert_fusion), channel_id=1, source_target_pairs={{0,1},{1,0},{2,33},{3,32},{4,65},{5,64},{6,97},{7,96},{8,129},{9,1... | collective-permute-start | bytes 393224 | tf_op jit(solution)/shard_map/ppermute | solution.py:31
  119.1 0.7 copy-start.12
  127.1 28.7 %all-to-all-start.3 = ((bf16[4,512,256]{2,1,0:T(8,128)(2,1)}), bf16[4,512,256]{2,1,0:T(8,128)(2,1)S(1)}, u32[]{:S(2)}, u32[]{:S(2)}) async-start(bf16[4,512,256]{2,1,0:T(8,128)(2,1)} %get-tuple-element.34), calls=%async_computation.3 | async-start | bytes 2097152 | tf_op jit(solution)/shard_map/all_to_all | solution.py:159
  140.6 15.6 %copy-start.3 = (f32[512,256]{1,0:T(8,128)S(1)}, f32[512,256]{1,0:T(8,128)}, u32[]{:S(2)}) copy-start(f32[512,256]{1,0:T(8,128)} %diag_ref.1) | copy-start | bytes 1572868
  140.6 15.6 %copy-start.4 = (f32[512,256]{1,0:T(8,128)S(1)}, f32[512,256]{1,0:T(8,128)}, u32[]{:S(2)}) copy-start(f32[512,256]{1,0:T(8,128)} %get-tuple-element.33) | copy-start | bytes 1572868
  140.6 0.6 copy-start.13
  141.2 0.6 copy-start.14

commit v7 on v6

--- a/solution.py
+++ b/solution.py
@@ -9,6 +9,8 @@
 ROW = ("zl", "x")
 COL = ("zh", "y", "co")
 W = 128
+STEP = 24_000_000_000
+LATE = 2_000_000_000
 VMEM_LIMIT = 56 * 1024 * 1024
 PARAMS = pltpu.CompilerParams(vmem_limit_bytes=VMEM_LIMIT)
 
@@ -155,6 +157,21 @@
     )(co, energy, here, there, coeffs, diag_energy)
 
 
+def copy_kernel(in_ref, out_ref):
+    out_ref[...] = in_ref[...]
+
+
+def step_kernel(value, flops):
+    return pl.pallas_call(
+        copy_kernel,
+        out_shape=jax.ShapeDtypeStruct(value.shape, value.dtype),
+        in_specs=[pl.BlockSpec(memory_space=pltpu.VMEM)],
+        out_specs=pl.BlockSpec(memory_space=pltpu.VMEM),
+        cost_estimate=pl.CostEstimate(flops=flops, bytes_accessed=1000, transcendentals=0),
+        name="step",
+    )(value)
+
+
 def exchanged(parts):
     return lax.all_to_all(parts, "x", 0, 0, tiled=True)
 
@@ -177,10 +194,6 @@
     tile = jnp.where(
         co == 0, jnp.concatenate([here, there], axis=1), jnp.concatenate([there, here], axis=1)
     )
-    direct_tiles = [tile] + [shifted(tile, "zl", d) for d in (1, 2, 3)]
-    later = lax.optimization_barrier((half, *direct_tiles[1:]))[0]
-    mirror_tiles = [half] + [shifted(later, "zl", d) for d in (1, 2, 3)]
-
     filled = jnp.arange(slots, dtype=jnp.int32)[None, :] < counts[:, None]
     begin = row_id * 4 + co * 2
     blk = lax.dynamic_slice_in_dim(pattern, begin, 2, 0)
@@ -188,14 +201,17 @@
     owner = blk // 4
     at = (owner % 4) * 8 + (owner // 4) * 2 + (blk % 4) // 2
     packed = pack(jnp.where(live, at, -1), co[None], h_blocks)
-    packed = lax.optimization_barrier((packed, tile))[0]
+    packed, tile = lax.optimization_barrier((packed, tile))
+    direct_tiles = [tile] + [shifted(tile, "zl", d) for d in (1, 2, 3)]
+    later = lax.optimization_barrier((half, *direct_tiles[1:]))[0]
+    mirror_tiles = [half] + [shifted(later, "zl", d) for d in (1, 2, 3)]
     own = lax.all_to_all(packed.reshape(4, 8, W, 2 * W), "x", 0, 0, tiled=True)
-    other = swap_cores(lax.optimization_barrier((own, *direct_tiles[1:]))[0])
-
     names = lax.dynamic_slice_in_dim(pattern, zl * 16, 16, 0).reshape(8, 1, 2 * slots)
     i = jnp.arange(8, dtype=jnp.int32)
     odd = (8 * (i // 2) + 2 * x + i % 2) * 2 + 1
     bits = jnp.any(names == odd[None, :, None], axis=2).astype(jnp.int32)
+    bits = step_kernel(lax.optimization_barrier((bits, *direct_tiles[1:]))[0], STEP)
+    other = swap_cores(lax.optimization_barrier((own, bits))[0])
     here_first = jnp.stack([zl, x, co])
     there_first = jnp.stack([zl, x, 1 - co])
 
@@ -203,14 +219,14 @@
     got_upper = exchanged(upper)
     direct_tiles[3], upper = lax.optimization_barrier((direct_tiles[3], upper))
     lower, kept_lower = partial_sums(direct_kernel, "direct", (256, 256), there_first, bits, direct_tiles, other)
-    lower, got_upper, mirror_tiles[1], mirror_tiles[3] = lax.optimization_barrier(
-        (lower, got_upper, mirror_tiles[1], mirror_tiles[3])
-    )
+    lower, got_upper = lax.optimization_barrier((lower, got_upper))
     got_lower = exchanged(lower)
     upper = summed(got_upper, kept_upper, x).astype(jnp.bfloat16)
+    bits, _, *mirror_tiles = lax.optimization_barrier((bits, lower, *mirror_tiles))
+    bits = step_kernel(bits, LATE)
+    got_lower, upper, bits = lax.optimization_barrier((got_lower, upper, bits))
     lower = summed(got_lower, kept_lower, x).astype(jnp.bfloat16)
     here, there = turned(upper, 0), turned(lower, 1)
-    mirror_tiles[3], lower = lax.optimization_barrier((mirror_tiles[3], lower))
     mirror, kept = partial_sums(
         mirror_kernel, "mirror", (512, 256), here_first, bits, mirror_tiles, own, other
     )

time: 159 us -> 168 us (1.057)
  the two profiles are of different devices: /device:TPU:24 before, /device:TPU:65 now
where the time goes in v7:
time: 168 us; the launch traced here: 167 us
  starting transfers between devices  77.5 us (46%)
  waiting for transfers between devices  53.3 us (32%)
  Pallas kernels  25.6 us (15%)
  other arithmetic  6.72 us (4%)
  local copies, waits for them, and re-layouts  2.44 us (1%)
    ppermute x4, starting transfers between devices, turned(): return lax.ppermute(value, AXES, pairs)  30.6 us
    all_to_all x3, waiting for transfers between devices, exchanged(): return lax.all_to_all(parts, 'x', 0, 0, tiled=True)  20.7 us
    all_to_all x1, waiting for transfers between devices, on_device(): own = lax.all_to_all(packed.reshape(4, 8, W, 2 * W), 'x', 0, 0, tiled=True)  19.2 us
    ppermute x6, starting transfers between devices, shifted(): return lax.ppermute(value, axis, [(i, (i + step) % 4) for i in range(4)])  18.5 us
    pallas_call x3, Pallas kernels, partial_sums(): pl.pallas_call(kernel, out_shape=(jax.ShapeDtypeStruct((4, *shape), jnp.b...  16.4 us
    all_to_all x3, starting transfers between devices, exchanged(): return lax.all_to_all(parts, 'x', 0, 0, tiled=True)  13.3 us
    all_to_all x1, starting transfers between devices, on_device(): own = lax.all_to_all(packed.reshape(4, 8, W, 2 * W), 'x', 0, 0, tiled=True)  10.7 us
    ppermute x4, waiting for transfers between devices, turned(): return lax.ppermute(value, AXES, pairs)  9.09 us
  transfers between devices with their start and end apart: 15, of which 7 were waited for; matrix products, arithmetic and copies ran while one was open for 3% of the time, Pallas kernels for 15%

profile of v7, /device:TPU:65, one launch (start us, length us, event | category | flops | bytes accessed | tf_op | source)
XLA Modules:
  0.0 166.6 jit_solution(9683021732856411688)
XLA Ops:
  0.0 1.1 convert_element_type.22.t0
  1.1 13.3 %collective-permute-start.1 = (bf16[256,256]{1,0:T(8,128)(2,1)S(1)}, bf16[256,256]{1,0:T(8,128)(2,1)S(1)}, u32[]{:S(2)}, u32[]{:S(2)}) collective-permute-start(bf16[256,256]{1,0:T(8,128)(2,1)S(1)} %get-tuple-element.50), channel_id=1, source_target_pairs={{0,1},{1,0},{2,33},{3,32},{4,65},{5,64},{6,97},{7,96},{8,129},{9,1... | collective-permute-start | bytes 393224 | tf_op jit(solution)/shard_map/ppermute | solution.py:33
  14.4 1.9 %collective-permute-start = (bf16[256,256]{1,0:T(8,128)(2,1)S(1)}, bf16[256,256]{1,0:T(8,128)(2,1)S(1)}, u32[]{:S(2)}, u32[]{:S(2)}) collective-permute-start(bf16[256,256]{1,0:T(8,128)(2,1)S(1)} %get-tuple-element.49), channel_id=1, source_target_pairs={{0,0},{1,1},{2,32},{3,33},{4,64},{5,65},{6,96},{7,97},{8,128},{9,1... | collective-permute-start | bytes 393224 | tf_op jit(solution)/shard_map/ppermute | solution.py:33
  16.5 0.7 dynamic-slice
  17.9 4.4 %pack.1 = bf16[32,128,256]{2,1,0:T(8,128)(2,1)} custom-call(s32[2,24]{1,0:T(2,128)} %compare_select_fusion.pos, s32[1]{0:T(128)} %bitcast.co, bf16[4,24,128,128]{3,2,1,0:T(8,128)(2,1)} %h_ref.1), custom_call_target="tpu_custom_call" | custom-call | tf_op jit(solution)/shard_map/pack/pallas_call | solution.py:54
  22.4 9.1 %collective-permute-done = bf16[256,256]{1,0:T(8,128)(2,1)S(1)} collective-permute-done((bf16[256,256]{1,0:T(8,128)(2,1)S(1)}, bf16[256,256]{1,0:T(8,128)(2,1)S(1)}, u32[]{:S(2)}, u32[]{:S(2)}) %collective-permute-start) | collective-permute-done | bytes 131104 | tf_op jit(solution)/shard_map/ppermute | solution.py:33
  31.6 1.9 %collective-permute-start.2 = (bf16[256,512]{1,0:T(8,128)(2,1)S(1)}, bf16[256,512]{1,0:T(8,128)(2,1)S(1)}, u32[]{:S(2)}, u32[]{:S(2)}) collective-permute-start(bf16[256,512]{1,0:T(8,128)(2,1)S(1)} %maximum_select_fusion.t0), channel_id=1, source_target_pairs={{0,128},{128,256},{256,384},{384,0},{1,129},{129,257},{257,385},{3... | collective-permute-start | bytes 786440 | tf_op jit(solution)/shard_map/ppermute | solution.py:19
  33.5 1.9 %collective-permute-start.3 = (bf16[256,512]{1,0:T(8,128)(2,1)S(1)}, bf16[256,512]{1,0:T(8,128)(2,1)S(1)}, u32[]{:S(2)}, u32[]{:S(2)}) collective-permute-start(bf16[256,512]{1,0:T(8,128)(2,1)S(1)} %maximum_select_fusion.t0), channel_id=1, source_target_pairs={{0,256},{128,384},{256,0},{384,128},{1,257},{129,385},{257,1},{385... | collective-permute-start | bytes 786440 | tf_op jit(solution)/shard_map/ppermute | solution.py:19
  35.4 3.4 %collective-permute-start.4 = (bf16[256,512]{1,0:T(8,128)(2,1)S(1)}, bf16[256,512]{1,0:T(8,128)(2,1)S(1)}, u32[]{:S(2)}, u32[]{:S(2)}) collective-permute-start(bf16[256,512]{1,0:T(8,128)(2,1)S(1)} %maximum_select_fusion.t0), channel_id=1, source_target_pairs={{0,384},{128,0},{256,128},{384,256},{1,385},{129,1},{257,129},{385... | collective-permute-start | bytes 786440 | tf_op jit(solution)/shard_map/ppermute | solution.py:19
  40.5 10.7 %all-to-all-start = ((bf16[4,8,128,256]{3,2,1,0:T(8,128)(2,1)}), bf16[4,8,128,256]{3,2,1,0:T(8,128)(2,1)S(1)}, u32[]{:S(2)}, u32[]{:S(2)}) async-start(bf16[4,8,128,256]{3,2,1,0:T(8,128)(2,1)} %bitcast.7), calls=%async_computation | async-start | bytes 4194304 | tf_op jit(solution)/shard_map/all_to_all | solution.py:208
  51.2 0.8 collective-permute-done.2.t1
  52.0 3.5 %collective-permute-done.4.t3 = bf16[256,512]{1,0:T(8,128)(2,1)S(1)} collective-permute-done((bf16[256,512]{1,0:T(8,128)(2,1)S(1)}, bf16[256,512]{1,0:T(8,128)(2,1)S(1)}, u32[]{:S(2)}, u32[]{:S(2)}) %collective-permute-start.4) | collective-permute-done | bytes 262176 | tf_op jit(solution)/shard_map/ppermute | solution.py:19
  55.5 1.3 step.2.bits.in_ref
  56.8 19.2 %all-to-all-done.h_ref.own_ref = bf16[4,8,128,256]{3,2,1,0:T(8,128)(2,1)S(1)} async-done(((bf16[4,8,128,256]{3,2,1,0:T(8,128)(2,1)}), bf16[4,8,128,256]{3,2,1,0:T(8,128)(2,1)S(1)}, u32[]{:S(2)}, u32[]{:S(2)}) %all-to-all-start) | async-done | bytes 2097184 | tf_op jit(solution)/shard_map/all_to_all | solution.py:208
  76.0 4.4 %collective-permute-start.5 = (bf16[4,8,128,256]{3,2,1,0:T(8,128)(2,1)S(1)}, bf16[4,8,128,256]{3,2,1,0:T(8,128)(2,1)}, u32[]{:S(2)}, u32[]{:S(2)}) collective-permute-start(bf16[4,8,128,256]{3,2,1,0:T(8,128)(2,1)S(1)} %all-to-all-done.h_ref.own_ref), channel_id=1, source_target_pairs={{0,1},{1,0},{2,3},{3,2},{4,5},{5,4},{6,7},{7,6},{8,9},{9,8},{10,11... | collective-permute-start | bytes 6291464 | tf_op jit(solution)/shard_map/ppermute | solution.py:23
  81.6 3.1 %collective-permute-start.6 = (bf16[512,256]{1,0:T(8,128)(2,1)S(1)}, bf16[512,256]{1,0:T(8,128)(2,1)S(1)}, u32[]{:S(2)}, u32[]{:S(2)}) collective-permute-start(bf16[512,256]{1,0:T(8,128)(2,1)S(1)} %convert_element_type.22.t0), channel_id=1, source_target_pairs={{0,128},{128,256},{256,384},{384,0},{1,129},{129,257},{257,385},{3... | collective-permute-start | bytes 786440 | tf_op jit(solution)/shard_map/ppermute | solution.py:19
  84.7 4.0 %collective-permute-start.7 = (bf16[512,256]{1,0:T(8,128)(2,1)S(1)}, bf16[512,256]{1,0:T(8,128)(2,1)S(1)}, u32[]{:S(2)}, u32[]{:S(2)}) collective-permute-start(bf16[512,256]{1,0:T(8,128)(2,1)S(1)} %convert_element_type.22.t0), channel_id=1, source_target_pairs={{0,256},{128,384},{256,0},{384,128},{1,257},{129,385},{257,1},{385... | collective-permute-start | bytes 786440 | tf_op jit(solution)/shard_map/ppermute | solution.py:19
  88.7 4.3 %collective-permute-start.8 = (bf16[512,256]{1,0:T(8,128)(2,1)S(1)}, bf16[512,256]{1,0:T(8,128)(2,1)}, u32[]{:S(2)}, u32[]{:S(2)}) collective-permute-start(bf16[512,256]{1,0:T(8,128)(2,1)S(1)} %convert_element_type.22.t0), channel_id=1, source_target_pairs={{0,384},{128,0},{256,128},{384,256},{1,385},{129,1},{257,129},{385... | collective-permute-start | bytes 786440 | tf_op jit(solution)/shard_map/ppermute | solution.py:19
  93.0 4.5 %direct.2 = (bf16[4,256,256]{2,1,0:T(8,128)(2,1)}, f32[256,256]{1,0:T(8,128)}) custom-call(s32[3]{0:T(128)} %pad_add_fusion.2.where, s32[8,8]{1,0:T(8,128)} %step.2.bits.in_ref, bf16[256,512]{1,0:T(8,128)(2,1)} %copy-done.5, bf16[256,512]{1,0:T(8,128)(2,1)} %copy-done.8, bf16[256,512]{1,0:T(8,128)(2,1)} %copy-done.10, bf16[256,512]{1,0:T(8,128)(2,1)} %copy-done.12, ...), custom_call_target="tpu_custom_call" | custom-call | flops 20000000000 | bytes 40000000 | tf_op jit(solution)/shard_map/direct/pallas_call | solution.py:126
  97.5 3.5 %all-to-all-start.1 = ((bf16[4,256,256]{2,1,0:T(8,128)(2,1)}), bf16[4,256,256]{2,1,0:T(8,128)(2,1)S(1)}, u32[]{:S(2)}, u32[]{:S(2)}) async-start(bf16[4,256,256]{2,1,0:T(8,128)(2,1)} %get-tuple-element.30), calls=%async_computation.1 | async-start | bytes 1048576 | tf_op jit(solution)/shard_map/all_to_all | solution.py:176
  101.0 4.6 %direct.3 = (bf16[4,256,256]{2,1,0:T(8,128)(2,1)}, f32[256,256]{1,0:T(8,128)}) custom-call(s32[3]{0:T(128)} %pad_add_fusion.where, s32[8,8]{1,0:T(8,128)} %step.2.bits.in_ref, bf16[256,512]{1,0:T(8,128)(2,1)} %copy-done.5, bf16[256,512]{1,0:T(8,128)(2,1)} %copy-done.8, bf16[256,512]{1,0:T(8,128)(2,1)} %copy-done.10, bf16[256,512]{1,0:T(8,128)(2,1)} %copy-done.12, ...), custom_call_target="tpu_custom_call" | custom-call | flops 20000000000 | bytes 40000000 | tf_op jit(solution)/shard_map/direct/pallas_call | solution.py:126
  105.5 4.1 %all-to-all-done.1 = bf16[4,256,256]{2,1,0:T(8,128)(2,1)S(1)} async-done(((bf16[4,256,256]{2,1,0:T(8,128)(2,1)}), bf16[4,256,256]{2,1,0:T(8,128)(2,1)S(1)}, u32[]{:S(2)}, u32[]{:S(2)}) %all-to-all-start.1) | async-done | bytes 524320 | tf_op jit(solution)/shard_map/all_to_all | solution.py:176
  109.6 3.5 %all-to-all-start.2 = ((bf16[4,256,256]{2,1,0:T(8,128)(2,1)}), bf16[4,256,256]{2,1,0:T(8,128)(2,1)S(1)}, u32[]{:S(2)}, u32[]{:S(2)}) async-start(bf16[4,256,256]{2,1,0:T(8,128)(2,1)} %get-tuple-element.34), calls=%async_computation.2 | async-start | bytes 1048576 | tf_op jit(solution)/shard_map/all_to_all | solution.py:176
  113.1 1.4 step.3.bits
  114.8 5.7 %all-to-all-done.2 = bf16[4,256,256]{2,1,0:T(8,128)(2,1)S(1)} async-done(((bf16[4,256,256]{2,1,0:T(8,128)(2,1)}), bf16[4,256,256]{2,1,0:T(8,128)(2,1)S(1)}, u32[]{:S(2)}, u32[]{:S(2)}) %all-to-all-start.2) | async-done | bytes 524320 | tf_op jit(solution)/shard_map/all_to_all | solution.py:176
  120.5 5.2 %collective-permute-start.9 = (bf16[256,256]{1,0:T(8,128)(2,1)S(1)}, bf16[256,256]{1,0:T(8,128)(2,1)S(1)}, u32[]{:S(2)}, u32[]{:S(2)}) collective-permute-start(bf16[256,256]{1,0:T(8,128)(2,1)S(1)} %add_convert_fusion.1), channel_id=1, source_target_pairs={{0,0},{1,1},{2,32},{3,33},{4,64},{5,65},{6,96},{7,97},{8,128},{9,1... | collective-permute-start | bytes 393224 | tf_op jit(solution)/shard_map/ppermute | solution.py:33
  125.9 10.2 %collective-permute-start.10 = (bf16[256,256]{1,0:T(8,128)(2,1)S(1)}, bf16[256,256]{1,0:T(8,128)(2,1)S(1)}, u32[]{:S(2)}, u32[]{:S(2)}) collective-permute-start(bf16[256,256]{1,0:T(8,128)(2,1)S(1)} %add_convert_fusion), channel_id=1, source_target_pairs={{0,1},{1,0},{2,33},{3,32},{4,65},{5,64},{6,97},{7,96},{8,129},{9,1... | collective-permute-start | bytes 393224 | tf_op jit(solution)/shard_map/ppermute | solution.py:33
  136.1 7.3 %mirror.1 = (bf16[4,512,256]{2,1,0:T(8,128)(2,1)}, f32[512,256]{1,0:T(8,128)}) custom-call(s32[3]{0:T(128)} %pad_add_fusion.2.where, s32[8,8]{1,0:T(8,128)} %step.3.bits, bf16[512,256]{1,0:T(8,128)(2,1)} %copy-done.2, bf16[512,256]{1,0:T(8,128)(2,1)} %copy-done.9, bf16[512,256]{1,0:T(8,128)(2,1)} %copy-done.11, bf16[512,256]{1,0:T(8,128)(2,1)} %collective-permute-done.8.t3, ...), custom_call_target="tpu_custom_call" | custom-call | flops 20000000000 | bytes 40000000 | tf_op jit(solution)/shard_map/mirror/pallas_call | solution.py:126
  143.4 6.4 %all-to-all-start.3 = ((bf16[4,512,256]{2,1,0:T(8,128)(2,1)}), bf16[4,512,256]{2,1,0:T(8,128)(2,1)S(1)}, u32[]{:S(2)}, u32[]{:S(2)}) async-start(bf16[4,512,256]{2,1,0:T(8,128)(2,1)} %get-tuple-element.48), calls=%async_computation.3 | async-start | bytes 2097152 | tf_op jit(solution)/shard_map/all_to_all | solution.py:176
  151.1 2.2 %base.1 = f32[512,256]{1,0:T(8,128)} custom-call(s32[1]{0:T(128)} %bitcast.co, f32[1]{0:T(128)} %copy.13.energy, bf16[256,256]{1,0:T(8,128)(2,1)} %copy-done.13, bf16[256,256]{1,0:T(8,128)(2,1)} %copy-done.14, f32[512,256]{1,0:T(8,128)} %coeffs_ref.1, f32[512,256]{1,0:T(8,128)} %diag_ref.1), custom_call_target="tpu_custom_call" | custom-call | flops 20000000000 | bytes 40000000 | tf_op jit(solution)/shard_map/base/pallas_call | solution.py:149
  153.3 10.9 %all-to-all-done.3 = bf16[4,512,256]{2,1,0:T(8,128)(2,1)S(1)} async-done(((bf16[4,512,256]{2,1,0:T(8,128)(2,1)}), bf16[4,512,256]{2,1,0:T(8,128)(2,1)S(1)}, u32[]{:S(2)}, u32[]{:S(2)}) %all-to-all-start.3) | async-done | bytes 1048608 | tf_op jit(solution)/shard_map/all_to_all | solution.py:176
  164.6 2.0 %maximum_divide_fusion = f32[512,256]{1,0:T(8,128)} fusion(f32[512,256]{1,0:T(8,128)S(1)} %copy-done.3, f32[512,256]{1,0:T(8,128)} %base.1, f32[512,256]{1,0:T(8,128)S(1)} %copy-done.4, f32[512,256]{1,0:T(8,128)S(1)} %convert_reduce_fusion, f32[]{:T(128)} %bitcast.6), kind=kLoop, calls=%fused_computation.3 | loop fusion | flops 786432 | bytes 2621444 | tf_op jit(solution)/shard_map/div | solution.py:235
  (57 shorter events, 5.4 us)
Async XLA Ops:
  0.0 16.4 %copy-start = (s32[64,24]{0,1:T(8,128)S(1)}, s32[64,24]{0,1:T(8,128)}, u32[]{:S(2)}) copy-start(s32[64,24]{0,1:T(8,128)} %param.10) | copy-start | bytes 18436
  1.1 87.6 %copy-start.2 = (bf16[512,256]{1,0:T(8,128)(2,1)}, bf16[512,256]{1,0:T(8,128)(2,1)S(1)}, u32[]{:S(2)}) copy-start(bf16[512,256]{1,0:T(8,128)(2,1)S(1)} %convert_element_type.22.t0) | copy-start | bytes 786436
  1.1 21.2 %collective-permute-start.1 = (bf16[256,256]{1,0:T(8,128)(2,1)S(1)}, bf16[256,256]{1,0:T(8,128)(2,1)S(1)}, u32[]{:S(2)}, u32[]{:S(2)}) collective-permute-start(bf16[256,256]{1,0:T(8,128)(2,1)S(1)} %get-tuple-element.50), channel_id=1, source_target_pairs={{0,1},{1,0},{2,33},{3,32},{4,65},{5,64},{6,97},{7,96},{8,129},{9,1... | collective-permute-start | bytes 393224 | tf_op jit(solution)/shard_map/ppermute | solution.py:33
  14.4 17.0 %collective-permute-start = (bf16[256,256]{1,0:T(8,128)(2,1)S(1)}, bf16[256,256]{1,0:T(8,128)(2,1)S(1)}, u32[]{:S(2)}, u32[]{:S(2)}) collective-permute-start(bf16[256,256]{1,0:T(8,128)(2,1)S(1)} %get-tuple-element.49), channel_id=1, source_target_pairs={{0,0},{1,1},{2,32},{3,33},{4,64},{5,65},{6,96},{7,97},{8,128},{9,1... | collective-permute-start | bytes 393224 | tf_op jit(solution)/shard_map/ppermute | solution.py:33
  31.6 8.9 %copy-start.5 = (bf16[256,512]{1,0:T(8,128)(2,1)}, bf16[256,512]{1,0:T(8,128)(2,1)S(1)}, u32[]{:S(2)}) copy-start(bf16[256,512]{1,0:T(8,128)(2,1)S(1)} %maximum_select_fusion.t0) | copy-start | bytes 786436
  31.6 20.4 %collective-permute-start.2 = (bf16[256,512]{1,0:T(8,128)(2,1)S(1)}, bf16[256,512]{1,0:T(8,128)(2,1)S(1)}, u32[]{:S(2)}, u32[]{:S(2)}) collective-permute-start(bf16[256,512]{1,0:T(8,128)(2,1)S(1)} %maximum_select_fusion.t0), channel_id=1, source_target_pairs={{0,128},{128,256},{256,384},{384,0},{1,129},{129,257},{257,385},{3... | collective-permute-start | bytes 786440 | tf_op jit(solution)/shard_map/ppermute | solution.py:19
  33.5 18.5 %collective-permute-start.3 = (bf16[256,512]{1,0:T(8,128)(2,1)S(1)}, bf16[256,512]{1,0:T(8,128)(2,1)S(1)}, u32[]{:S(2)}, u32[]{:S(2)}) collective-permute-start(bf16[256,512]{1,0:T(8,128)(2,1)S(1)} %maximum_select_fusion.t0), channel_id=1, source_target_pairs={{0,256},{128,384},{256,0},{384,128},{1,257},{129,385},{257,1},{385... | collective-permute-start | bytes 786440 | tf_op jit(solution)/shard_map/ppermute | solution.py:19
  35.4 20.1 %collective-permute-start.4 = (bf16[256,512]{1,0:T(8,128)(2,1)S(1)}, bf16[256,512]{1,0:T(8,128)(2,1)S(1)}, u32[]{:S(2)}, u32[]{:S(2)}) collective-permute-start(bf16[256,512]{1,0:T(8,128)(2,1)S(1)} %maximum_select_fusion.t0), channel_id=1, source_target_pairs={{0,384},{128,0},{256,128},{384,256},{1,385},{129,1},{257,129},{385... | collective-permute-start | bytes 786440 | tf_op jit(solution)/shard_map/ppermute | solution.py:19
  40.5 35.4 %all-to-all-start = ((bf16[4,8,128,256]{3,2,1,0:T(8,128)(2,1)}), bf16[4,8,128,256]{3,2,1,0:T(8,128)(2,1)S(1)}, u32[]{:S(2)}, u32[]{:S(2)}) async-start(bf16[4,8,128,256]{3,2,1,0:T(8,128)(2,1)} %bitcast.7), calls=%async_computation | async-start | bytes 4194304 | tf_op jit(solution)/shard_map/all_to_all | solution.py:208
  52.0 4.8 %copy-start.8 = (bf16[256,512]{1,0:T(8,128)(2,1)}, bf16[256,512]{1,0:T(8,128)(2,1)S(1)}, u32[]{:S(2)}) copy-start(bf16[256,512]{1,0:T(8,128)(2,1)S(1)} %collective-permute-done.2.t1) | copy-start | bytes 786436
  52.0 4.8 %copy-start.10 = (bf16[256,512]{1,0:T(8,128)(2,1)}, bf16[256,512]{1,0:T(8,128)(2,1)S(1)}, u32[]{:S(2)}) copy-start(bf16[256,512]{1,0:T(8,128)(2,1)S(1)} %collective-permute-done.3.t2) | copy-start | bytes 786436
  55.5 1.3 copy-start.12
  76.0 17.0 %copy-start.1 = (bf16[4,8,128,256]{3,2,1,0:T(8,128)(2,1)}, bf16[4,8,128,256]{3,2,1,0:T(8,128)(2,1)S(1)}, u32[]{:S(2)}) copy-start(bf16[4,8,128,256]{3,2,1,0:T(8,128)(2,1)S(1)} %all-to-all-done.h_ref.own_ref) | copy-start | bytes 6291460
  76.0 25.0 %collective-permute-start.5 = (bf16[4,8,128,256]{3,2,1,0:T(8,128)(2,1)S(1)}, bf16[4,8,128,256]{3,2,1,0:T(8,128)(2,1)}, u32[]{:S(2)}, u32[]{:S(2)}) collective-permute-start(bf16[4,8,128,256]{3,2,1,0:T(8,128)(2,1)S(1)} %all-to-all-done.h_ref.own_ref), channel_id=1, source_target_pairs={{0,1},{1,0},{2,3},{3,2},{4,5},{5,4},{6,7},{7,6},{8,9},{9,8},{10,11... | collective-permute-start | bytes 6291464 | tf_op jit(solution)/shard_map/ppermute | solution.py:23
  81.6 31.5 %collective-permute-start.6 = (bf16[512,256]{1,0:T(8,128)(2,1)S(1)}, bf16[512,256]{1,0:T(8,128)(2,1)S(1)}, u32[]{:S(2)}, u32[]{:S(2)}) collective-permute-start(bf16[512,256]{1,0:T(8,128)(2,1)S(1)} %convert_element_type.22.t0), channel_id=1, source_target_pairs={{0,128},{128,256},{256,384},{384,0},{1,129},{129,257},{257,385},{3... | collective-permute-start | bytes 786440 | tf_op jit(solution)/shard_map/ppermute | solution.py:19
  84.7 28.4 %collective-permute-start.7 = (bf16[512,256]{1,0:T(8,128)(2,1)S(1)}, bf16[512,256]{1,0:T(8,128)(2,1)S(1)}, u32[]{:S(2)}, u32[]{:S(2)}) collective-permute-start(bf16[512,256]{1,0:T(8,128)(2,1)S(1)} %convert_element_type.22.t0), channel_id=1, source_target_pairs={{0,256},{128,384},{256,0},{384,128},{1,257},{129,385},{257,1},{385... | collective-permute-start | bytes 786440 | tf_op jit(solution)/shard_map/ppermute | solution.py:19
  88.7 24.4 %collective-permute-start.8 = (bf16[512,256]{1,0:T(8,128)(2,1)S(1)}, bf16[512,256]{1,0:T(8,128)(2,1)}, u32[]{:S(2)}, u32[]{:S(2)}) collective-permute-start(bf16[512,256]{1,0:T(8,128)(2,1)S(1)} %convert_element_type.22.t0), channel_id=1, source_target_pairs={{0,384},{128,0},{256,128},{384,256},{1,385},{129,1},{257,129},{385... | collective-permute-start | bytes 786440 | tf_op jit(solution)/shard_map/ppermute | solution.py:19
  97.5 12.1 %all-to-all-start.1 = ((bf16[4,256,256]{2,1,0:T(8,128)(2,1)}), bf16[4,256,256]{2,1,0:T(8,128)(2,1)S(1)}, u32[]{:S(2)}, u32[]{:S(2)}) async-start(bf16[4,256,256]{2,1,0:T(8,128)(2,1)} %get-tuple-element.30), calls=%async_computation.1 | async-start | bytes 1048576 | tf_op jit(solution)/shard_map/all_to_all | solution.py:176
  109.6 10.9 %all-to-all-start.2 = ((bf16[4,256,256]{2,1,0:T(8,128)(2,1)}), bf16[4,256,256]{2,1,0:T(8,128)(2,1)S(1)}, u32[]{:S(2)}, u32[]{:S(2)}) async-start(bf16[4,256,256]{2,1,0:T(8,128)(2,1)} %get-tuple-element.34), calls=%async_computation.2 | async-start | bytes 1048576 | tf_op jit(solution)/shard_map/all_to_all | solution.py:176
  113.1 1.6 copy-start.7
  113.1 1.4 copy-start.9
  113.1 1.4 copy-start.11
  114.5 11.3 %copy-start.6 = (f32[256,256]{1,0:T(8,128)S(1)}, f32[256,256]{1,0:T(8,128)}, u32[]{:S(2)}) copy-start(f32[256,256]{1,0:T(8,128)} %get-tuple-element.40) | copy-start | bytes 786436
  120.5 29.3 %collective-permute-start.9 = (bf16[256,256]{1,0:T(8,128)(2,1)S(1)}, bf16[256,256]{1,0:T(8,128)(2,1)S(1)}, u32[]{:S(2)}, u32[]{:S(2)}) collective-permute-start(bf16[256,256]{1,0:T(8,128)(2,1)S(1)} %add_convert_fusion.1), channel_id=1, source_target_pairs={{0,0},{1,1},{2,32},{3,33},{4,64},{5,65},{6,96},{7,97},{8,128},{9,1... | collective-permute-start | bytes 393224 | tf_op jit(solution)/shard_map/ppermute | solution.py:33
  125.9 23.9 %collective-permute-start.10 = (bf16[256,256]{1,0:T(8,128)(2,1)S(1)}, bf16[256,256]{1,0:T(8,128)(2,1)S(1)}, u32[]{:S(2)}, u32[]{:S(2)}) collective-permute-start(bf16[256,256]{1,0:T(8,128)(2,1)S(1)} %add_convert_fusion), channel_id=1, source_target_pairs={{0,1},{1,0},{2,33},{3,32},{4,65},{5,64},{6,97},{7,96},{8,129},{9,1... | collective-permute-start | bytes 393224 | tf_op jit(solution)/shard_map/ppermute | solution.py:33
  143.4 20.9 %all-to-all-start.3 = ((bf16[4,512,256]{2,1,0:T(8,128)(2,1)}), bf16[4,512,256]{2,1,0:T(8,128)(2,1)S(1)}, u32[]{:S(2)}, u32[]{:S(2)}) async-start(bf16[4,512,256]{2,1,0:T(8,128)(2,1)} %get-tuple-element.48), calls=%async_computation.3 | async-start | bytes 2097152 | tf_op jit(solution)/shard_map/all_to_all | solution.py:176
  149.8 14.8 %copy-start.3 = (f32[512,256]{1,0:T(8,128)S(1)}, f32[512,256]{1,0:T(8,128)}, u32[]{:S(2)}) copy-start(f32[512,256]{1,0:T(8,128)} %diag_ref.1) | copy-start | bytes 1572868
  149.8 14.8 %copy-start.4 = (f32[512,256]{1,0:T(8,128)S(1)}, f32[512,256]{1,0:T(8,128)}, u32[]{:S(2)}) copy-start(f32[512,256]{1,0:T(8,128)} %get-tuple-element.47) | copy-start | bytes 1572868
  149.8 0.7 copy-start.13
  150.4 0.6 copy-start.14

commit v8 on v7

--- a/solution.py
+++ b/solution.py
@@ -9,7 +9,7 @@
 ROW = ("zl", "x")
 COL = ("zh", "y", "co")
 W = 128
-STEP = 24_000_000_000
+STEP = 16_000_000_000
 LATE = 2_000_000_000
 VMEM_LIMIT = 56 * 1024 * 1024
 PARAMS = pltpu.CompilerParams(vmem_limit_bytes=VMEM_LIMIT)
@@ -201,7 +201,6 @@
     owner = blk // 4
     at = (owner % 4) * 8 + (owner // 4) * 2 + (blk % 4) // 2
     packed = pack(jnp.where(live, at, -1), co[None], h_blocks)
-    packed, tile = lax.optimization_barrier((packed, tile))
     direct_tiles = [tile] + [shifted(tile, "zl", d) for d in (1, 2, 3)]
     later = lax.optimization_barrier((half, *direct_tiles[1:]))[0]
     mirror_tiles = [half] + [shifted(later, "zl", d) for d in (1, 2, 3)]
@@ -224,12 +223,12 @@
     upper = summed(got_upper, kept_upper, x).astype(jnp.bfloat16)
     bits, _, *mirror_tiles = lax.optimization_barrier((bits, lower, *mirror_tiles))
     bits = step_kernel(bits, LATE)
-    got_lower, upper, bits = lax.optimization_barrier((got_lower, upper, bits))
-    lower = summed(got_lower, kept_lower, x).astype(jnp.bfloat16)
-    here, there = turned(upper, 0), turned(lower, 1)
     mirror, kept = partial_sums(
         mirror_kernel, "mirror", (512, 256), here_first, bits, mirror_tiles, own, other
     )
+    got_lower, upper, mirror = lax.optimization_barrier((got_lower, upper, mirror))
+    lower = summed(got_lower, kept_lower, x).astype(jnp.bfloat16)
+    here, there = turned(upper, 0), turned(lower, 1)
     mirror_term = summed(exchanged(mirror), kept, x)
     base = direct_base(co[None], energy, here, there, coeffs, diag_energy)
     return (base + mirror_term) / jnp.maximum(jnp.abs(diag_energy - energy[0]), 1.0)

time: 168 us -> 154 us (0.917)
  waiting for transfers between devices: 53.3 us -> 41.7 us
    all_to_all x1, waiting for transfers between devices: 19.2 us -> 3.53 us  [on_device(): own = lax.all_to_all(packed.reshape(4, 8, W, 2 * W), 'x', 0, 0, tiled=True)]
    ppermute x6, waiting for transfers between devices: 4.31 us -> 15.6 us  [shifted(): return lax.ppermute(value, axis, [(i, (i + step) % 4) for i in range(4)])]
    all_to_all x3, starting transfers between devices: 13.3 us -> 22.7 us  [exchanged(): return lax.all_to_all(parts, 'x', 0, 0, tiled=True)]
    ppermute x4, waiting for transfers between devices: 9.09 us -> 3.55 us  [turned(): return lax.ppermute(value, AXES, pairs)]
    all_to_all x1, starting transfers between devices: 10.7 us -> 6.57 us  [on_device(): own = lax.all_to_all(packed.reshape(4, 8, W, 2 * W), 'x', 0, 0, tiled=True)]
    ppermute x6, starting transfers between devices: 18.5 us -> 15 us  [shifted(): return lax.ppermute(value, axis, [(i, (i + step) % 4) for i in range(4)])]
    all_to_all x3, waiting for transfers between devices: 20.7 us -> 19 us  [exchanged(): return lax.all_to_all(parts, 'x', 0, 0, tiled=True)]
  transfers between devices with their start and end apart: 15 -> 15, of which waited for: 7 -> 7; matrix products, arithmetic and copies ran while one was open for 3% -> 3% of each run, Pallas kernels for 15% -> 17%
where the time goes in v8:
time: 154 us; the launch traced here: 153 us
  starting transfers between devices  76.6 us (50%)
  waiting for transfers between devices  41.7 us (27%)
  Pallas kernels  25.5 us (17%)
  other arithmetic  6.76 us (4%)
  local copies, waits for them, and re-layouts  1.81 us (1%)
    ppermute x4, starting transfers between devices, turned(): return lax.ppermute(value, AXES, pairs)  29.3 us
    all_to_all x3, starting transfers between devices, exchanged(): return lax.all_to_all(parts, 'x', 0, 0, tiled=True)  22.7 us
    all_to_all x3, waiting for transfers between devices, exchanged(): return lax.all_to_all(parts, 'x', 0, 0, tiled=True)  19 us
    pallas_call x3, Pallas kernels, partial_sums(): pl.pallas_call(kernel, out_shape=(jax.ShapeDtypeStruct((4, *shape), jnp.b...  16.4 us
    ppermute x6, waiting for transfers between devices, shifted(): return lax.ppermute(value, axis, [(i, (i + step) % 4) for i in range(4)])  15.6 us
    ppermute x6, starting transfers between devices, shifted(): return lax.ppermute(value, axis, [(i, (i + step) % 4) for i in range(4)])  15 us
    all_to_all x1, starting transfers between devices, on_device(): own = lax.all_to_all(packed.reshape(4, 8, W, 2 * W), 'x', 0, 0, tiled=True)  6.57 us
    pallas_call x1, Pallas kernels, pack(): pl.pallas_call(pack_kernel, out_shape=jax.ShapeDtypeStruct((32, W, 2 * W)...  4.37 us
  transfers between devices with their start and end apart: 15, of which 7 were waited for; matrix products, arithmetic and copies ran while one was open for 3% of the time, Pallas kernels for 17%

profile of v8, /device:TPU:65, one launch (start us, length us, event | category | flops | bytes accessed | tf_op | source)
XLA Modules:
  0.0 153.4 jit_solution(2029026061286939052)
XLA Ops:
  0.0 1.1 convert_element_type.22.t0
  1.1 13.3 %collective-permute-start.1 = (bf16[256,256]{1,0:T(8,128)(2,1)S(1)}, bf16[256,256]{1,0:T(8,128)(2,1)S(1)}, u32[]{:S(2)}, u32[]{:S(2)}) collective-permute-start(bf16[256,256]{1,0:T(8,128)(2,1)S(1)} %get-tuple-element.46), channel_id=1, source_target_pairs={{0,1},{1,0},{2,33},{3,32},{4,65},{5,64},{6,97},{7,96},{8,129},{9,1... | collective-permute-start | bytes 393224 | tf_op jit(solution)/shard_map/ppermute | solution.py:33
  14.4 1.9 %collective-permute-start = (bf16[256,256]{1,0:T(8,128)(2,1)S(1)}, bf16[256,256]{1,0:T(8,128)(2,1)S(1)}, u32[]{:S(2)}, u32[]{:S(2)}) collective-permute-start(bf16[256,256]{1,0:T(8,128)(2,1)S(1)} %get-tuple-element.45), channel_id=1, source_target_pairs={{0,0},{1,1},{2,32},{3,33},{4,64},{5,65},{6,96},{7,97},{8,128},{9,1... | collective-permute-start | bytes 393224 | tf_op jit(solution)/shard_map/ppermute | solution.py:33
  16.5 0.7 dynamic-slice
  17.9 4.4 %pack.1 = bf16[32,128,256]{2,1,0:T(8,128)(2,1)} custom-call(s32[2,24]{1,0:T(2,128)} %compare_select_fusion.pos, s32[1]{0:T(128)} %bitcast.co, bf16[4,24,128,128]{3,2,1,0:T(8,128)(2,1)} %h_ref.1), custom_call_target="tpu_custom_call" | custom-call | tf_op jit(solution)/shard_map/pack/pallas_call | solution.py:54
  22.3 6.6 %all-to-all-start = ((bf16[4,8,128,256]{3,2,1,0:T(8,128)(2,1)}), bf16[4,8,128,256]{3,2,1,0:T(8,128)(2,1)S(1)}, u32[]{:S(2)}, u32[]{:S(2)}) async-start(bf16[4,8,128,256]{3,2,1,0:T(8,128)(2,1)} %bitcast.7), calls=%async_computation | async-start | bytes 4194304 | tf_op jit(solution)/shard_map/all_to_all | solution.py:207
  28.9 2.5 %collective-permute-done = bf16[256,256]{1,0:T(8,128)(2,1)S(1)} collective-permute-done((bf16[256,256]{1,0:T(8,128)(2,1)S(1)}, bf16[256,256]{1,0:T(8,128)(2,1)S(1)}, u32[]{:S(2)}, u32[]{:S(2)}) %collective-permute-start) | collective-permute-done | bytes 131104 | tf_op jit(solution)/shard_map/ppermute | solution.py:33
  31.6 1.9 %collective-permute-start.2 = (bf16[256,512]{1,0:T(8,128)(2,1)S(1)}, bf16[256,512]{1,0:T(8,128)(2,1)S(1)}, u32[]{:S(2)}, u32[]{:S(2)}) collective-permute-start(bf16[256,512]{1,0:T(8,128)(2,1)S(1)} %maximum_select_fusion.t0), channel_id=1, source_target_pairs={{0,128},{128,256},{256,384},{384,0},{1,129},{129,257},{257,385},{3... | collective-permute-start | bytes 786440 | tf_op jit(solution)/shard_map/ppermute | solution.py:19
  33.5 1.9 %collective-permute-start.3 = (bf16[256,512]{1,0:T(8,128)(2,1)S(1)}, bf16[256,512]{1,0:T(8,128)(2,1)S(1)}, u32[]{:S(2)}, u32[]{:S(2)}) collective-permute-start(bf16[256,512]{1,0:T(8,128)(2,1)S(1)} %maximum_select_fusion.t0), channel_id=1, source_target_pairs={{0,256},{128,384},{256,0},{384,128},{1,257},{129,385},{257,1},{385... | collective-permute-start | bytes 786440 | tf_op jit(solution)/shard_map/ppermute | solution.py:19
  35.4 3.4 %collective-permute-start.4 = (bf16[256,512]{1,0:T(8,128)(2,1)S(1)}, bf16[256,512]{1,0:T(8,128)(2,1)}, u32[]{:S(2)}, u32[]{:S(2)}) collective-permute-start(bf16[256,512]{1,0:T(8,128)(2,1)S(1)} %maximum_select_fusion.t0), channel_id=1, source_target_pairs={{0,384},{128,0},{256,128},{384,256},{1,385},{129,1},{257,129},{385... | collective-permute-start | bytes 786440 | tf_op jit(solution)/shard_map/ppermute | solution.py:19
  39.9 12.1 %collective-permute-done.2.t1 = bf16[256,512]{1,0:T(8,128)(2,1)S(1)} collective-permute-done((bf16[256,512]{1,0:T(8,128)(2,1)S(1)}, bf16[256,512]{1,0:T(8,128)(2,1)S(1)}, u32[]{:S(2)}, u32[]{:S(2)}) %collective-permute-start.2) | collective-permute-done | bytes 262176 | tf_op jit(solution)/shard_map/ppermute | solution.py:19
  52.0 3.5 %collective-permute-done.4.t3 = bf16[256,512]{1,0:T(8,128)(2,1)} collective-permute-done((bf16[256,512]{1,0:T(8,128)(2,1)S(1)}, bf16[256,512]{1,0:T(8,128)(2,1)}, u32[]{:S(2)}, u32[]{:S(2)}) %collective-permute-start.4) | collective-permute-done | bytes 262176 | tf_op jit(solution)/shard_map/ppermute | solution.py:19
  55.5 1.3 step.2.bits.in_ref
  56.8 3.5 %all-to-all-done.h_ref.own_ref = bf16[4,8,128,256]{3,2,1,0:T(8,128)(2,1)S(1)} async-done(((bf16[4,8,128,256]{3,2,1,0:T(8,128)(2,1)}), bf16[4,8,128,256]{3,2,1,0:T(8,128)(2,1)S(1)}, u32[]{:S(2)}, u32[]{:S(2)}) %all-to-all-start) | async-done | bytes 2097184 | tf_op jit(solution)/shard_map/all_to_all | solution.py:207
  60.3 3.0 %collective-permute-start.5 = (bf16[4,8,128,256]{3,2,1,0:T(8,128)(2,1)S(1)}, bf16[4,8,128,256]{3,2,1,0:T(8,128)(2,1)}, u32[]{:S(2)}, u32[]{:S(2)}) collective-permute-start(bf16[4,8,128,256]{3,2,1,0:T(8,128)(2,1)S(1)} %all-to-all-done.h_ref.own_ref), channel_id=1, source_target_pairs={{0,1},{1,0},{2,3},{3,2},{4,5},{5,4},{6,7},{7,6},{8,9},{9,8},{10,11... | collective-permute-start | bytes 6291464 | tf_op jit(solution)/shard_map/ppermute | solution.py:23
  64.6 2.8 %collective-permute-start.6 = (bf16[512,256]{1,0:T(8,128)(2,1)S(1)}, bf16[512,256]{1,0:T(8,128)(2,1)S(1)}, u32[]{:S(2)}, u32[]{:S(2)}) collective-permute-start(bf16[512,256]{1,0:T(8,128)(2,1)S(1)} %convert_element_type.22.t0), channel_id=1, source_target_pairs={{0,128},{128,256},{256,384},{384,0},{1,129},{129,257},{257,385},{3... | collective-permute-start | bytes 786440 | tf_op jit(solution)/shard_map/ppermute | solution.py:19
  67.4 1.9 %collective-permute-start.7 = (bf16[512,256]{1,0:T(8,128)(2,1)S(1)}, bf16[512,256]{1,0:T(8,128)(2,1)S(1)}, u32[]{:S(2)}, u32[]{:S(2)}) collective-permute-start(bf16[512,256]{1,0:T(8,128)(2,1)S(1)} %convert_element_type.22.t0), channel_id=1, source_target_pairs={{0,256},{128,384},{256,0},{384,128},{1,257},{129,385},{257,1},{385... | collective-permute-start | bytes 786440 | tf_op jit(solution)/shard_map/ppermute | solution.py:19
  69.3 3.1 %collective-permute-start.8 = (bf16[512,256]{1,0:T(8,128)(2,1)S(1)}, bf16[512,256]{1,0:T(8,128)(2,1)}, u32[]{:S(2)}, u32[]{:S(2)}) collective-permute-start(bf16[512,256]{1,0:T(8,128)(2,1)S(1)} %convert_element_type.22.t0), channel_id=1, source_target_pairs={{0,384},{128,0},{256,128},{384,256},{1,385},{129,1},{257,129},{385... | collective-permute-start | bytes 786440 | tf_op jit(solution)/shard_map/ppermute | solution.py:19
  72.4 4.5 %direct.2 = (bf16[4,256,256]{2,1,0:T(8,128)(2,1)}, f32[256,256]{1,0:T(8,128)}) custom-call(s32[3]{0:T(128)} %pad_add_fusion.2.where, s32[8,8]{1,0:T(8,128)} %step.2.bits.in_ref, bf16[256,512]{1,0:T(8,128)(2,1)} %copy-done.5, bf16[256,512]{1,0:T(8,128)(2,1)} %copy-done.8, bf16[256,512]{1,0:T(8,128)(2,1)} %copy-done.9, ...), custom_call_target="tpu_custom_call" | custom-call | flops 20000000000 | bytes 40000000 | tf_op jit(solution)/shard_map/direct/pallas_call | solution.py:126
  77.0 9.9 %all-to-all-start.1 = ((bf16[4,256,256]{2,1,0:T(8,128)(2,1)}), bf16[4,256,256]{2,1,0:T(8,128)(2,1)S(1)}, u32[]{:S(2)}, u32[]{:S(2)}) async-start(bf16[4,256,256]{2,1,0:T(8,128)(2,1)} %get-tuple-element.26), calls=%async_computation.1 | async-start | bytes 1048576 | tf_op jit(solution)/shard_map/all_to_all | solution.py:176
  86.9 4.5 %direct.3 = (bf16[4,256,256]{2,1,0:T(8,128)(2,1)}, f32[256,256]{1,0:T(8,128)}) custom-call(s32[3]{0:T(128)} %pad_add_fusion.where, s32[8,8]{1,0:T(8,128)} %step.2.bits.in_ref, bf16[256,512]{1,0:T(8,128)(2,1)} %copy-done.5, bf16[256,512]{1,0:T(8,128)(2,1)} %copy-done.8, bf16[256,512]{1,0:T(8,128)(2,1)} %copy-done.9, ...), custom_call_target="tpu_custom_call" | custom-call | flops 20000000000 | bytes 40000000 | tf_op jit(solution)/shard_map/direct/pallas_call | solution.py:126
  91.5 4.1 %all-to-all-done.1 = bf16[4,256,256]{2,1,0:T(8,128)(2,1)S(1)} async-done(((bf16[4,256,256]{2,1,0:T(8,128)(2,1)}), bf16[4,256,256]{2,1,0:T(8,128)(2,1)S(1)}, u32[]{:S(2)}, u32[]{:S(2)}) %all-to-all-start.1) | async-done | bytes 524320 | tf_op jit(solution)/shard_map/all_to_all | solution.py:176
  95.6 3.5 %all-to-all-start.2 = ((bf16[4,256,256]{2,1,0:T(8,128)(2,1)}), bf16[4,256,256]{2,1,0:T(8,128)(2,1)S(1)}, u32[]{:S(2)}, u32[]{:S(2)}) async-start(bf16[4,256,256]{2,1,0:T(8,128)(2,1)} %get-tuple-element.30), calls=%async_computation.2 | async-start | bytes 1048576 | tf_op jit(solution)/shard_map/all_to_all | solution.py:176
  99.1 1.3 step.3.bits
  100.4 7.3 %mirror.1 = (bf16[4,512,256]{2,1,0:T(8,128)(2,1)}, f32[512,256]{1,0:T(8,128)}) custom-call(s32[3]{0:T(128)} %pad_add_fusion.2.where, s32[8,8]{1,0:T(8,128)} %step.3.bits, bf16[512,256]{1,0:T(8,128)(2,1)} %copy-done.2, bf16[512,256]{1,0:T(8,128)(2,1)} %copy-done.10, bf16[512,256]{1,0:T(8,128)(2,1)} %copy-done.11, bf16[512,256]{1,0:T(8,128)(2,1)} %collective-permute-done.8.t3, ...), custom_call_target="tpu_custom_call" | custom-call | flops 20000000000 | bytes 40000000 | tf_op jit(solution)/shard_map/mirror/pallas_call | solution.py:126
  107.9 7.0 %collective-permute-start.9 = (bf16[256,256]{1,0:T(8,128)(2,1)S(1)}, bf16[256,256]{1,0:T(8,128)(2,1)S(1)}, u32[]{:S(2)}, u32[]{:S(2)}) collective-permute-start(bf16[256,256]{1,0:T(8,128)(2,1)S(1)} %add_convert_fusion.1), channel_id=1, source_target_pairs={{0,0},{1,1},{2,32},{3,33},{4,64},{5,65},{6,96},{7,97},{8,128},{9,1... | collective-permute-start | bytes 393224 | tf_op jit(solution)/shard_map/ppermute | solution.py:33
  115.2 7.1 %collective-permute-start.10 = (bf16[256,256]{1,0:T(8,128)(2,1)S(1)}, bf16[256,256]{1,0:T(8,128)(2,1)S(1)}, u32[]{:S(2)}, u32[]{:S(2)}) collective-permute-start(bf16[256,256]{1,0:T(8,128)(2,1)S(1)} %add_convert_fusion), channel_id=1, source_target_pairs={{0,1},{1,0},{2,33},{3,32},{4,65},{5,64},{6,97},{7,96},{8,129},{9,1... | collective-permute-start | bytes 393224 | tf_op jit(solution)/shard_map/ppermute | solution.py:33
  123.0 9.3 %all-to-all-start.3 = ((bf16[4,512,256]{2,1,0:T(8,128)(2,1)}), bf16[4,512,256]{2,1,0:T(8,128)(2,1)S(1)}, u32[]{:S(2)}, u32[]{:S(2)}) async-start(bf16[4,512,256]{2,1,0:T(8,128)(2,1)} %get-tuple-element.44), calls=%async_computation.3 | async-start | bytes 2097152 | tf_op jit(solution)/shard_map/all_to_all | solution.py:176
  132.3 1.0 collective-permute-done.10.there_ref
  134.0 2.2 %base.1 = f32[512,256]{1,0:T(8,128)} custom-call(s32[1]{0:T(128)} %bitcast.co, f32[1]{0:T(128)} %copy.13.energy, bf16[256,256]{1,0:T(8,128)(2,1)} %copy-done.12, bf16[256,256]{1,0:T(8,128)(2,1)} %copy-done.13, f32[512,256]{1,0:T(8,128)} %coeffs_ref.1, f32[512,256]{1,0:T(8,128)} %diag_ref.1), custom_call_target="tpu_custom_call" | custom-call | flops 20000000000 | bytes 40000000 | tf_op jit(solution)/shard_map/base/pallas_call | solution.py:149
  136.2 14.9 %all-to-all-done.3 = bf16[4,512,256]{2,1,0:T(8,128)(2,1)S(1)} async-done(((bf16[4,512,256]{2,1,0:T(8,128)(2,1)}), bf16[4,512,256]{2,1,0:T(8,128)(2,1)S(1)}, u32[]{:S(2)}, u32[]{:S(2)}) %all-to-all-start.3) | async-done | bytes 1048608 | tf_op jit(solution)/shard_map/all_to_all | solution.py:176
  151.4 2.0 %maximum_divide_fusion = f32[512,256]{1,0:T(8,128)} fusion(f32[512,256]{1,0:T(8,128)S(1)} %copy-done.3, f32[512,256]{1,0:T(8,128)} %base.1, f32[512,256]{1,0:T(8,128)S(1)} %copy-done.4, f32[512,256]{1,0:T(8,128)S(1)} %convert_reduce_fusion, f32[]{:T(128)} %bitcast.6), kind=kLoop, calls=%fused_computation.3 | loop fusion | flops 786432 | bytes 2621444 | tf_op jit(solution)/shard_map/div | solution.py:234
  (55 shorter events, 4.8 us)
Async XLA Ops:
  0.0 16.4 %copy-start = (s32[64,24]{0,1:T(8,128)S(1)}, s32[64,24]{0,1:T(8,128)}, u32[]{:S(2)}) copy-start(s32[64,24]{0,1:T(8,128)} %param.10) | copy-start | bytes 18436
  1.1 68.2 %copy-start.2 = (bf16[512,256]{1,0:T(8,128)(2,1)}, bf16[512,256]{1,0:T(8,128)(2,1)S(1)}, u32[]{:S(2)}) copy-start(bf16[512,256]{1,0:T(8,128)(2,1)S(1)} %convert_element_type.22.t0) | copy-start | bytes 786436
  1.1 27.8 %collective-permute-start.1 = (bf16[256,256]{1,0:T(8,128)(2,1)S(1)}, bf16[256,256]{1,0:T(8,128)(2,1)S(1)}, u32[]{:S(2)}, u32[]{:S(2)}) collective-permute-start(bf16[256,256]{1,0:T(8,128)(2,1)S(1)} %get-tuple-element.46), channel_id=1, source_target_pairs={{0,1},{1,0},{2,33},{3,32},{4,65},{5,64},{6,97},{7,96},{8,129},{9,1... | collective-permute-start | bytes 393224 | tf_op jit(solution)/shard_map/ppermute | solution.py:33
  14.4 17.0 %collective-permute-start = (bf16[256,256]{1,0:T(8,128)(2,1)S(1)}, bf16[256,256]{1,0:T(8,128)(2,1)S(1)}, u32[]{:S(2)}, u32[]{:S(2)}) collective-permute-start(bf16[256,256]{1,0:T(8,128)(2,1)S(1)} %get-tuple-element.45), channel_id=1, source_target_pairs={{0,0},{1,1},{2,32},{3,33},{4,64},{5,65},{6,96},{7,97},{8,128},{9,1... | collective-permute-start | bytes 393224 | tf_op jit(solution)/shard_map/ppermute | solution.py:33
  22.3 38.0 %all-to-all-start = ((bf16[4,8,128,256]{3,2,1,0:T(8,128)(2,1)}), bf16[4,8,128,256]{3,2,1,0:T(8,128)(2,1)S(1)}, u32[]{:S(2)}, u32[]{:S(2)}) async-start(bf16[4,8,128,256]{3,2,1,0:T(8,128)(2,1)} %bitcast.7), calls=%async_computation | async-start | bytes 4194304 | tf_op jit(solution)/shard_map/all_to_all | solution.py:207
  31.6 25.2 %copy-start.5 = (bf16[256,512]{1,0:T(8,128)(2,1)}, bf16[256,512]{1,0:T(8,128)(2,1)S(1)}, u32[]{:S(2)}) copy-start(bf16[256,512]{1,0:T(8,128)(2,1)S(1)} %maximum_select_fusion.t0) | copy-start | bytes 786436
  31.6 20.4 %collective-permute-start.2 = (bf16[256,512]{1,0:T(8,128)(2,1)S(1)}, bf16[256,512]{1,0:T(8,128)(2,1)S(1)}, u32[]{:S(2)}, u32[]{:S(2)}) collective-permute-start(bf16[256,512]{1,0:T(8,128)(2,1)S(1)} %maximum_select_fusion.t0), channel_id=1, source_target_pairs={{0,128},{128,256},{256,384},{384,0},{1,129},{129,257},{257,385},{3... | collective-permute-start | bytes 786440 | tf_op jit(solution)/shard_map/ppermute | solution.py:19
  33.5 18.5 %collective-permute-start.3 = (bf16[256,512]{1,0:T(8,128)(2,1)S(1)}, bf16[256,512]{1,0:T(8,128)(2,1)S(1)}, u32[]{:S(2)}, u32[]{:S(2)}) collective-permute-start(bf16[256,512]{1,0:T(8,128)(2,1)S(1)} %maximum_select_fusion.t0), channel_id=1, source_target_pairs={{0,256},{128,384},{256,0},{384,128},{1,257},{129,385},{257,1},{385... | collective-permute-start | bytes 786440 | tf_op jit(solution)/shard_map/ppermute | solution.py:19
  35.4 20.1 %collective-permute-start.4 = (bf16[256,512]{1,0:T(8,128)(2,1)S(1)}, bf16[256,512]{1,0:T(8,128)(2,1)}, u32[]{:S(2)}, u32[]{:S(2)}) collective-permute-start(bf16[256,512]{1,0:T(8,128)(2,1)S(1)} %maximum_select_fusion.t0), channel_id=1, source_target_pairs={{0,384},{128,0},{256,128},{384,256},{1,385},{129,1},{257,129},{385... | collective-permute-start | bytes 786440 | tf_op jit(solution)/shard_map/ppermute | solution.py:19
  52.0 4.8 %copy-start.8 = (bf16[256,512]{1,0:T(8,128)(2,1)}, bf16[256,512]{1,0:T(8,128)(2,1)S(1)}, u32[]{:S(2)}) copy-start(bf16[256,512]{1,0:T(8,128)(2,1)S(1)} %collective-permute-done.2.t1) | copy-start | bytes 786436
  52.0 4.8 %copy-start.9 = (bf16[256,512]{1,0:T(8,128)(2,1)}, bf16[256,512]{1,0:T(8,128)(2,1)S(1)}, u32[]{:S(2)}) copy-start(bf16[256,512]{1,0:T(8,128)(2,1)S(1)} %collective-permute-done.3.t2) | copy-start | bytes 786436
  60.3 12.1 %copy-start.1 = (bf16[4,8,128,256]{3,2,1,0:T(8,128)(2,1)}, bf16[4,8,128,256]{3,2,1,0:T(8,128)(2,1)S(1)}, u32[]{:S(2)}) copy-start(bf16[4,8,128,256]{3,2,1,0:T(8,128)(2,1)S(1)} %all-to-all-done.h_ref.own_ref) | copy-start | bytes 6291460
  60.3 26.6 %collective-permute-start.5 = (bf16[4,8,128,256]{3,2,1,0:T(8,128)(2,1)S(1)}, bf16[4,8,128,256]{3,2,1,0:T(8,128)(2,1)}, u32[]{:S(2)}, u32[]{:S(2)}) collective-permute-start(bf16[4,8,128,256]{3,2,1,0:T(8,128)(2,1)S(1)} %all-to-all-done.h_ref.own_ref), channel_id=1, source_target_pairs={{0,1},{1,0},{2,3},{3,2},{4,5},{5,4},{6,7},{7,6},{8,9},{9,8},{10,11... | collective-permute-start | bytes 6291464 | tf_op jit(solution)/shard_map/ppermute | solution.py:23
  64.6 34.5 %collective-permute-start.6 = (bf16[512,256]{1,0:T(8,128)(2,1)S(1)}, bf16[512,256]{1,0:T(8,128)(2,1)S(1)}, u32[]{:S(2)}, u32[]{:S(2)}) collective-permute-start(bf16[512,256]{1,0:T(8,128)(2,1)S(1)} %convert_element_type.22.t0), channel_id=1, source_target_pairs={{0,128},{128,256},{256,384},{384,0},{1,129},{129,257},{257,385},{3... | collective-permute-start | bytes 786440 | tf_op jit(solution)/shard_map/ppermute | solution.py:19
  67.4 31.7 %collective-permute-start.7 = (bf16[512,256]{1,0:T(8,128)(2,1)S(1)}, bf16[512,256]{1,0:T(8,128)(2,1)S(1)}, u32[]{:S(2)}, u32[]{:S(2)}) collective-permute-start(bf16[512,256]{1,0:T(8,128)(2,1)S(1)} %convert_element_type.22.t0), channel_id=1, source_target_pairs={{0,256},{128,384},{256,0},{384,128},{1,257},{129,385},{257,1},{385... | collective-permute-start | bytes 786440 | tf_op jit(solution)/shard_map/ppermute | solution.py:19
  69.3 29.8 %collective-permute-start.8 = (bf16[512,256]{1,0:T(8,128)(2,1)S(1)}, bf16[512,256]{1,0:T(8,128)(2,1)}, u32[]{:S(2)}, u32[]{:S(2)}) collective-permute-start(bf16[512,256]{1,0:T(8,128)(2,1)S(1)} %convert_element_type.22.t0), channel_id=1, source_target_pairs={{0,384},{128,0},{256,128},{384,256},{1,385},{129,1},{257,129},{385... | collective-permute-start | bytes 786440 | tf_op jit(solution)/shard_map/ppermute | solution.py:19
  77.0 18.6 %all-to-all-start.1 = ((bf16[4,256,256]{2,1,0:T(8,128)(2,1)}), bf16[4,256,256]{2,1,0:T(8,128)(2,1)S(1)}, u32[]{:S(2)}, u32[]{:S(2)}) async-start(bf16[4,256,256]{2,1,0:T(8,128)(2,1)} %get-tuple-element.26), calls=%async_computation.1 | async-start | bytes 1048576 | tf_op jit(solution)/shard_map/all_to_all | solution.py:176
  95.6 12.4 %all-to-all-start.2 = ((bf16[4,256,256]{2,1,0:T(8,128)(2,1)}), bf16[4,256,256]{2,1,0:T(8,128)(2,1)S(1)}, u32[]{:S(2)}, u32[]{:S(2)}) async-start(bf16[4,256,256]{2,1,0:T(8,128)(2,1)} %get-tuple-element.30), calls=%async_computation.2 | async-start | bytes 1048576 | tf_op jit(solution)/shard_map/all_to_all | solution.py:176
  99.1 1.3 copy-start.10
  99.1 1.3 copy-start.11
  100.4 7.5 %copy-start.7 = (f32[256,256]{1,0:T(8,128)S(1)}, f32[256,256]{1,0:T(8,128)}, u32[]{:S(2)}) copy-start(f32[256,256]{1,0:T(8,128)} %get-tuple-element.31) | copy-start | bytes 786436
  107.7 7.5 %copy-start.6 = (f32[256,256]{1,0:T(8,128)S(1)}, f32[256,256]{1,0:T(8,128)}, u32[]{:S(2)}) copy-start(f32[256,256]{1,0:T(8,128)} %get-tuple-element.41) | copy-start | bytes 786436
  107.9 24.3 %collective-permute-start.9 = (bf16[256,256]{1,0:T(8,128)(2,1)S(1)}, bf16[256,256]{1,0:T(8,128)(2,1)S(1)}, u32[]{:S(2)}, u32[]{:S(2)}) collective-permute-start(bf16[256,256]{1,0:T(8,128)(2,1)S(1)} %add_convert_fusion.1), channel_id=1, source_target_pairs={{0,0},{1,1},{2,32},{3,33},{4,64},{5,65},{6,96},{7,97},{8,128},{9,1... | collective-permute-start | bytes 393224 | tf_op jit(solution)/shard_map/ppermute | solution.py:33
  115.2 18.1 %collective-permute-start.10 = (bf16[256,256]{1,0:T(8,128)(2,1)S(1)}, bf16[256,256]{1,0:T(8,128)(2,1)S(1)}, u32[]{:S(2)}, u32[]{:S(2)}) collective-permute-start(bf16[256,256]{1,0:T(8,128)(2,1)S(1)} %add_convert_fusion), channel_id=1, source_target_pairs={{0,1},{1,0},{2,33},{3,32},{4,65},{5,64},{6,97},{7,96},{8,129},{9,1... | collective-permute-start | bytes 393224 | tf_op jit(solution)/shard_map/ppermute | solution.py:33
  123.0 28.1 %all-to-all-start.3 = ((bf16[4,512,256]{2,1,0:T(8,128)(2,1)}), bf16[4,512,256]{2,1,0:T(8,128)(2,1)S(1)}, u32[]{:S(2)}, u32[]{:S(2)}) async-start(bf16[4,512,256]{2,1,0:T(8,128)(2,1)} %get-tuple-element.44), calls=%async_computation.3 | async-start | bytes 2097152 | tf_op jit(solution)/shard_map/all_to_all | solution.py:176
  132.3 19.2 %copy-start.3 = (f32[512,256]{1,0:T(8,128)S(1)}, f32[512,256]{1,0:T(8,128)}, u32[]{:S(2)}) copy-start(f32[512,256]{1,0:T(8,128)} %diag_ref.1) | copy-start | bytes 1572868
  132.3 19.2 %copy-start.4 = (f32[512,256]{1,0:T(8,128)S(1)}, f32[512,256]{1,0:T(8,128)}, u32[]{:S(2)}) copy-start(f32[512,256]{1,0:T(8,128)} %get-tuple-element.43) | copy-start | bytes 1572868
  132.3 1.0 copy-start.12
  133.3 0.7 copy-start.13

commit v9 on v8

--- a/solution.py
+++ b/solution.py
@@ -77,23 +77,25 @@
     return strings, jnp.concatenate(blocks, axis=0)
 
 
-def direct_kernel(where, bits, t0, t1, t2, t3, h_ref, out_ref, kept_ref):
+def direct_kernel(where, bits, t0, t1, t2, t3, own_ref, other_ref, out_ref, kept_ref):
     for column in range(4):
-        strings, blocks = strings_and_blocks(
-            where,
-            bits,
-            (t0, t1, t2, t3),
-            h_ref,
-            column,
-            column * 2 + where[2],
-            lambda tile, start: tile[:, pl.ds(start, W)],
-        )
-        part = jnp.dot(jnp.concatenate(strings, axis=1), blocks, preferred_element_type=jnp.float32)
-        out_ref[column] = part.astype(jnp.bfloat16)
-
-        @pl.when(where[1] == column)
-        def _():
-            kept_ref[...] = part
+        for order, h_ref in enumerate((own_ref, other_ref)):
+            strings, blocks = strings_and_blocks(
+                where,
+                bits,
+                (t0, t1, t2, t3),
+                h_ref,
+                column,
+                column * 2 + (where[2] if order == 0 else 1 - where[2]),
+                lambda tile, start: tile[:, pl.ds(start, W)],
+            )
+            part = jnp.dot(jnp.concatenate(strings, axis=1), blocks, preferred_element_type=jnp.float32)
+            rows = slice(order * 256, (order + 1) * 256)
+            out_ref[column, rows, :] = part.astype(jnp.bfloat16)
+
+            @pl.when(where[1] == column)
+            def _():
+                kept_ref[rows, :] = part
 
 
 def mirror_kernel(where, bits, t0, t1, t2, t3, own_ref, other_ref, out_ref, kept_ref):
@@ -202,7 +204,7 @@
     at = (owner % 4) * 8 + (owner // 4) * 2 + (blk % 4) // 2
     packed = pack(jnp.where(live, at, -1), co[None], h_blocks)
     direct_tiles = [tile] + [shifted(tile, "zl", d) for d in (1, 2, 3)]
-    later = lax.optimization_barrier((half, *direct_tiles[1:]))[0]
+    later = lax.optimization_barrier((half, direct_tiles[1]))[0]
     mirror_tiles = [half] + [shifted(later, "zl", d) for d in (1, 2, 3)]
     own = lax.all_to_all(packed.reshape(4, 8, W, 2 * W), "x", 0, 0, tiled=True)
     names = lax.dynamic_slice_in_dim(pattern, zl * 16, 16, 0).reshape(8, 1, 2 * slots)
@@ -212,24 +214,22 @@
     bits = step_kernel(lax.optimization_barrier((bits, *direct_tiles[1:]))[0], STEP)
     other = swap_cores(lax.optimization_barrier((own, bits))[0])
     here_first = jnp.stack([zl, x, co])
-    there_first = jnp.stack([zl, x, 1 - co])
-
-    upper, kept_upper = partial_sums(direct_kernel, "direct", (256, 256), here_first, bits, direct_tiles, own)
-    got_upper = exchanged(upper)
-    direct_tiles[3], upper = lax.optimization_barrier((direct_tiles[3], upper))
-    lower, kept_lower = partial_sums(direct_kernel, "direct", (256, 256), there_first, bits, direct_tiles, other)
-    lower, got_upper = lax.optimization_barrier((lower, got_upper))
-    got_lower = exchanged(lower)
-    upper = summed(got_upper, kept_upper, x).astype(jnp.bfloat16)
-    bits, _, *mirror_tiles = lax.optimization_barrier((bits, lower, *mirror_tiles))
+
+    direct, kept_direct = partial_sums(
+        direct_kernel, "direct", (512, 256), here_first, bits, direct_tiles, own, other
+    )
+    got_direct = exchanged(direct)
+    bits, _, *mirror_tiles = lax.optimization_barrier((bits, direct, *mirror_tiles))
     bits = step_kernel(bits, LATE)
     mirror, kept = partial_sums(
         mirror_kernel, "mirror", (512, 256), here_first, bits, mirror_tiles, own, other
     )
-    got_lower, upper, mirror = lax.optimization_barrier((got_lower, upper, mirror))
-    lower = summed(got_lower, kept_lower, x).astype(jnp.bfloat16)
-    here, there = turned(upper, 0), turned(lower, 1)
-    mirror_term = summed(exchanged(mirror), kept, x)
+    got_direct, mirror = lax.optimization_barrier((got_direct, mirror))
+    direct = summed(got_direct, kept_direct, x).astype(jnp.bfloat16)
+    sums = lax.optimization_barrier((direct[:256], direct[256:]))
+    here, there = turned(sums[0], 0), turned(sums[1], 1)
+    got_mirror, direct = lax.optimization_barrier((exchanged(mirror), direct))
+    mirror_term = summed(got_mirror, kept, x)
     base = direct_base(co[None], energy, here, there, coeffs, diag_energy)
     return (base + mirror_term) / jnp.maximum(jnp.abs(diag_energy - energy[0]), 1.0)
 

time: 154 us -> 153 us (level)
  starting transfers between devices: 76.6 us -> 69.7 us
  waiting for transfers between devices: 41.7 us -> 48.4 us
  Pallas kernels: 25.5 us -> 23.6 us
    all_to_all x3 -> x2, starting transfers between devices: 22.7 us -> 16.2 us  [exchanged(): return lax.all_to_all(parts, 'x', 0, 0, tiled=True)]
    ppermute x4, waiting for transfers between devices: 3.55 us -> 7.64 us  [turned(): return lax.ppermute(value, AXES, pairs)]
    all_to_all x3 -> x2, waiting for transfers between devices: 19 us -> 21.8 us  [exchanged(): return lax.all_to_all(parts, 'x', 0, 0, tiled=True)]
    pallas_call x3 -> x2, Pallas kernels: 16.4 us -> 14.5 us  [partial_sums(): pl.pallas_call(kernel, out_shape=(jax.ShapeDtypeStruct((4, *shape), jnp.b...]
  transfers between devices with their start and end apart: 15 -> 14, of which waited for: 7 -> 8; matrix products, arithmetic and copies ran while one was open for 3% -> 2% of each run, Pallas kernels for 17% -> 16%
where the time goes in v9:
time: 153 us; the launch traced here: 152 us
  starting transfers between devices  69.7 us (46%)
  waiting for transfers between devices  48.4 us (32%)
  Pallas kernels  23.6 us (15%)
  other arithmetic  6.09 us (4%)
  local copies, waits for them, and re-layouts  3.15 us (2%)
    ppermute x4, starting transfers between devices, turned(): return lax.ppermute(value, AXES, pairs)  29.1 us
    all_to_all x2, waiting for transfers between devices, exchanged(): return lax.all_to_all(parts, 'x', 0, 0, tiled=True)  21.8 us
    all_to_all x2, starting transfers between devices, exchanged(): return lax.all_to_all(parts, 'x', 0, 0, tiled=True)  16.2 us
    ppermute x6, starting transfers between devices, shifted(): return lax.ppermute(value, axis, [(i, (i + step) % 4) for i in range(4)])  15.3 us
    ppermute x6, waiting for transfers between devices, shifted(): return lax.ppermute(value, axis, [(i, (i + step) % 4) for i in range(4)])  14.8 us
    pallas_call x2, Pallas kernels, partial_sums(): pl.pallas_call(kernel, out_shape=(jax.ShapeDtypeStruct((4, *shape), jnp.b...  14.5 us
    ppermute x4, waiting for transfers between devices, turned(): return lax.ppermute(value, AXES, pairs)  7.64 us
    all_to_all x1, starting transfers between devices, on_device(): own = lax.all_to_all(packed.reshape(4, 8, W, 2 * W), 'x', 0, 0, tiled=True)  6.64 us
  transfers between devices with their start and end apart: 14, of which 8 were waited for; matrix products, arithmetic and copies ran while one was open for 2% of the time, Pallas kernels for 16%

profile of v9, /device:TPU:65, one launch (start us, length us, event | category | flops | bytes accessed | tf_op | source)
XLA Modules:
  0.0 152.0 jit_solution(1756180411968914068)
XLA Ops:
  0.0 1.1 convert_element_type.16.t0
  1.1 12.7 %collective-permute-start = (bf16[256,256]{1,0:T(8,128)(2,1)S(1)}, bf16[256,256]{1,0:T(8,128)(2,1)S(1)}, u32[]{:S(2)}, u32[]{:S(2)}) collective-permute-start(bf16[256,256]{1,0:T(8,128)(2,1)S(1)} %get-tuple-element.41), channel_id=1, source_target_pairs={{0,0},{1,1},{2,32},{3,33},{4,64},{5,65},{6,96},{7,97},{8,128},{9,1... | collective-permute-start | bytes 393224 | tf_op jit(solution)/shard_map/ppermute | solution.py:33
  13.9 2.5 %collective-permute-start.1 = (bf16[256,256]{1,0:T(8,128)(2,1)S(1)}, bf16[256,256]{1,0:T(8,128)(2,1)S(1)}, u32[]{:S(2)}, u32[]{:S(2)}) collective-permute-start(bf16[256,256]{1,0:T(8,128)(2,1)S(1)} %get-tuple-element.42), channel_id=1, source_target_pairs={{0,1},{1,0},{2,33},{3,32},{4,65},{5,64},{6,97},{7,96},{8,129},{9,1... | collective-permute-start | bytes 393224 | tf_op jit(solution)/shard_map/ppermute | solution.py:33
  16.5 0.7 dynamic-slice
  17.9 4.4 %pack.1 = bf16[32,128,256]{2,1,0:T(8,128)(2,1)} custom-call(s32[2,24]{1,0:T(2,128)} %compare_select_fusion.pos, s32[1]{0:T(128)} %bitcast.co, bf16[4,24,128,128]{3,2,1,0:T(8,128)(2,1)} %h_ref.1), custom_call_target="tpu_custom_call" | custom-call | tf_op jit(solution)/shard_map/pack/pallas_call | solution.py:54
  22.3 6.6 %all-to-all-start = ((bf16[4,8,128,256]{3,2,1,0:T(8,128)(2,1)}), bf16[4,8,128,256]{3,2,1,0:T(8,128)(2,1)S(1)}, u32[]{:S(2)}, u32[]{:S(2)}) async-start(bf16[4,8,128,256]{3,2,1,0:T(8,128)(2,1)} %bitcast.6), calls=%async_computation | async-start | bytes 4194304 | tf_op jit(solution)/shard_map/all_to_all | solution.py:209
  29.0 3.2 %collective-permute-done.1 = bf16[256,256]{1,0:T(8,128)(2,1)S(1)} collective-permute-done((bf16[256,256]{1,0:T(8,128)(2,1)S(1)}, bf16[256,256]{1,0:T(8,128)(2,1)S(1)}, u32[]{:S(2)}, u32[]{:S(2)}) %collective-permute-start.1) | collective-permute-done | bytes 131104 | tf_op jit(solution)/shard_map/ppermute | solution.py:33
  32.3 1.9 %collective-permute-start.2 = (bf16[256,512]{1,0:T(8,128)(2,1)S(1)}, bf16[256,512]{1,0:T(8,128)(2,1)S(1)}, u32[]{:S(2)}, u32[]{:S(2)}) collective-permute-start(bf16[256,512]{1,0:T(8,128)(2,1)S(1)} %maximum_select_fusion.t0), channel_id=1, source_target_pairs={{0,128},{128,256},{256,384},{384,0},{1,129},{129,257},{257,385},{3... | collective-permute-start | bytes 786440 | tf_op jit(solution)/shard_map/ppermute | solution.py:19
  34.2 1.9 %collective-permute-start.3 = (bf16[256,512]{1,0:T(8,128)(2,1)S(1)}, bf16[256,512]{1,0:T(8,128)(2,1)S(1)}, u32[]{:S(2)}, u32[]{:S(2)}) collective-permute-start(bf16[256,512]{1,0:T(8,128)(2,1)S(1)} %maximum_select_fusion.t0), channel_id=1, source_target_pairs={{0,256},{128,384},{256,0},{384,128},{1,257},{129,385},{257,1},{385... | collective-permute-start | bytes 786440 | tf_op jit(solution)/shard_map/ppermute | solution.py:19
  36.2 3.4 %collective-permute-start.4 = (bf16[256,512]{1,0:T(8,128)(2,1)S(1)}, bf16[256,512]{1,0:T(8,128)(2,1)S(1)}, u32[]{:S(2)}, u32[]{:S(2)}) collective-permute-start(bf16[256,512]{1,0:T(8,128)(2,1)S(1)} %maximum_select_fusion.t0), channel_id=1, source_target_pairs={{0,384},{128,0},{256,128},{384,256},{1,385},{129,1},{257,129},{385... | collective-permute-start | bytes 786440 | tf_op jit(solution)/shard_map/ppermute | solution.py:19
  40.7 12.2 %collective-permute-done.2.t1 = bf16[256,512]{1,0:T(8,128)(2,1)S(1)} collective-permute-done((bf16[256,512]{1,0:T(8,128)(2,1)S(1)}, bf16[256,512]{1,0:T(8,128)(2,1)S(1)}, u32[]{:S(2)}, u32[]{:S(2)}) %collective-permute-start.2) | collective-permute-done | bytes 262176 | tf_op jit(solution)/shard_map/ppermute | solution.py:19
  52.9 2.6 %collective-permute-done.4.t3 = bf16[256,512]{1,0:T(8,128)(2,1)S(1)} collective-permute-done((bf16[256,512]{1,0:T(8,128)(2,1)S(1)}, bf16[256,512]{1,0:T(8,128)(2,1)S(1)}, u32[]{:S(2)}, u32[]{:S(2)}) %collective-permute-start.4) | collective-permute-done | bytes 262176 | tf_op jit(solution)/shard_map/ppermute | solution.py:19
  55.5 1.3 step.2.bits.in_ref
  56.8 4.1 %all-to-all-done.own_ref = bf16[4,8,128,256]{3,2,1,0:T(8,128)(2,1)S(1)} async-done(((bf16[4,8,128,256]{3,2,1,0:T(8,128)(2,1)}), bf16[4,8,128,256]{3,2,1,0:T(8,128)(2,1)S(1)}, u32[]{:S(2)}, u32[]{:S(2)}) %all-to-all-start) | async-done | bytes 2097184 | tf_op jit(solution)/shard_map/all_to_all | solution.py:209
  60.9 2.5 %collective-permute-start.5 = (bf16[4,8,128,256]{3,2,1,0:T(8,128)(2,1)S(1)}, bf16[4,8,128,256]{3,2,1,0:T(8,128)(2,1)S(1)}, u32[]{:S(2)}, u32[]{:S(2)}) collective-permute-start(bf16[4,8,128,256]{3,2,1,0:T(8,128)(2,1)S(1)} %all-to-all-done.own_ref), channel_id=1, source_target_pairs={{0,1},{1,0},{2,3},{3,2},{4,5},{5,4},{6,7},{7,6},{8,9},{9,8},{10,11... | collective-permute-start | bytes 6291464 | tf_op jit(solution)/shard_map/ppermute | solution.py:23
  64.1 3.1 %collective-permute-start.6 = (bf16[512,256]{1,0:T(8,128)(2,1)S(1)}, bf16[512,256]{1,0:T(8,128)(2,1)S(1)}, u32[]{:S(2)}, u32[]{:S(2)}) collective-permute-start(bf16[512,256]{1,0:T(8,128)(2,1)S(1)} %convert_element_type.16.t0), channel_id=1, source_target_pairs={{0,128},{128,256},{256,384},{384,0},{1,129},{129,257},{257,385},{3... | collective-permute-start | bytes 786440 | tf_op jit(solution)/shard_map/ppermute | solution.py:19
  67.2 1.9 %collective-permute-start.7 = (bf16[512,256]{1,0:T(8,128)(2,1)S(1)}, bf16[512,256]{1,0:T(8,128)(2,1)S(1)}, u32[]{:S(2)}, u32[]{:S(2)}) collective-permute-start(bf16[512,256]{1,0:T(8,128)(2,1)S(1)} %convert_element_type.16.t0), channel_id=1, source_target_pairs={{0,256},{128,384},{256,0},{384,128},{1,257},{129,385},{257,1},{385... | collective-permute-start | bytes 786440 | tf_op jit(solution)/shard_map/ppermute | solution.py:19
  69.1 3.1 %collective-permute-start.8 = (bf16[512,256]{1,0:T(8,128)(2,1)S(1)}, bf16[512,256]{1,0:T(8,128)(2,1)S(1)}, u32[]{:S(2)}, u32[]{:S(2)}) collective-permute-start(bf16[512,256]{1,0:T(8,128)(2,1)S(1)} %convert_element_type.16.t0), channel_id=1, source_target_pairs={{0,384},{128,0},{256,128},{384,256},{1,385},{129,1},{257,129},{385... | collective-permute-start | bytes 786440 | tf_op jit(solution)/shard_map/ppermute | solution.py:19
  72.2 1.3 copy-done.7
  73.5 7.1 %direct.1 = (bf16[4,512,256]{2,1,0:T(8,128)(2,1)}, f32[512,256]{1,0:T(8,128)}) custom-call(s32[3]{0:T(128)} %pad_add_fusion.where, s32[8,8]{1,0:T(8,128)} %step.2.bits.in_ref, bf16[256,512]{1,0:T(8,128)(2,1)} %copy-done.6, bf16[256,512]{1,0:T(8,128)(2,1)} %copy-done.8, bf16[256,512]{1,0:T(8,128)(2,1)} %copy-done.9, bf16[256,512]{1,0:T(8,128)(2,1)} %copy-done.10, ...), custom_call_target="tpu_custom_call" | custom-call | flops 20000000000 | bytes 40000000 | tf_op jit(solution)/shard_map/direct/pallas_call | solution.py:128
  80.6 9.2 %all-to-all-start.1 = ((bf16[4,512,256]{2,1,0:T(8,128)(2,1)}), bf16[4,512,256]{2,1,0:T(8,128)(2,1)S(1)}, u32[]{:S(2)}, u32[]{:S(2)}) async-start(bf16[4,512,256]{2,1,0:T(8,128)(2,1)} %get-tuple-element.25), calls=%async_computation.1 | async-start | bytes 2097152 | tf_op jit(solution)/shard_map/all_to_all | solution.py:178
  89.9 1.3 step.3.bits
  91.2 7.4 %mirror.1 = (bf16[4,512,256]{2,1,0:T(8,128)(2,1)}, f32[512,256]{1,0:T(8,128)}) custom-call(s32[3]{0:T(128)} %pad_add_fusion.where, s32[8,8]{1,0:T(8,128)} %step.3.bits, bf16[512,256]{1,0:T(8,128)(2,1)} %copy-done.2, bf16[512,256]{1,0:T(8,128)(2,1)} %copy-done.11, bf16[512,256]{1,0:T(8,128)(2,1)} %copy-done.12, bf16[512,256]{1,0:T(8,128)(2,1)} %copy-done.13, ...), custom_call_target="tpu_custom_call" | custom-call | flops 20000000000 | bytes 40000000 | tf_op jit(solution)/shard_map/mirror/pallas_call | solution.py:128
  98.5 5.6 %all-to-all-done.1 = bf16[4,512,256]{2,1,0:T(8,128)(2,1)S(1)} async-done(((bf16[4,512,256]{2,1,0:T(8,128)(2,1)}), bf16[4,512,256]{2,1,0:T(8,128)(2,1)S(1)}, u32[]{:S(2)}, u32[]{:S(2)}) %all-to-all-start.1) | async-done | bytes 1048608 | tf_op jit(solution)/shard_map/all_to_all | solution.py:178
  104.6 8.4 %collective-permute-start.10 = (bf16[256,256]{1,0:T(8,128)(2,1)S(1)}, bf16[256,256]{1,0:T(8,128)(2,1)S(1)}, u32[]{:S(2)}, u32[]{:S(2)}) collective-permute-start(bf16[256,256]{1,0:T(8,128)(2,1)S(1)} %get-tuple-element.35), channel_id=1, source_target_pairs={{0,1},{1,0},{2,33},{3,32},{4,65},{5,64},{6,97},{7,96},{8,129},{9,1... | collective-permute-start | bytes 393224 | tf_op jit(solution)/shard_map/ppermute | solution.py:33
  113.0 5.4 %collective-permute-start.9 = (bf16[256,256]{1,0:T(8,128)(2,1)S(1)}, bf16[256,256]{1,0:T(8,128)(2,1)S(1)}, u32[]{:S(2)}, u32[]{:S(2)}) collective-permute-start(bf16[256,256]{1,0:T(8,128)(2,1)S(1)} %get-tuple-element.34), channel_id=1, source_target_pairs={{0,0},{1,1},{2,32},{3,33},{4,64},{5,65},{6,96},{7,97},{8,128},{9,1... | collective-permute-start | bytes 393224 | tf_op jit(solution)/shard_map/ppermute | solution.py:33
  119.1 7.0 %all-to-all-start.2 = ((bf16[4,512,256]{2,1,0:T(8,128)(2,1)}), bf16[4,512,256]{2,1,0:T(8,128)(2,1)S(1)}, u32[]{:S(2)}, u32[]{:S(2)}) async-start(bf16[4,512,256]{2,1,0:T(8,128)(2,1)} %get-tuple-element.37), calls=%async_computation.2 | async-start | bytes 2097152 | tf_op jit(solution)/shard_map/all_to_all | solution.py:178
  126.1 0.9 collective-permute-done.10.there_ref
  127.0 3.5 %collective-permute-done.9.here_ref = bf16[256,256]{1,0:T(8,128)(2,1)S(1)} collective-permute-done((bf16[256,256]{1,0:T(8,128)(2,1)S(1)}, bf16[256,256]{1,0:T(8,128)(2,1)S(1)}, u32[]{:S(2)}, u32[]{:S(2)}) %collective-permute-start.9) | collective-permute-done | bytes 131104 | tf_op jit(solution)/shard_map/ppermute | solution.py:33
  131.2 2.2 %base.1 = f32[512,256]{1,0:T(8,128)} custom-call(s32[1]{0:T(128)} %bitcast.co, f32[1]{0:T(128)} %copy.13.energy, bf16[256,256]{1,0:T(8,128)(2,1)} %copy-done.15, bf16[256,256]{1,0:T(8,128)(2,1)} %copy-done.14, f32[512,256]{1,0:T(8,128)} %coeffs_ref.1, f32[512,256]{1,0:T(8,128)} %diag_ref.1), custom_call_target="tpu_custom_call" | custom-call | flops 20000000000 | bytes 40000000 | tf_op jit(solution)/shard_map/base/pallas_call | solution.py:151
  133.4 16.2 %all-to-all-done.2 = bf16[4,512,256]{2,1,0:T(8,128)(2,1)S(1)} async-done(((bf16[4,512,256]{2,1,0:T(8,128)(2,1)}), bf16[4,512,256]{2,1,0:T(8,128)(2,1)S(1)}, u32[]{:S(2)}, u32[]{:S(2)}) %all-to-all-start.2) | async-done | bytes 1048608 | tf_op jit(solution)/shard_map/all_to_all | solution.py:178
  150.0 2.0 %maximum_divide_fusion = f32[512,256]{1,0:T(8,128)} fusion(f32[512,256]{1,0:T(8,128)S(1)} %copy-done.4, f32[512,256]{1,0:T(8,128)} %base.1, f32[512,256]{1,0:T(8,128)S(1)} %copy-done.5, f32[512,256]{1,0:T(8,128)S(1)} %convert_reduce_fusion, f32[]{:T(128)} %bitcast.5), kind=kLoop, calls=%fused_computation.2 | loop fusion | flops 786432 | bytes 2621444 | tf_op jit(solution)/shard_map/div | solution.py:234
  (54 shorter events, 4.1 us)
Async XLA Ops:
  0.0 16.4 %copy-start = (s32[64,24]{0,1:T(8,128)S(1)}, s32[64,24]{0,1:T(8,128)}, u32[]{:S(2)}) copy-start(s32[64,24]{0,1:T(8,128)} %param.10) | copy-start | bytes 18436
  1.1 68.0 %copy-start.2 = (bf16[512,256]{1,0:T(8,128)(2,1)}, bf16[512,256]{1,0:T(8,128)(2,1)S(1)}, u32[]{:S(2)}) copy-start(bf16[512,256]{1,0:T(8,128)(2,1)S(1)} %convert_element_type.16.t0) | copy-start | bytes 786436
  1.1 27.8 %collective-permute-start = (bf16[256,256]{1,0:T(8,128)(2,1)S(1)}, bf16[256,256]{1,0:T(8,128)(2,1)S(1)}, u32[]{:S(2)}, u32[]{:S(2)}) collective-permute-start(bf16[256,256]{1,0:T(8,128)(2,1)S(1)} %get-tuple-element.41), channel_id=1, source_target_pairs={{0,0},{1,1},{2,32},{3,33},{4,64},{5,65},{6,96},{7,97},{8,128},{9,1... | collective-permute-start | bytes 393224 | tf_op jit(solution)/shard_map/ppermute | solution.py:33
  13.9 18.3 %collective-permute-start.1 = (bf16[256,256]{1,0:T(8,128)(2,1)S(1)}, bf16[256,256]{1,0:T(8,128)(2,1)S(1)}, u32[]{:S(2)}, u32[]{:S(2)}) collective-permute-start(bf16[256,256]{1,0:T(8,128)(2,1)S(1)} %get-tuple-element.42), channel_id=1, source_target_pairs={{0,1},{1,0},{2,33},{3,32},{4,65},{5,64},{6,97},{7,96},{8,129},{9,1... | collective-permute-start | bytes 393224 | tf_op jit(solution)/shard_map/ppermute | solution.py:33
  22.3 38.6 %all-to-all-start = ((bf16[4,8,128,256]{3,2,1,0:T(8,128)(2,1)}), bf16[4,8,128,256]{3,2,1,0:T(8,128)(2,1)S(1)}, u32[]{:S(2)}, u32[]{:S(2)}) async-start(bf16[4,8,128,256]{3,2,1,0:T(8,128)(2,1)} %bitcast.6), calls=%async_computation | async-start | bytes 4194304 | tf_op jit(solution)/shard_map/all_to_all | solution.py:209
  32.3 24.5 %copy-start.6 = (bf16[256,512]{1,0:T(8,128)(2,1)}, bf16[256,512]{1,0:T(8,128)(2,1)S(1)}, u32[]{:S(2)}) copy-start(bf16[256,512]{1,0:T(8,128)(2,1)S(1)} %maximum_select_fusion.t0) | copy-start | bytes 786436
  32.3 20.6 %collective-permute-start.2 = (bf16[256,512]{1,0:T(8,128)(2,1)S(1)}, bf16[256,512]{1,0:T(8,128)(2,1)S(1)}, u32[]{:S(2)}, u32[]{:S(2)}) collective-permute-start(bf16[256,512]{1,0:T(8,128)(2,1)S(1)} %maximum_select_fusion.t0), channel_id=1, source_target_pairs={{0,128},{128,256},{256,384},{384,0},{1,129},{129,257},{257,385},{3... | collective-permute-start | bytes 786440 | tf_op jit(solution)/shard_map/ppermute | solution.py:19
  34.2 18.7 %collective-permute-start.3 = (bf16[256,512]{1,0:T(8,128)(2,1)S(1)}, bf16[256,512]{1,0:T(8,128)(2,1)S(1)}, u32[]{:S(2)}, u32[]{:S(2)}) collective-permute-start(bf16[256,512]{1,0:T(8,128)(2,1)S(1)} %maximum_select_fusion.t0), channel_id=1, source_target_pairs={{0,256},{128,384},{256,0},{384,128},{1,257},{129,385},{257,1},{385... | collective-permute-start | bytes 786440 | tf_op jit(solution)/shard_map/ppermute | solution.py:19
  36.2 19.3 %collective-permute-start.4 = (bf16[256,512]{1,0:T(8,128)(2,1)S(1)}, bf16[256,512]{1,0:T(8,128)(2,1)S(1)}, u32[]{:S(2)}, u32[]{:S(2)}) collective-permute-start(bf16[256,512]{1,0:T(8,128)(2,1)S(1)} %maximum_select_fusion.t0), channel_id=1, source_target_pairs={{0,384},{128,0},{256,128},{384,256},{1,385},{129,1},{257,129},{385... | collective-permute-start | bytes 786440 | tf_op jit(solution)/shard_map/ppermute | solution.py:19
  52.9 3.9 %copy-start.8 = (bf16[256,512]{1,0:T(8,128)(2,1)}, bf16[256,512]{1,0:T(8,128)(2,1)S(1)}, u32[]{:S(2)}) copy-start(bf16[256,512]{1,0:T(8,128)(2,1)S(1)} %collective-permute-done.2.t1) | copy-start | bytes 786436
  52.9 3.9 %copy-start.9 = (bf16[256,512]{1,0:T(8,128)(2,1)}, bf16[256,512]{1,0:T(8,128)(2,1)S(1)}, u32[]{:S(2)}) copy-start(bf16[256,512]{1,0:T(8,128)(2,1)S(1)} %collective-permute-done.3.t2) | copy-start | bytes 786436
  55.5 1.3 copy-start.10
  60.9 11.3 %copy-start.1 = (bf16[4,8,128,256]{3,2,1,0:T(8,128)(2,1)}, bf16[4,8,128,256]{3,2,1,0:T(8,128)(2,1)S(1)}, u32[]{:S(2)}) copy-start(bf16[4,8,128,256]{3,2,1,0:T(8,128)(2,1)S(1)} %all-to-all-done.own_ref) | copy-start | bytes 6291460
  60.9 11.3 %collective-permute-start.5 = (bf16[4,8,128,256]{3,2,1,0:T(8,128)(2,1)S(1)}, bf16[4,8,128,256]{3,2,1,0:T(8,128)(2,1)S(1)}, u32[]{:S(2)}, u32[]{:S(2)}) collective-permute-start(bf16[4,8,128,256]{3,2,1,0:T(8,128)(2,1)S(1)} %all-to-all-done.own_ref), channel_id=1, source_target_pairs={{0,1},{1,0},{2,3},{3,2},{4,5},{5,4},{6,7},{7,6},{8,9},{9,8},{10,11... | collective-permute-start | bytes 6291464 | tf_op jit(solution)/shard_map/ppermute | solution.py:23
  64.1 25.8 %collective-permute-start.6 = (bf16[512,256]{1,0:T(8,128)(2,1)S(1)}, bf16[512,256]{1,0:T(8,128)(2,1)S(1)}, u32[]{:S(2)}, u32[]{:S(2)}) collective-permute-start(bf16[512,256]{1,0:T(8,128)(2,1)S(1)} %convert_element_type.16.t0), channel_id=1, source_target_pairs={{0,128},{128,256},{256,384},{384,0},{1,129},{129,257},{257,385},{3... | collective-permute-start | bytes 786440 | tf_op jit(solution)/shard_map/ppermute | solution.py:19
  67.2 22.7 %collective-permute-start.7 = (bf16[512,256]{1,0:T(8,128)(2,1)S(1)}, bf16[512,256]{1,0:T(8,128)(2,1)S(1)}, u32[]{:S(2)}, u32[]{:S(2)}) collective-permute-start(bf16[512,256]{1,0:T(8,128)(2,1)S(1)} %convert_element_type.16.t0), channel_id=1, source_target_pairs={{0,256},{128,384},{256,0},{384,128},{1,257},{129,385},{257,1},{385... | collective-permute-start | bytes 786440 | tf_op jit(solution)/shard_map/ppermute | solution.py:19
  69.1 20.8 %collective-permute-start.8 = (bf16[512,256]{1,0:T(8,128)(2,1)S(1)}, bf16[512,256]{1,0:T(8,128)(2,1)S(1)}, u32[]{:S(2)}, u32[]{:S(2)}) collective-permute-start(bf16[512,256]{1,0:T(8,128)(2,1)S(1)} %convert_element_type.16.t0), channel_id=1, source_target_pairs={{0,384},{128,0},{256,128},{384,256},{1,385},{129,1},{257,129},{385... | collective-permute-start | bytes 786440 | tf_op jit(solution)/shard_map/ppermute | solution.py:19
  72.2 1.3 copy-start.7
  80.6 23.5 %all-to-all-start.1 = ((bf16[4,512,256]{2,1,0:T(8,128)(2,1)}), bf16[4,512,256]{2,1,0:T(8,128)(2,1)S(1)}, u32[]{:S(2)}, u32[]{:S(2)}) async-start(bf16[4,512,256]{2,1,0:T(8,128)(2,1)} %get-tuple-element.25), calls=%async_computation.1 | async-start | bytes 2097152 | tf_op jit(solution)/shard_map/all_to_all | solution.py:178
  89.8 1.3 copy-start.11
  89.8 1.3 copy-start.12
  89.9 1.3 copy-start.13
  91.1 13.3 %copy-start.3 = (f32[512,256]{1,0:T(8,128)S(1)}, f32[512,256]{1,0:T(8,128)}, u32[]{:S(2)}) copy-start(f32[512,256]{1,0:T(8,128)} %get-tuple-element.24) | copy-start | bytes 1572868
  104.6 22.4 %collective-permute-start.10 = (bf16[256,256]{1,0:T(8,128)(2,1)S(1)}, bf16[256,256]{1,0:T(8,128)(2,1)S(1)}, u32[]{:S(2)}, u32[]{:S(2)}) collective-permute-start(bf16[256,256]{1,0:T(8,128)(2,1)S(1)} %get-tuple-element.35), channel_id=1, source_target_pairs={{0,1},{1,0},{2,33},{3,32},{4,65},{5,64},{6,97},{7,96},{8,129},{9,1... | collective-permute-start | bytes 393224 | tf_op jit(solution)/shard_map/ppermute | solution.py:33
  113.0 17.5 %collective-permute-start.9 = (bf16[256,256]{1,0:T(8,128)(2,1)S(1)}, bf16[256,256]{1,0:T(8,128)(2,1)S(1)}, u32[]{:S(2)}, u32[]{:S(2)}) collective-permute-start(bf16[256,256]{1,0:T(8,128)(2,1)S(1)} %get-tuple-element.34), channel_id=1, source_target_pairs={{0,0},{1,1},{2,32},{3,33},{4,64},{5,65},{6,96},{7,97},{8,128},{9,1... | collective-permute-start | bytes 393224 | tf_op jit(solution)/shard_map/ppermute | solution.py:33
  119.1 30.6 %all-to-all-start.2 = ((bf16[4,512,256]{2,1,0:T(8,128)(2,1)}), bf16[4,512,256]{2,1,0:T(8,128)(2,1)S(1)}, u32[]{:S(2)}, u32[]{:S(2)}) async-start(bf16[4,512,256]{2,1,0:T(8,128)(2,1)} %get-tuple-element.37), calls=%async_computation.2 | async-start | bytes 2097152 | tf_op jit(solution)/shard_map/all_to_all | solution.py:178
  126.1 23.9 %copy-start.4 = (f32[512,256]{1,0:T(8,128)S(1)}, f32[512,256]{1,0:T(8,128)}, u32[]{:S(2)}) copy-start(f32[512,256]{1,0:T(8,128)} %diag_ref.1) | copy-start | bytes 1572868
  126.1 23.9 %copy-start.5 = (f32[512,256]{1,0:T(8,128)S(1)}, f32[512,256]{1,0:T(8,128)}, u32[]{:S(2)}) copy-start(f32[512,256]{1,0:T(8,128)} %get-tuple-element.36) | copy-start | bytes 1572868
  127.0 3.5 %copy-start.14 = (bf16[256,256]{1,0:T(8,128)(2,1)}, bf16[256,256]{1,0:T(8,128)(2,1)S(1)}, u32[]{:S(2)}) copy-start(bf16[256,256]{1,0:T(8,128)(2,1)S(1)} %collective-permute-done.10.there_ref) | copy-start | bytes 393220
  130.5 0.7 copy-start.15

commit v10 on v9

--- a/solution.py
+++ b/solution.py
@@ -9,7 +9,7 @@
 ROW = ("zl", "x")
 COL = ("zh", "y", "co")
 W = 128
-STEP = 16_000_000_000
+STEP = 8_000_000_000
 LATE = 2_000_000_000
 VMEM_LIMIT = 56 * 1024 * 1024
 PARAMS = pltpu.CompilerParams(vmem_limit_bytes=VMEM_LIMIT)
@@ -154,7 +154,7 @@
         in_specs=[pl.BlockSpec(memory_space=pltpu.SMEM)] * 2 + [pl.BlockSpec(memory_space=pltpu.VMEM)] * 4,
         out_specs=pl.BlockSpec(memory_space=pltpu.VMEM),
         compiler_params=PARAMS,
-        cost_estimate=pl.CostEstimate(flops=20_000_000_000, bytes_accessed=40_000_000, transcendentals=0),
+        cost_estimate=pl.CostEstimate(flops=1, bytes_accessed=1, transcendentals=0),
         name="base",
     )(co, energy, here, there, coeffs, diag_energy)
 
@@ -211,7 +211,7 @@
     i = jnp.arange(8, dtype=jnp.int32)
     odd = (8 * (i // 2) + 2 * x + i % 2) * 2 + 1
     bits = jnp.any(names == odd[None, :, None], axis=2).astype(jnp.int32)
-    bits = step_kernel(lax.optimization_barrier((bits, *direct_tiles[1:]))[0], STEP)
+    bits = step_kernel(lax.optimization_barrier((bits, *direct_tiles[1:], mirror_tiles[1]))[0], STEP)
     other = swap_cores(lax.optimization_barrier((own, bits))[0])
     here_first = jnp.stack([zl, x, co])
 

time: 153 us -> 152 us (level)
  the two profiles are of different devices: /device:TPU:65 before, /device:TPU:71 now
where the time goes in v10:
time: 152 us
  starting transfers between devices  70.9 us (47%)
  waiting for transfers between devices  47 us (31%)
  Pallas kernels  23.6 us (16%)
  other arithmetic  6.07 us (4%)
  local copies, waits for them, and re-layouts  3.12 us (2%)
    ppermute x4, starting transfers between devices, turned(): return lax.ppermute(value, AXES, pairs)  36.1 us
    ppermute x4, waiting for transfers between devices, turned(): return lax.ppermute(value, AXES, pairs)  22.7 us
    ppermute x6, waiting for transfers between devices, shifted(): return lax.ppermute(value, axis, [(i, (i + step) % 4) for i in range(4)])  20.3 us
    ppermute x6, starting transfers between devices, shifted(): return lax.ppermute(value, axis, [(i, (i + step) % 4) for i in range(4)])  15.1 us
    pallas_call x2, Pallas kernels, partial_sums(): pl.pallas_call(kernel, out_shape=(jax.ShapeDtypeStruct((4, *shape), jnp.b...  14.4 us
    all_to_all x2, starting transfers between devices, exchanged(): return lax.all_to_all(parts, 'x', 0, 0, tiled=True)  11.3 us
    all_to_all x1, starting transfers between devices, on_device(): own = lax.all_to_all(packed.reshape(4, 8, W, 2 * W), 'x', 0, 0, tiled=True)  4.45 us
    pallas_call x1, Pallas kernels, pack(): pl.pallas_call(pack_kernel, out_shape=jax.ShapeDtypeStruct((32, W, 2 * W)...  4.4 us
  transfers between devices with their start and end apart: 14, of which 7 were waited for; matrix products, arithmetic and copies ran while one was open for 2% of the time, Pallas kernels for 16%

profile of v10, /device:TPU:71, one launch (start us, length us, event | category | flops | bytes accessed | tf_op | source)
XLA Modules:
  0.0 151.6 jit_solution(3526391827204010838)
XLA Ops:
  0.0 1.1 convert_element_type.16.t0
  1.1 15.1 %collective-permute-start = (bf16[256,256]{1,0:T(8,128)(2,1)S(1)}, bf16[256,256]{1,0:T(8,128)(2,1)S(1)}, u32[]{:S(2)}, u32[]{:S(2)}) collective-permute-start(bf16[256,256]{1,0:T(8,128)(2,1)S(1)} %get-tuple-element.41), channel_id=1, source_target_pairs={{0,0},{1,1},{2,32},{3,33},{4,64},{5,65},{6,96},{7,97},{8,128},{9,1... | collective-permute-start | bytes 393224 | tf_op jit(solution)/shard_map/ppermute | solution.py:33
  16.2 2.5 %collective-permute-start.1 = (bf16[256,256]{1,0:T(8,128)(2,1)S(1)}, bf16[256,256]{1,0:T(8,128)(2,1)S(1)}, u32[]{:S(2)}, u32[]{:S(2)}) collective-permute-start(bf16[256,256]{1,0:T(8,128)(2,1)S(1)} %get-tuple-element.42), channel_id=1, source_target_pairs={{0,1},{1,0},{2,33},{3,32},{4,65},{5,64},{6,97},{7,96},{8,129},{9,1... | collective-permute-start | bytes 393224 | tf_op jit(solution)/shard_map/ppermute | solution.py:33
  18.9 0.7 dynamic-slice
  19.6 0.6 compare_select_fusion.pos
  20.3 4.4 %pack.1 = bf16[32,128,256]{2,1,0:T(8,128)(2,1)} custom-call(s32[2,24]{1,0:T(2,128)} %compare_select_fusion.pos, s32[1]{0:T(128)} %bitcast.co, bf16[4,24,128,128]{3,2,1,0:T(8,128)(2,1)} %h_ref.1), custom_call_target="tpu_custom_call" | custom-call | tf_op jit(solution)/shard_map/pack/pallas_call | solution.py:54
  24.7 4.5 %all-to-all-start = ((bf16[4,8,128,256]{3,2,1,0:T(8,128)(2,1)}), bf16[4,8,128,256]{3,2,1,0:T(8,128)(2,1)S(1)}, u32[]{:S(2)}, u32[]{:S(2)}) async-start(bf16[4,8,128,256]{3,2,1,0:T(8,128)(2,1)} %bitcast.6), calls=%async_computation | async-start | bytes 4194304 | tf_op jit(solution)/shard_map/all_to_all | solution.py:209
  29.1 7.3 %collective-permute-done.1 = bf16[256,256]{1,0:T(8,128)(2,1)S(1)} collective-permute-done((bf16[256,256]{1,0:T(8,128)(2,1)S(1)}, bf16[256,256]{1,0:T(8,128)(2,1)S(1)}, u32[]{:S(2)}, u32[]{:S(2)}) %collective-permute-start.1) | collective-permute-done | bytes 131104 | tf_op jit(solution)/shard_map/ppermute | solution.py:33
  36.6 2.6 %collective-permute-start.2 = (bf16[256,512]{1,0:T(8,128)(2,1)S(1)}, bf16[256,512]{1,0:T(8,128)(2,1)S(1)}, u32[]{:S(2)}, u32[]{:S(2)}) collective-permute-start(bf16[256,512]{1,0:T(8,128)(2,1)S(1)} %maximum_select_fusion.t0), channel_id=1, source_target_pairs={{0,128},{128,256},{256,384},{384,0},{1,129},{129,257},{257,385},{3... | collective-permute-start | bytes 786440 | tf_op jit(solution)/shard_map/ppermute | solution.py:19
  39.1 1.9 %collective-permute-start.3 = (bf16[256,512]{1,0:T(8,128)(2,1)S(1)}, bf16[256,512]{1,0:T(8,128)(2,1)}, u32[]{:S(2)}, u32[]{:S(2)}) collective-permute-start(bf16[256,512]{1,0:T(8,128)(2,1)S(1)} %maximum_select_fusion.t0), channel_id=1, source_target_pairs={{0,256},{128,384},{256,0},{384,128},{1,257},{129,385},{257,1},{385... | collective-permute-start | bytes 786440 | tf_op jit(solution)/shard_map/ppermute | solution.py:19
  41.1 3.1 %collective-permute-start.4 = (bf16[256,512]{1,0:T(8,128)(2,1)S(1)}, bf16[256,512]{1,0:T(8,128)(2,1)}, u32[]{:S(2)}, u32[]{:S(2)}) collective-permute-start(bf16[256,512]{1,0:T(8,128)(2,1)S(1)} %maximum_select_fusion.t0), channel_id=1, source_target_pairs={{0,384},{128,0},{256,128},{384,256},{1,385},{129,1},{257,129},{385... | collective-permute-start | bytes 786440 | tf_op jit(solution)/shard_map/ppermute | solution.py:19
  44.2 11.1 %collective-permute-done.2.t1 = bf16[256,512]{1,0:T(8,128)(2,1)S(1)} collective-permute-done((bf16[256,512]{1,0:T(8,128)(2,1)S(1)}, bf16[256,512]{1,0:T(8,128)(2,1)S(1)}, u32[]{:S(2)}, u32[]{:S(2)}) %collective-permute-start.2) | collective-permute-done | bytes 262176 | tf_op jit(solution)/shard_map/ppermute | solution.py:19
  55.3 1.9 %collective-permute-start.5 = (bf16[512,256]{1,0:T(8,128)(2,1)S(1)}, bf16[512,256]{1,0:T(8,128)(2,1)S(1)}, u32[]{:S(2)}, u32[]{:S(2)}) collective-permute-start(bf16[512,256]{1,0:T(8,128)(2,1)S(1)} %convert_element_type.16.t0), channel_id=1, source_target_pairs={{0,128},{128,256},{256,384},{384,0},{1,129},{129,257},{257,385},{3... | collective-permute-start | bytes 786440 | tf_op jit(solution)/shard_map/ppermute | solution.py:19
  58.3 9.1 %collective-permute-done.4.t3 = bf16[256,512]{1,0:T(8,128)(2,1)} collective-permute-done((bf16[256,512]{1,0:T(8,128)(2,1)S(1)}, bf16[256,512]{1,0:T(8,128)(2,1)}, u32[]{:S(2)}, u32[]{:S(2)}) %collective-permute-start.4) | collective-permute-done | bytes 262176 | tf_op jit(solution)/shard_map/ppermute | solution.py:19
  67.6 1.3 step.2.bits.in_ref
  68.9 4.0 %collective-permute-start.6 = (bf16[4,8,128,256]{3,2,1,0:T(8,128)(2,1)S(1)}, bf16[4,8,128,256]{3,2,1,0:T(8,128)(2,1)S(1)}, u32[]{:S(2)}, u32[]{:S(2)}) collective-permute-start(bf16[4,8,128,256]{3,2,1,0:T(8,128)(2,1)S(1)} %all-to-all-done.own_ref), channel_id=1, source_target_pairs={{0,1},{1,0},{2,3},{3,2},{4,5},{5,4},{6,7},{7,6},{8,9},{9,8},{10,11... | collective-permute-start | bytes 6291464 | tf_op jit(solution)/shard_map/ppermute | solution.py:23
  73.6 1.9 %collective-permute-start.7 = (bf16[512,256]{1,0:T(8,128)(2,1)S(1)}, bf16[512,256]{1,0:T(8,128)(2,1)S(1)}, u32[]{:S(2)}, u32[]{:S(2)}) collective-permute-start(bf16[512,256]{1,0:T(8,128)(2,1)S(1)} %convert_element_type.16.t0), channel_id=1, source_target_pairs={{0,256},{128,384},{256,0},{384,128},{1,257},{129,385},{257,1},{385... | collective-permute-start | bytes 786440 | tf_op jit(solution)/shard_map/ppermute | solution.py:19
  75.5 3.7 %collective-permute-start.8 = (bf16[512,256]{1,0:T(8,128)(2,1)S(1)}, bf16[512,256]{1,0:T(8,128)(2,1)S(1)}, u32[]{:S(2)}, u32[]{:S(2)}) collective-permute-start(bf16[512,256]{1,0:T(8,128)(2,1)S(1)} %convert_element_type.16.t0), channel_id=1, source_target_pairs={{0,384},{128,0},{256,128},{384,256},{1,385},{129,1},{257,129},{385... | collective-permute-start | bytes 786440 | tf_op jit(solution)/shard_map/ppermute | solution.py:19
  79.2 1.3 copy-done.9
  80.5 7.1 %direct.1 = (bf16[4,512,256]{2,1,0:T(8,128)(2,1)}, f32[512,256]{1,0:T(8,128)}) custom-call(s32[3]{0:T(128)} %pad_add_fusion.where, s32[8,8]{1,0:T(8,128)} %step.2.bits.in_ref, bf16[256,512]{1,0:T(8,128)(2,1)} %copy-done.6, bf16[256,512]{1,0:T(8,128)(2,1)} %copy-done.10, bf16[256,512]{1,0:T(8,128)(2,1)} %collective-permute-done.3.t2, ...), custom_call_target="tpu_custom_call" | custom-call | flops 20000000000 | bytes 40000000 | tf_op jit(solution)/shard_map/direct/pallas_call | solution.py:128
  87.6 6.0 %all-to-all-start.1 = ((bf16[4,512,256]{2,1,0:T(8,128)(2,1)}), bf16[4,512,256]{2,1,0:T(8,128)(2,1)S(1)}, u32[]{:S(2)}, u32[]{:S(2)}) async-start(bf16[4,512,256]{2,1,0:T(8,128)(2,1)} %get-tuple-element.26), calls=%async_computation.1 | async-start | bytes 2097152 | tf_op jit(solution)/shard_map/all_to_all | solution.py:178
  93.7 1.3 step.3.bits
  94.9 7.3 %mirror.1 = (bf16[4,512,256]{2,1,0:T(8,128)(2,1)}, f32[512,256]{1,0:T(8,128)}) custom-call(s32[3]{0:T(128)} %pad_add_fusion.where, s32[8,8]{1,0:T(8,128)} %step.3.bits, bf16[512,256]{1,0:T(8,128)(2,1)} %copy-done.3, bf16[512,256]{1,0:T(8,128)(2,1)} %copy-done.11, bf16[512,256]{1,0:T(8,128)(2,1)} %copy-done.12, bf16[512,256]{1,0:T(8,128)(2,1)} %copy-done.13, ...), custom_call_target="tpu_custom_call" | custom-call | flops 20000000000 | bytes 40000000 | tf_op jit(solution)/shard_map/mirror/pallas_call | solution.py:128
  102.2 3.9 %all-to-all-done.1 = bf16[4,512,256]{2,1,0:T(8,128)(2,1)S(1)} async-done(((bf16[4,512,256]{2,1,0:T(8,128)(2,1)}), bf16[4,512,256]{2,1,0:T(8,128)(2,1)S(1)}, u32[]{:S(2)}, u32[]{:S(2)}) %all-to-all-start.1) | async-done | bytes 1048608 | tf_op jit(solution)/shard_map/all_to_all | solution.py:178
  106.1 5.3 %all-to-all-start.2 = ((bf16[4,512,256]{2,1,0:T(8,128)(2,1)}), bf16[4,512,256]{2,1,0:T(8,128)(2,1)S(1)}, u32[]{:S(2)}, u32[]{:S(2)}) async-start(bf16[4,512,256]{2,1,0:T(8,128)(2,1)} %get-tuple-element.37), calls=%async_computation.2 | async-start | bytes 2097152 | tf_op jit(solution)/shard_map/all_to_all | solution.py:178
  111.9 10.6 %collective-permute-start.10 = (bf16[256,256]{1,0:T(8,128)(2,1)S(1)}, bf16[256,256]{1,0:T(8,128)(2,1)S(1)}, u32[]{:S(2)}, u32[]{:S(2)}) collective-permute-start(bf16[256,256]{1,0:T(8,128)(2,1)S(1)} %get-tuple-element.35), channel_id=1, source_target_pairs={{0,1},{1,0},{2,33},{3,32},{4,65},{5,64},{6,97},{7,96},{8,129},{9,1... | collective-permute-start | bytes 393224 | tf_op jit(solution)/shard_map/ppermute | solution.py:33
  122.4 7.9 %collective-permute-start.9 = (bf16[256,256]{1,0:T(8,128)(2,1)S(1)}, bf16[256,256]{1,0:T(8,128)(2,1)S(1)}, u32[]{:S(2)}, u32[]{:S(2)}) collective-permute-start(bf16[256,256]{1,0:T(8,128)(2,1)S(1)} %get-tuple-element.34), channel_id=1, source_target_pairs={{0,0},{1,1},{2,32},{3,33},{4,64},{5,65},{6,96},{7,97},{8,128},{9,1... | collective-permute-start | bytes 393224 | tf_op jit(solution)/shard_map/ppermute | solution.py:33
  131.0 8.6 %collective-permute-done.10.there_ref = bf16[256,256]{1,0:T(8,128)(2,1)S(1)} collective-permute-done((bf16[256,256]{1,0:T(8,128)(2,1)S(1)}, bf16[256,256]{1,0:T(8,128)(2,1)S(1)}, u32[]{:S(2)}, u32[]{:S(2)}) %collective-permute-start.10) | collective-permute-done | bytes 131104 | tf_op jit(solution)/shard_map/ppermute | solution.py:33
  139.6 6.8 %collective-permute-done.9.here_ref = bf16[256,256]{1,0:T(8,128)(2,1)S(1)} collective-permute-done((bf16[256,256]{1,0:T(8,128)(2,1)S(1)}, bf16[256,256]{1,0:T(8,128)(2,1)S(1)}, u32[]{:S(2)}, u32[]{:S(2)}) %collective-permute-start.9) | collective-permute-done | bytes 131104 | tf_op jit(solution)/shard_map/ppermute | solution.py:33
  146.4 0.7 copy-done.8
  147.0 2.2 %base.1 = f32[512,256]{1,0:T(8,128)} custom-call(s32[1]{0:T(128)} %bitcast.co, f32[1]{0:T(128)} %copy.13.energy, bf16[256,256]{1,0:T(8,128)(2,1)} %copy-done.8, bf16[256,256]{1,0:T(8,128)(2,1)} %copy-done.7, f32[512,256]{1,0:T(8,128)} %coeffs_ref.1, f32[512,256]{1,0:T(8,128)} %diag_ref.1), custom_call_target="tpu_custom_call" | custom-call | flops 1 | bytes 1 | tf_op jit(solution)/shard_map/base/pallas_call | solution.py:151
  149.6 2.0 %maximum_divide_fusion = f32[512,256]{1,0:T(8,128)} fusion(f32[512,256]{1,0:T(8,128)S(1)} %copy-done.2, f32[512,256]{1,0:T(8,128)} %base.1, f32[512,256]{1,0:T(8,128)S(1)} %copy-done.5, f32[512,256]{1,0:T(8,128)S(1)} %convert_reduce_fusion, f32[]{:T(128)} %bitcast.5), kind=kLoop, calls=%fused_computation.2 | loop fusion | flops 786432 | bytes 2621444 | tf_op jit(solution)/shard_map/div | solution.py:234
  (50 shorter events, 3.0 us)
Async XLA Ops:
  0.0 18.7 %copy-start = (s32[64,24]{0,1:T(8,128)S(1)}, s32[64,24]{0,1:T(8,128)}, u32[]{:S(2)}) copy-start(s32[64,24]{0,1:T(8,128)} %param.10) | copy-start | bytes 18436
  1.1 74.4 %copy-start.3 = (bf16[512,256]{1,0:T(8,128)(2,1)}, bf16[512,256]{1,0:T(8,128)(2,1)S(1)}, u32[]{:S(2)}) copy-start(bf16[512,256]{1,0:T(8,128)(2,1)S(1)} %convert_element_type.16.t0) | copy-start | bytes 786436
  1.1 28.0 %collective-permute-start = (bf16[256,256]{1,0:T(8,128)(2,1)S(1)}, bf16[256,256]{1,0:T(8,128)(2,1)S(1)}, u32[]{:S(2)}, u32[]{:S(2)}) collective-permute-start(bf16[256,256]{1,0:T(8,128)(2,1)S(1)} %get-tuple-element.41), channel_id=1, source_target_pairs={{0,0},{1,1},{2,32},{3,33},{4,64},{5,65},{6,96},{7,97},{8,128},{9,1... | collective-permute-start | bytes 393224 | tf_op jit(solution)/shard_map/ppermute | solution.py:33
  16.2 20.2 %collective-permute-start.1 = (bf16[256,256]{1,0:T(8,128)(2,1)S(1)}, bf16[256,256]{1,0:T(8,128)(2,1)S(1)}, u32[]{:S(2)}, u32[]{:S(2)}) collective-permute-start(bf16[256,256]{1,0:T(8,128)(2,1)S(1)} %get-tuple-element.42), channel_id=1, source_target_pairs={{0,1},{1,0},{2,33},{3,32},{4,65},{5,64},{6,97},{7,96},{8,129},{9,1... | collective-permute-start | bytes 393224 | tf_op jit(solution)/shard_map/ppermute | solution.py:33
  24.7 44.2 %all-to-all-start = ((bf16[4,8,128,256]{3,2,1,0:T(8,128)(2,1)}), bf16[4,8,128,256]{3,2,1,0:T(8,128)(2,1)S(1)}, u32[]{:S(2)}, u32[]{:S(2)}) async-start(bf16[4,8,128,256]{3,2,1,0:T(8,128)(2,1)} %bitcast.6), calls=%async_computation | async-start | bytes 4194304 | tf_op jit(solution)/shard_map/all_to_all | solution.py:209
  36.6 32.3 %copy-start.6 = (bf16[256,512]{1,0:T(8,128)(2,1)}, bf16[256,512]{1,0:T(8,128)(2,1)S(1)}, u32[]{:S(2)}) copy-start(bf16[256,512]{1,0:T(8,128)(2,1)S(1)} %maximum_select_fusion.t0) | copy-start | bytes 786436
  36.6 18.7 %collective-permute-start.2 = (bf16[256,512]{1,0:T(8,128)(2,1)S(1)}, bf16[256,512]{1,0:T(8,128)(2,1)S(1)}, u32[]{:S(2)}, u32[]{:S(2)}) collective-permute-start(bf16[256,512]{1,0:T(8,128)(2,1)S(1)} %maximum_select_fusion.t0), channel_id=1, source_target_pairs={{0,128},{128,256},{256,384},{384,0},{1,129},{129,257},{257,385},{3... | collective-permute-start | bytes 786440 | tf_op jit(solution)/shard_map/ppermute | solution.py:19
  39.1 19.2 %collective-permute-start.3 = (bf16[256,512]{1,0:T(8,128)(2,1)S(1)}, bf16[256,512]{1,0:T(8,128)(2,1)}, u32[]{:S(2)}, u32[]{:S(2)}) collective-permute-start(bf16[256,512]{1,0:T(8,128)(2,1)S(1)} %maximum_select_fusion.t0), channel_id=1, source_target_pairs={{0,256},{128,384},{256,0},{384,128},{1,257},{129,385},{257,1},{385... | collective-permute-start | bytes 786440 | tf_op jit(solution)/shard_map/ppermute | solution.py:19
  41.1 26.3 %collective-permute-start.4 = (bf16[256,512]{1,0:T(8,128)(2,1)S(1)}, bf16[256,512]{1,0:T(8,128)(2,1)}, u32[]{:S(2)}, u32[]{:S(2)}) collective-permute-start(bf16[256,512]{1,0:T(8,128)(2,1)S(1)} %maximum_select_fusion.t0), channel_id=1, source_target_pairs={{0,384},{128,0},{256,128},{384,256},{1,385},{129,1},{257,129},{385... | collective-permute-start | bytes 786440 | tf_op jit(solution)/shard_map/ppermute | solution.py:19
  55.3 13.6 %copy-start.10 = (bf16[256,512]{1,0:T(8,128)(2,1)}, bf16[256,512]{1,0:T(8,128)(2,1)S(1)}, u32[]{:S(2)}) copy-start(bf16[256,512]{1,0:T(8,128)(2,1)S(1)} %collective-permute-done.2.t1) | copy-start | bytes 786436
  55.3 12.3 %collective-permute-start.5 = (bf16[512,256]{1,0:T(8,128)(2,1)S(1)}, bf16[512,256]{1,0:T(8,128)(2,1)S(1)}, u32[]{:S(2)}, u32[]{:S(2)}) collective-permute-start(bf16[512,256]{1,0:T(8,128)(2,1)S(1)} %convert_element_type.16.t0), channel_id=1, source_target_pairs={{0,128},{128,256},{256,384},{384,0},{1,129},{129,257},{257,385},{3... | collective-permute-start | bytes 786440 | tf_op jit(solution)/shard_map/ppermute | solution.py:19
  67.6 1.3 copy-start.11
  68.9 10.3 %copy-start.1 = (bf16[4,8,128,256]{3,2,1,0:T(8,128)(2,1)}, bf16[4,8,128,256]{3,2,1,0:T(8,128)(2,1)S(1)}, u32[]{:S(2)}) copy-start(bf16[4,8,128,256]{3,2,1,0:T(8,128)(2,1)S(1)} %all-to-all-done.own_ref) | copy-start | bytes 6291460
  68.9 10.3 %collective-permute-start.6 = (bf16[4,8,128,256]{3,2,1,0:T(8,128)(2,1)S(1)}, bf16[4,8,128,256]{3,2,1,0:T(8,128)(2,1)S(1)}, u32[]{:S(2)}, u32[]{:S(2)}) collective-permute-start(bf16[4,8,128,256]{3,2,1,0:T(8,128)(2,1)S(1)} %all-to-all-done.own_ref), channel_id=1, source_target_pairs={{0,1},{1,0},{2,3},{3,2},{4,5},{5,4},{6,7},{7,6},{8,9},{9,8},{10,11... | collective-permute-start | bytes 6291464 | tf_op jit(solution)/shard_map/ppermute | solution.py:23
  73.6 20.1 %collective-permute-start.7 = (bf16[512,256]{1,0:T(8,128)(2,1)S(1)}, bf16[512,256]{1,0:T(8,128)(2,1)S(1)}, u32[]{:S(2)}, u32[]{:S(2)}) collective-permute-start(bf16[512,256]{1,0:T(8,128)(2,1)S(1)} %convert_element_type.16.t0), channel_id=1, source_target_pairs={{0,256},{128,384},{256,0},{384,128},{1,257},{129,385},{257,1},{385... | collective-permute-start | bytes 786440 | tf_op jit(solution)/shard_map/ppermute | solution.py:19
  75.5 18.2 %collective-permute-start.8 = (bf16[512,256]{1,0:T(8,128)(2,1)S(1)}, bf16[512,256]{1,0:T(8,128)(2,1)S(1)}, u32[]{:S(2)}, u32[]{:S(2)}) collective-permute-start(bf16[512,256]{1,0:T(8,128)(2,1)S(1)} %convert_element_type.16.t0), channel_id=1, source_target_pairs={{0,384},{128,0},{256,128},{384,256},{1,385},{129,1},{257,129},{385... | collective-permute-start | bytes 786440 | tf_op jit(solution)/shard_map/ppermute | solution.py:19
  79.2 1.3 copy-start.9
  87.6 18.5 %all-to-all-start.1 = ((bf16[4,512,256]{2,1,0:T(8,128)(2,1)}), bf16[4,512,256]{2,1,0:T(8,128)(2,1)S(1)}, u32[]{:S(2)}, u32[]{:S(2)}) async-start(bf16[4,512,256]{2,1,0:T(8,128)(2,1)} %get-tuple-element.26), calls=%async_computation.1 | async-start | bytes 2097152 | tf_op jit(solution)/shard_map/all_to_all | solution.py:178
  93.6 1.3 copy-start.12
  93.7 1.3 copy-start.13
  102.2 9.5 %copy-start.4 = (f32[512,256]{1,0:T(8,128)S(1)}, f32[512,256]{1,0:T(8,128)}, u32[]{:S(2)}) copy-start(f32[512,256]{1,0:T(8,128)} %get-tuple-element.25) | copy-start | bytes 1572868
  106.1 43.1 %all-to-all-start.2 = ((bf16[4,512,256]{2,1,0:T(8,128)(2,1)}), bf16[4,512,256]{2,1,0:T(8,128)(2,1)S(1)}, u32[]{:S(2)}, u32[]{:S(2)}) async-start(bf16[4,512,256]{2,1,0:T(8,128)(2,1)} %get-tuple-element.37), calls=%async_computation.2 | async-start | bytes 2097152 | tf_op jit(solution)/shard_map/all_to_all | solution.py:178
  111.8 37.8 %copy-start.2 = (f32[512,256]{1,0:T(8,128)S(1)}, f32[512,256]{1,0:T(8,128)}, u32[]{:S(2)}) copy-start(f32[512,256]{1,0:T(8,128)} %diag_ref.1) | copy-start | bytes 1572868
  111.8 37.8 %copy-start.5 = (f32[512,256]{1,0:T(8,128)S(1)}, f32[512,256]{1,0:T(8,128)}, u32[]{:S(2)}) copy-start(f32[512,256]{1,0:T(8,128)} %get-tuple-element.36) | copy-start | bytes 1572868
  111.9 27.7 %collective-permute-start.10 = (bf16[256,256]{1,0:T(8,128)(2,1)S(1)}, bf16[256,256]{1,0:T(8,128)(2,1)S(1)}, u32[]{:S(2)}, u32[]{:S(2)}) collective-permute-start(bf16[256,256]{1,0:T(8,128)(2,1)S(1)} %get-tuple-element.35), channel_id=1, source_target_pairs={{0,1},{1,0},{2,33},{3,32},{4,65},{5,64},{6,97},{7,96},{8,129},{9,1... | collective-permute-start | bytes 393224 | tf_op jit(solution)/shard_map/ppermute | solution.py:33
  122.4 24.0 %collective-permute-start.9 = (bf16[256,256]{1,0:T(8,128)(2,1)S(1)}, bf16[256,256]{1,0:T(8,128)(2,1)S(1)}, u32[]{:S(2)}, u32[]{:S(2)}) collective-permute-start(bf16[256,256]{1,0:T(8,128)(2,1)S(1)} %get-tuple-element.34), channel_id=1, source_target_pairs={{0,0},{1,1},{2,32},{3,33},{4,64},{5,65},{6,96},{7,97},{8,128},{9,1... | collective-permute-start | bytes 393224 | tf_op jit(solution)/shard_map/ppermute | solution.py:33
  139.6 6.8 %copy-start.7 = (bf16[256,256]{1,0:T(8,128)(2,1)}, bf16[256,256]{1,0:T(8,128)(2,1)S(1)}, u32[]{:S(2)}) copy-start(bf16[256,256]{1,0:T(8,128)(2,1)S(1)} %collective-permute-done.10.there_ref) | copy-start | bytes 393220
  146.4 0.7 copy-start.8

commit v11 on v9

--- a/solution.py
+++ b/solution.py
@@ -154,7 +154,7 @@
         in_specs=[pl.BlockSpec(memory_space=pltpu.SMEM)] * 2 + [pl.BlockSpec(memory_space=pltpu.VMEM)] * 4,
         out_specs=pl.BlockSpec(memory_space=pltpu.VMEM),
         compiler_params=PARAMS,
-        cost_estimate=pl.CostEstimate(flops=20_000_000_000, bytes_accessed=40_000_000, transcendentals=0),
+        cost_estimate=pl.CostEstimate(flops=1, bytes_accessed=1, transcendentals=0),
         name="base",
     )(co, energy, here, there, coeffs, diag_energy)
 

time: 153 us -> 150 us (0.980)
  the two profiles are of different devices: /device:TPU:65 before, /device:TPU:101 now
where the time goes in v11:
time: 150 us; the launch traced here: 149 us
  starting transfers between devices  67.6 us (45%)
  waiting for transfers between devices  47.7 us (32%)
  Pallas kernels  23.6 us (16%)
  other arithmetic  6.11 us (4%)
  local copies, waits for them, and re-layouts  3.12 us (2%)
    ppermute x4, starting transfers between devices, turned(): return lax.ppermute(value, AXES, pairs)  35.6 us
    ppermute x4, waiting for transfers between devices, turned(): return lax.ppermute(value, AXES, pairs)  24.9 us
    ppermute x6, waiting for transfers between devices, shifted(): return lax.ppermute(value, axis, [(i, (i + step) % 4) for i in range(4)])  22.8 us
    ppermute x6, starting transfers between devices, shifted(): return lax.ppermute(value, axis, [(i, (i + step) % 4) for i in range(4)])  15.4 us
    pallas_call x2, Pallas kernels, partial_sums(): pl.pallas_call(kernel, out_shape=(jax.ShapeDtypeStruct((4, *shape), jnp.b...  14.4 us
    all_to_all x2, starting transfers between devices, exchanged(): return lax.all_to_all(parts, 'x', 0, 0, tiled=True)  8.62 us
    pallas_call x1, Pallas kernels, pack(): pl.pallas_call(pack_kernel, out_shape=jax.ShapeDtypeStruct((32, W, 2 * W)...  4.43 us
    all_to_all x1, starting transfers between devices, on_device(): own = lax.all_to_all(packed.reshape(4, 8, W, 2 * W), 'x', 0, 0, tiled=True)  4.24 us
  transfers between devices with their start and end apart: 14, of which 5 were waited for; matrix products, arithmetic and copies ran while one was open for 3% of the time, Pallas kernels for 16%

profile of v11, /device:TPU:101, one launch (start us, length us, event | category | flops | bytes accessed | tf_op | source)
XLA Modules:
  0.0 149.1 jit_solution(15402224946152527048)
XLA Ops:
  0.0 1.1 convert_element_type.16.t0
  1.1 13.7 %collective-permute-start = (bf16[256,256]{1,0:T(8,128)(2,1)S(1)}, bf16[256,256]{1,0:T(8,128)(2,1)S(1)}, u32[]{:S(2)}, u32[]{:S(2)}) collective-permute-start(bf16[256,256]{1,0:T(8,128)(2,1)S(1)} %get-tuple-element.41), channel_id=1, source_target_pairs={{0,0},{1,1},{2,32},{3,33},{4,64},{5,65},{6,96},{7,97},{8,128},{9,1... | collective-permute-start | bytes 393224 | tf_op jit(solution)/shard_map/ppermute | solution.py:33
  14.8 3.9 %collective-permute-start.1 = (bf16[256,256]{1,0:T(8,128)(2,1)S(1)}, bf16[256,256]{1,0:T(8,128)(2,1)S(1)}, u32[]{:S(2)}, u32[]{:S(2)}) collective-permute-start(bf16[256,256]{1,0:T(8,128)(2,1)S(1)} %get-tuple-element.42), channel_id=1, source_target_pairs={{0,1},{1,0},{2,33},{3,32},{4,65},{5,64},{6,97},{7,96},{8,129},{9,1... | collective-permute-start | bytes 393224 | tf_op jit(solution)/shard_map/ppermute | solution.py:33
  18.9 0.7 dynamic-slice
  19.6 0.6 compare_select_fusion.pos
  20.2 4.4 %pack.1 = bf16[32,128,256]{2,1,0:T(8,128)(2,1)} custom-call(s32[2,24]{1,0:T(2,128)} %compare_select_fusion.pos, s32[1]{0:T(128)} %bitcast.co, bf16[4,24,128,128]{3,2,1,0:T(8,128)(2,1)} %h_ref.1), custom_call_target="tpu_custom_call" | custom-call | tf_op jit(solution)/shard_map/pack/pallas_call | solution.py:54
  24.7 4.2 %all-to-all-start = ((bf16[4,8,128,256]{3,2,1,0:T(8,128)(2,1)}), bf16[4,8,128,256]{3,2,1,0:T(8,128)(2,1)S(1)}, u32[]{:S(2)}, u32[]{:S(2)}) async-start(bf16[4,8,128,256]{3,2,1,0:T(8,128)(2,1)} %bitcast.6), calls=%async_computation | async-start | bytes 4194304 | tf_op jit(solution)/shard_map/all_to_all | solution.py:209
  28.9 7.7 %collective-permute-done.1 = bf16[256,256]{1,0:T(8,128)(2,1)S(1)} collective-permute-done((bf16[256,256]{1,0:T(8,128)(2,1)S(1)}, bf16[256,256]{1,0:T(8,128)(2,1)S(1)}, u32[]{:S(2)}, u32[]{:S(2)}) %collective-permute-start.1) | collective-permute-done | bytes 131104 | tf_op jit(solution)/shard_map/ppermute | solution.py:33
  36.7 1.9 %collective-permute-start.2 = (bf16[256,512]{1,0:T(8,128)(2,1)S(1)}, bf16[256,512]{1,0:T(8,128)(2,1)S(1)}, u32[]{:S(2)}, u32[]{:S(2)}) collective-permute-start(bf16[256,512]{1,0:T(8,128)(2,1)S(1)} %maximum_select_fusion.t0), channel_id=1, source_target_pairs={{0,128},{128,256},{256,384},{384,0},{1,129},{129,257},{257,385},{3... | collective-permute-start | bytes 786440 | tf_op jit(solution)/shard_map/ppermute | solution.py:19
  38.7 4.0 %collective-permute-start.3 = (bf16[256,512]{1,0:T(8,128)(2,1)S(1)}, bf16[256,512]{1,0:T(8,128)(2,1)S(1)}, u32[]{:S(2)}, u32[]{:S(2)}) collective-permute-start(bf16[256,512]{1,0:T(8,128)(2,1)S(1)} %maximum_select_fusion.t0), channel_id=1, source_target_pairs={{0,256},{128,384},{256,0},{384,128},{1,257},{129,385},{257,1},{385... | collective-permute-start | bytes 786440 | tf_op jit(solution)/shard_map/ppermute | solution.py:19
  42.7 1.9 %collective-permute-start.4 = (bf16[256,512]{1,0:T(8,128)(2,1)S(1)}, bf16[256,512]{1,0:T(8,128)(2,1)}, u32[]{:S(2)}, u32[]{:S(2)}) collective-permute-start(bf16[256,512]{1,0:T(8,128)(2,1)S(1)} %maximum_select_fusion.t0), channel_id=1, source_target_pairs={{0,384},{128,0},{256,128},{384,256},{1,385},{129,1},{257,129},{385... | collective-permute-start | bytes 786440 | tf_op jit(solution)/shard_map/ppermute | solution.py:19
  45.8 17.2 %collective-permute-done.3.t2 = bf16[256,512]{1,0:T(8,128)(2,1)S(1)} collective-permute-done((bf16[256,512]{1,0:T(8,128)(2,1)S(1)}, bf16[256,512]{1,0:T(8,128)(2,1)S(1)}, u32[]{:S(2)}, u32[]{:S(2)}) %collective-permute-start.3) | collective-permute-done | bytes 262176 | tf_op jit(solution)/shard_map/ppermute | solution.py:19
  63.0 1.3 step.2.bits.in_ref
  64.3 3.8 %collective-permute-start.5 = (bf16[4,8,128,256]{3,2,1,0:T(8,128)(2,1)S(1)}, bf16[4,8,128,256]{3,2,1,0:T(8,128)(2,1)S(1)}, u32[]{:S(2)}, u32[]{:S(2)}) collective-permute-start(bf16[4,8,128,256]{3,2,1,0:T(8,128)(2,1)S(1)} %all-to-all-done.own_ref), channel_id=1, source_target_pairs={{0,1},{1,0},{2,3},{3,2},{4,5},{5,4},{6,7},{7,6},{8,9},{9,8},{10,11... | collective-permute-start | bytes 6291464 | tf_op jit(solution)/shard_map/ppermute | solution.py:23
  68.1 0.7 pad_add_fusion.where
  68.8 1.9 %collective-permute-start.6 = (bf16[512,256]{1,0:T(8,128)(2,1)S(1)}, bf16[512,256]{1,0:T(8,128)(2,1)S(1)}, u32[]{:S(2)}, u32[]{:S(2)}) collective-permute-start(bf16[512,256]{1,0:T(8,128)(2,1)S(1)} %convert_element_type.16.t0), channel_id=1, source_target_pairs={{0,128},{128,256},{256,384},{384,0},{1,129},{129,257},{257,385},{3... | collective-permute-start | bytes 786440 | tf_op jit(solution)/shard_map/ppermute | solution.py:19
  70.7 2.3 %collective-permute-start.7 = (bf16[512,256]{1,0:T(8,128)(2,1)S(1)}, bf16[512,256]{1,0:T(8,128)(2,1)S(1)}, u32[]{:S(2)}, u32[]{:S(2)}) collective-permute-start(bf16[512,256]{1,0:T(8,128)(2,1)S(1)} %convert_element_type.16.t0), channel_id=1, source_target_pairs={{0,256},{128,384},{256,0},{384,128},{1,257},{129,385},{257,1},{385... | collective-permute-start | bytes 786440 | tf_op jit(solution)/shard_map/ppermute | solution.py:19
  73.0 3.4 %collective-permute-start.8 = (bf16[512,256]{1,0:T(8,128)(2,1)S(1)}, bf16[512,256]{1,0:T(8,128)(2,1)S(1)}, u32[]{:S(2)}, u32[]{:S(2)}) collective-permute-start(bf16[512,256]{1,0:T(8,128)(2,1)S(1)} %convert_element_type.16.t0), channel_id=1, source_target_pairs={{0,384},{128,0},{256,128},{384,256},{1,385},{129,1},{257,129},{385... | collective-permute-start | bytes 786440 | tf_op jit(solution)/shard_map/ppermute | solution.py:19
  76.4 1.3 copy-done.9
  77.7 7.1 %direct.1 = (bf16[4,512,256]{2,1,0:T(8,128)(2,1)}, f32[512,256]{1,0:T(8,128)}) custom-call(s32[3]{0:T(128)} %pad_add_fusion.where, s32[8,8]{1,0:T(8,128)} %step.2.bits.in_ref, bf16[256,512]{1,0:T(8,128)(2,1)} %copy-done.6, bf16[256,512]{1,0:T(8,128)(2,1)} %copy-done.10, bf16[256,512]{1,0:T(8,128)(2,1)} %copy-done.11, ...), custom_call_target="tpu_custom_call" | custom-call | flops 20000000000 | bytes 40000000 | tf_op jit(solution)/shard_map/direct/pallas_call | solution.py:128
  84.8 4.2 %all-to-all-start.1 = ((bf16[4,512,256]{2,1,0:T(8,128)(2,1)}), bf16[4,512,256]{2,1,0:T(8,128)(2,1)S(1)}, u32[]{:S(2)}, u32[]{:S(2)}) async-start(bf16[4,512,256]{2,1,0:T(8,128)(2,1)} %get-tuple-element.25), calls=%async_computation.1 | async-start | bytes 2097152 | tf_op jit(solution)/shard_map/all_to_all | solution.py:178
  89.0 5.5 %collective-permute-done.7.t2 = bf16[512,256]{1,0:T(8,128)(2,1)S(1)} collective-permute-done((bf16[512,256]{1,0:T(8,128)(2,1)S(1)}, bf16[512,256]{1,0:T(8,128)(2,1)S(1)}, u32[]{:S(2)}, u32[]{:S(2)}) %collective-permute-start.7) | collective-permute-done | bytes 262176 | tf_op jit(solution)/shard_map/ppermute | solution.py:19
  94.6 1.3 step.3.bits
  95.9 7.3 %mirror.1 = (bf16[4,512,256]{2,1,0:T(8,128)(2,1)}, f32[512,256]{1,0:T(8,128)}) custom-call(s32[3]{0:T(128)} %pad_add_fusion.where, s32[8,8]{1,0:T(8,128)} %step.3.bits, bf16[512,256]{1,0:T(8,128)(2,1)} %copy-done.3, bf16[512,256]{1,0:T(8,128)(2,1)} %copy-done.12, bf16[512,256]{1,0:T(8,128)(2,1)} %copy-done.13, bf16[512,256]{1,0:T(8,128)(2,1)} %copy-done.14, ...), custom_call_target="tpu_custom_call" | custom-call | flops 20000000000 | bytes 40000000 | tf_op jit(solution)/shard_map/mirror/pallas_call | solution.py:128
  103.2 4.4 %all-to-all-start.2 = ((bf16[4,512,256]{2,1,0:T(8,128)(2,1)}), bf16[4,512,256]{2,1,0:T(8,128)(2,1)S(1)}, u32[]{:S(2)}, u32[]{:S(2)}) async-start(bf16[4,512,256]{2,1,0:T(8,128)(2,1)} %get-tuple-element.37), calls=%async_computation.2 | async-start | bytes 2097152 | tf_op jit(solution)/shard_map/all_to_all | solution.py:178
  108.0 11.0 %collective-permute-start.10 = (bf16[256,256]{1,0:T(8,128)(2,1)S(1)}, bf16[256,256]{1,0:T(8,128)(2,1)S(1)}, u32[]{:S(2)}, u32[]{:S(2)}) collective-permute-start(bf16[256,256]{1,0:T(8,128)(2,1)S(1)} %get-tuple-element.35), channel_id=1, source_target_pairs={{0,1},{1,0},{2,33},{3,32},{4,65},{5,64},{6,97},{7,96},{8,129},{9,1... | collective-permute-start | bytes 393224 | tf_op jit(solution)/shard_map/ppermute | solution.py:33
  119.0 7.0 %collective-permute-start.9 = (bf16[256,256]{1,0:T(8,128)(2,1)S(1)}, bf16[256,256]{1,0:T(8,128)(2,1)S(1)}, u32[]{:S(2)}, u32[]{:S(2)}) collective-permute-start(bf16[256,256]{1,0:T(8,128)(2,1)S(1)} %get-tuple-element.34), channel_id=1, source_target_pairs={{0,0},{1,1},{2,32},{3,33},{4,64},{5,65},{6,96},{7,97},{8,128},{9,1... | collective-permute-start | bytes 393224 | tf_op jit(solution)/shard_map/ppermute | solution.py:33
  126.7 4.8 %collective-permute-done.10.there_ref = bf16[256,256]{1,0:T(8,128)(2,1)S(1)} collective-permute-done((bf16[256,256]{1,0:T(8,128)(2,1)S(1)}, bf16[256,256]{1,0:T(8,128)(2,1)S(1)}, u32[]{:S(2)}, u32[]{:S(2)}) %collective-permute-start.10) | collective-permute-done | bytes 131104 | tf_op jit(solution)/shard_map/ppermute | solution.py:33
  131.4 12.4 %collective-permute-done.9.here_ref = bf16[256,256]{1,0:T(8,128)(2,1)S(1)} collective-permute-done((bf16[256,256]{1,0:T(8,128)(2,1)S(1)}, bf16[256,256]{1,0:T(8,128)(2,1)S(1)}, u32[]{:S(2)}, u32[]{:S(2)}) %collective-permute-start.9) | collective-permute-done | bytes 131104 | tf_op jit(solution)/shard_map/ppermute | solution.py:33
  143.9 0.6 copy-done.8
  144.5 2.2 %base.1 = f32[512,256]{1,0:T(8,128)} custom-call(s32[1]{0:T(128)} %bitcast.co, f32[1]{0:T(128)} %copy.13.energy, bf16[256,256]{1,0:T(8,128)(2,1)} %copy-done.8, bf16[256,256]{1,0:T(8,128)(2,1)} %copy-done.7, f32[512,256]{1,0:T(8,128)} %coeffs_ref.1, f32[512,256]{1,0:T(8,128)} %diag_ref.1), custom_call_target="tpu_custom_call" | custom-call | flops 1 | bytes 1 | tf_op jit(solution)/shard_map/base/pallas_call | solution.py:151
  147.1 2.0 %maximum_divide_fusion = f32[512,256]{1,0:T(8,128)} fusion(f32[512,256]{1,0:T(8,128)S(1)} %copy-done.2, f32[512,256]{1,0:T(8,128)} %base.1, f32[512,256]{1,0:T(8,128)S(1)} %copy-done.5, f32[512,256]{1,0:T(8,128)S(1)} %convert_reduce_fusion, f32[]{:T(128)} %bitcast.5), kind=kLoop, calls=%fused_computation.2 | loop fusion | flops 786432 | bytes 2621444 | tf_op jit(solution)/shard_map/div | solution.py:234
  (52 shorter events, 2.2 us)
Async XLA Ops:
  0.0 18.7 %copy-start = (s32[64,24]{0,1:T(8,128)S(1)}, s32[64,24]{0,1:T(8,128)}, u32[]{:S(2)}) copy-start(s32[64,24]{0,1:T(8,128)} %param.10) | copy-start | bytes 18436
  1.1 71.9 %copy-start.3 = (bf16[512,256]{1,0:T(8,128)(2,1)}, bf16[512,256]{1,0:T(8,128)(2,1)S(1)}, u32[]{:S(2)}) copy-start(bf16[512,256]{1,0:T(8,128)(2,1)S(1)} %convert_element_type.16.t0) | copy-start | bytes 786436
  1.1 27.8 %collective-permute-start = (bf16[256,256]{1,0:T(8,128)(2,1)S(1)}, bf16[256,256]{1,0:T(8,128)(2,1)S(1)}, u32[]{:S(2)}, u32[]{:S(2)}) collective-permute-start(bf16[256,256]{1,0:T(8,128)(2,1)S(1)} %get-tuple-element.41), channel_id=1, source_target_pairs={{0,0},{1,1},{2,32},{3,33},{4,64},{5,65},{6,96},{7,97},{8,128},{9,1... | collective-permute-start | bytes 393224 | tf_op jit(solution)/shard_map/ppermute | solution.py:33
  14.8 21.8 %collective-permute-start.1 = (bf16[256,256]{1,0:T(8,128)(2,1)S(1)}, bf16[256,256]{1,0:T(8,128)(2,1)S(1)}, u32[]{:S(2)}, u32[]{:S(2)}) collective-permute-start(bf16[256,256]{1,0:T(8,128)(2,1)S(1)} %get-tuple-element.42), channel_id=1, source_target_pairs={{0,1},{1,0},{2,33},{3,32},{4,65},{5,64},{6,97},{7,96},{8,129},{9,1... | collective-permute-start | bytes 393224 | tf_op jit(solution)/shard_map/ppermute | solution.py:33
  24.7 39.7 %all-to-all-start = ((bf16[4,8,128,256]{3,2,1,0:T(8,128)(2,1)}), bf16[4,8,128,256]{3,2,1,0:T(8,128)(2,1)S(1)}, u32[]{:S(2)}, u32[]{:S(2)}) async-start(bf16[4,8,128,256]{3,2,1,0:T(8,128)(2,1)} %bitcast.6), calls=%async_computation | async-start | bytes 4194304 | tf_op jit(solution)/shard_map/all_to_all | solution.py:209
  36.7 27.6 %copy-start.6 = (bf16[256,512]{1,0:T(8,128)(2,1)}, bf16[256,512]{1,0:T(8,128)(2,1)S(1)}, u32[]{:S(2)}) copy-start(bf16[256,512]{1,0:T(8,128)(2,1)S(1)} %maximum_select_fusion.t0) | copy-start | bytes 786436
  36.7 9.0 %collective-permute-start.2 = (bf16[256,512]{1,0:T(8,128)(2,1)S(1)}, bf16[256,512]{1,0:T(8,128)(2,1)S(1)}, u32[]{:S(2)}, u32[]{:S(2)}) collective-permute-start(bf16[256,512]{1,0:T(8,128)(2,1)S(1)} %maximum_select_fusion.t0), channel_id=1, source_target_pairs={{0,128},{128,256},{256,384},{384,0},{1,129},{129,257},{257,385},{3... | collective-permute-start | bytes 786440 | tf_op jit(solution)/shard_map/ppermute | solution.py:19
  38.7 24.3 %collective-permute-start.3 = (bf16[256,512]{1,0:T(8,128)(2,1)S(1)}, bf16[256,512]{1,0:T(8,128)(2,1)S(1)}, u32[]{:S(2)}, u32[]{:S(2)}) collective-permute-start(bf16[256,512]{1,0:T(8,128)(2,1)S(1)} %maximum_select_fusion.t0), channel_id=1, source_target_pairs={{0,256},{128,384},{256,0},{384,128},{1,257},{129,385},{257,1},{385... | collective-permute-start | bytes 786440 | tf_op jit(solution)/shard_map/ppermute | solution.py:19
  42.7 20.3 %collective-permute-start.4 = (bf16[256,512]{1,0:T(8,128)(2,1)S(1)}, bf16[256,512]{1,0:T(8,128)(2,1)}, u32[]{:S(2)}, u32[]{:S(2)}) collective-permute-start(bf16[256,512]{1,0:T(8,128)(2,1)S(1)} %maximum_select_fusion.t0), channel_id=1, source_target_pairs={{0,384},{128,0},{256,128},{384,256},{1,385},{129,1},{257,129},{385... | collective-permute-start | bytes 786440 | tf_op jit(solution)/shard_map/ppermute | solution.py:19
  45.8 18.5 %copy-start.10 = (bf16[256,512]{1,0:T(8,128)(2,1)}, bf16[256,512]{1,0:T(8,128)(2,1)S(1)}, u32[]{:S(2)}) copy-start(bf16[256,512]{1,0:T(8,128)(2,1)S(1)} %collective-permute-done.2.t1) | copy-start | bytes 786436
  63.0 1.3 copy-start.11
  64.3 12.1 %copy-start.1 = (bf16[4,8,128,256]{3,2,1,0:T(8,128)(2,1)}, bf16[4,8,128,256]{3,2,1,0:T(8,128)(2,1)S(1)}, u32[]{:S(2)}) copy-start(bf16[4,8,128,256]{3,2,1,0:T(8,128)(2,1)S(1)} %all-to-all-done.own_ref) | copy-start | bytes 6291460
  64.3 12.0 %collective-permute-start.5 = (bf16[4,8,128,256]{3,2,1,0:T(8,128)(2,1)S(1)}, bf16[4,8,128,256]{3,2,1,0:T(8,128)(2,1)S(1)}, u32[]{:S(2)}, u32[]{:S(2)}) collective-permute-start(bf16[4,8,128,256]{3,2,1,0:T(8,128)(2,1)S(1)} %all-to-all-done.own_ref), channel_id=1, source_target_pairs={{0,1},{1,0},{2,3},{3,2},{4,5},{5,4},{6,7},{7,6},{8,9},{9,8},{10,11... | collective-permute-start | bytes 6291464 | tf_op jit(solution)/shard_map/ppermute | solution.py:23
  68.8 20.2 %collective-permute-start.6 = (bf16[512,256]{1,0:T(8,128)(2,1)S(1)}, bf16[512,256]{1,0:T(8,128)(2,1)S(1)}, u32[]{:S(2)}, u32[]{:S(2)}) collective-permute-start(bf16[512,256]{1,0:T(8,128)(2,1)S(1)} %convert_element_type.16.t0), channel_id=1, source_target_pairs={{0,128},{128,256},{256,384},{384,0},{1,129},{129,257},{257,385},{3... | collective-permute-start | bytes 786440 | tf_op jit(solution)/shard_map/ppermute | solution.py:19
  70.7 23.9 %collective-permute-start.7 = (bf16[512,256]{1,0:T(8,128)(2,1)S(1)}, bf16[512,256]{1,0:T(8,128)(2,1)S(1)}, u32[]{:S(2)}, u32[]{:S(2)}) collective-permute-start(bf16[512,256]{1,0:T(8,128)(2,1)S(1)} %convert_element_type.16.t0), channel_id=1, source_target_pairs={{0,256},{128,384},{256,0},{384,128},{1,257},{129,385},{257,1},{385... | collective-permute-start | bytes 786440 | tf_op jit(solution)/shard_map/ppermute | solution.py:19
  73.0 21.6 %collective-permute-start.8 = (bf16[512,256]{1,0:T(8,128)(2,1)S(1)}, bf16[512,256]{1,0:T(8,128)(2,1)S(1)}, u32[]{:S(2)}, u32[]{:S(2)}) collective-permute-start(bf16[512,256]{1,0:T(8,128)(2,1)S(1)} %convert_element_type.16.t0), channel_id=1, source_target_pairs={{0,384},{128,0},{256,128},{384,256},{1,385},{129,1},{257,129},{385... | collective-permute-start | bytes 786440 | tf_op jit(solution)/shard_map/ppermute | solution.py:19
  76.4 1.3 copy-start.9
  84.8 18.4 %all-to-all-start.1 = ((bf16[4,512,256]{2,1,0:T(8,128)(2,1)}), bf16[4,512,256]{2,1,0:T(8,128)(2,1)S(1)}, u32[]{:S(2)}, u32[]{:S(2)}) async-start(bf16[4,512,256]{2,1,0:T(8,128)(2,1)} %get-tuple-element.25), calls=%async_computation.1 | async-start | bytes 2097152 | tf_op jit(solution)/shard_map/all_to_all | solution.py:178
  89.0 6.8 %copy-start.12 = (bf16[512,256]{1,0:T(8,128)(2,1)}, bf16[512,256]{1,0:T(8,128)(2,1)S(1)}, u32[]{:S(2)}) copy-start(bf16[512,256]{1,0:T(8,128)(2,1)S(1)} %collective-permute-done.6.t1) | copy-start | bytes 786436
  94.6 1.3 copy-start.13
  94.6 1.3 copy-start.14
  103.2 4.7 %copy-start.4 = (f32[512,256]{1,0:T(8,128)S(1)}, f32[512,256]{1,0:T(8,128)}, u32[]{:S(2)}) copy-start(f32[512,256]{1,0:T(8,128)} %get-tuple-element.24) | copy-start | bytes 1572868
  103.2 43.6 %all-to-all-start.2 = ((bf16[4,512,256]{2,1,0:T(8,128)(2,1)}), bf16[4,512,256]{2,1,0:T(8,128)(2,1)S(1)}, u32[]{:S(2)}, u32[]{:S(2)}) async-start(bf16[4,512,256]{2,1,0:T(8,128)(2,1)} %get-tuple-element.37), calls=%async_computation.2 | async-start | bytes 2097152 | tf_op jit(solution)/shard_map/all_to_all | solution.py:178
  107.9 39.1 %copy-start.2 = (f32[512,256]{1,0:T(8,128)S(1)}, f32[512,256]{1,0:T(8,128)}, u32[]{:S(2)}) copy-start(f32[512,256]{1,0:T(8,128)} %diag_ref.1) | copy-start | bytes 1572868
  108.0 39.1 %copy-start.5 = (f32[512,256]{1,0:T(8,128)S(1)}, f32[512,256]{1,0:T(8,128)}, u32[]{:S(2)}) copy-start(f32[512,256]{1,0:T(8,128)} %get-tuple-element.36) | copy-start | bytes 1572868
  108.0 23.5 %collective-permute-start.10 = (bf16[256,256]{1,0:T(8,128)(2,1)S(1)}, bf16[256,256]{1,0:T(8,128)(2,1)S(1)}, u32[]{:S(2)}, u32[]{:S(2)}) collective-permute-start(bf16[256,256]{1,0:T(8,128)(2,1)S(1)} %get-tuple-element.35), channel_id=1, source_target_pairs={{0,1},{1,0},{2,33},{3,32},{4,65},{5,64},{6,97},{7,96},{8,129},{9,1... | collective-permute-start | bytes 393224 | tf_op jit(solution)/shard_map/ppermute | solution.py:33
  119.0 24.9 %collective-permute-start.9 = (bf16[256,256]{1,0:T(8,128)(2,1)S(1)}, bf16[256,256]{1,0:T(8,128)(2,1)S(1)}, u32[]{:S(2)}, u32[]{:S(2)}) collective-permute-start(bf16[256,256]{1,0:T(8,128)(2,1)S(1)} %get-tuple-element.34), channel_id=1, source_target_pairs={{0,0},{1,1},{2,32},{3,33},{4,64},{5,65},{6,96},{7,97},{8,128},{9,1... | collective-permute-start | bytes 393224 | tf_op jit(solution)/shard_map/ppermute | solution.py:33
  131.4 12.4 %copy-start.7 = (bf16[256,256]{1,0:T(8,128)(2,1)}, bf16[256,256]{1,0:T(8,128)(2,1)S(1)}, u32[]{:S(2)}) copy-start(bf16[256,256]{1,0:T(8,128)(2,1)S(1)} %collective-permute-done.10.there_ref) | copy-start | bytes 393220
  143.9 0.6 copy-start.8
